TPU v7x, 128 devices: a whole 4x4x4 slice. The times are simulated.
128 devices in a mesh: strike: 32 (over y, z, core), depth: 4 (over x).
Axes of the slice: x: 4, y: 4, z: 4, core: 2. Of those that a mesh axis runs over, the one named last changes fastest.
Arguments:
- dofs: float32 [27, 20, 65536], P(None, None, ('strike', 'depth')), may hold values from -6 to 6
- star: float32 [3, 9, 9, 65536], P(None, None, None, ('strike', 'depth')), may hold values from -1.25 to 1.25
- kdiff: float32 [3, 20, 20], replicated, may hold values from -1.25 to 1.25
- couple: float32 [3, 6, 65536], P(None, None, ('strike', 'depth')), may hold values from 0.1 to 1
- omega: float32 [3, 65536], P(None, ('strike', 'depth')), may hold values from 0.2 to 2
- flux_minus: float32 [9, 9, 65536], P(None, None, ('strike', 'depth')), may hold values from -1.5 to 1.5
- flux_plus: float32 [9, 9, 65536], P(None, None, ('strike', 'depth')), may hold values from -1.5 to 1.5
- area: float32 [4, 65536], P(None, ('strike', 'depth')), may hold values from 0.5 to 2
- face_proj: float32 [4, 20, 16], replicated, may hold values from -1.25 to 1.25
- face_lift: float32 [4, 16, 20], replicated, may hold values from -0.75 to 0.75
- nbr_elem: int32 [4, 65536], P(None, ('strike', 'depth')), may hold values from 0 to 1023, as said below
- nbr_face: int32 [4, 65536], P(None, ('strike', 'depth')), may hold values from 0 to 3
- weight_class: int32 [65536], P(('strike', 'depth')), may hold values from 0 to 2
- send_rows: int32 [4, 16384], P(None, ('strike', 'depth')), may hold values from 0 to 511
- fault_send_elem: int32 [128, 2048], P(('strike', 'depth')), may hold values from 0 to 511
- fault_send_face: int32 [128, 2048], P(('strike', 'depth')), may hold values from 0 to 3
- fault_minus_elem: int32 [128, 2048], P(('strike', 'depth')), may hold values from 0 to 511
- fault_minus_face: int32 [128, 2048], P(('strike', 'depth')), may hold values from 0 to 3
- fault_live: int32 [128, 2048], P(('strike', 'depth')), may hold values from 0 to 1
- normal_load: float32 [128, 16, 2048], P(('strike', 'depth')), may hold values from 0.5 to 2
- state: float32 [128, 16, 2048], P(('strike', 'depth')), may hold values from 1 to 30
Outputs:
- dofs_next: float32 [27, 20, 65536], P(None, None, ('strike', 'depth'))
Inputs may be any that keep to these rules, and one draw needn't show every extreme that they name: Where nbr_elem is 512 + k * 128 + b, nbr_face is k.
All inputs are finite; a program needn't handle non-finite values.
Results may differ from a plain program's by a relative error of at most 0.0003.
Values sent between devices are 32-bit elements; how exact they have to be, the bound alone decides.
No kernel may reach another device: no remote copies, remote signals or barrier semaphores. Data moves between devices by JAX's collectives and lax.ppermute only.
A program may use at most 256 MiB of HBM per device.

v0:
```python
import jax
import jax.numpy as jnp
from jax import lax
from jax.sharding import PartitionSpec as P

NE = 9
MECH = 3
NB = 20
NP = 16
ORDER = 4
NEWTON = 4


ETA = 1.0
AFRIC = 0.5
HIGH = lax.Precision.HIGHEST


def extended(x, sides, width):
    for axis, dim in sides:
        count, length = (lax.axis_size(axis), x.shape[dim])
        up = [(i, (i + 1) % count) for i in range(count - 1)]
        down = [(j, i) for i, j in up]
        last = lax.slice_in_dim(x, length - width, length, axis=dim)
        first = lax.slice_in_dim(x, 0, width, axis=dim)
        before = lax.ppermute(last, axis, up)
        after = lax.ppermute(first, axis, down)
        x = jnp.concatenate([before, x, after], axis=dim)
    return x


def inverse_sine(value):
    magnitude = jnp.abs(value)
    return jnp.sign(value) * jnp.log(magnitude + jnp.sqrt(1.0 + magnitude * magnitude))


def derive(field, star, kdiff, couple, omega):
    count = field.shape[-1]
    grads = jnp.einsum("jce,dcb->djbe", field[:NE], kdiff, precision=HIGH)
    stress = jnp.einsum("dije,djbe->ibe", star, grads, precision=HIGH)
    memory = field[NE:].reshape(MECH, 6, NB, count)
    relax = jnp.sum(couple[:, :, None, :] * memory, axis=0)
    upper = stress[:6] - relax
    d_mem = omega[:, None, None, :] * (stress[None, :6] - memory)
    return jnp.concatenate([upper, stress[6:], d_mem.reshape(MECH * 6, NB, count)], 0)


def predict(dofs, star, kdiff, couple, omega, weight_class):
    step = 1.0 / (1.0 + weight_class.astype(dofs.dtype))
    term = dofs
    power = step
    integ = step * dofs
    for order in range(1, ORDER):
        term = derive(term, star, kdiff, couple, omega)
        power = power * step / (order + 1)
        integ = integ + power * term
    return integ


def friction(minus, plus, load, state):
    trial = 0.5 * (minus[..., 1, :, :] + plus[..., 1, :, :]) + 0.5 * ETA * (
        plus[..., 2, :, :] - minus[..., 2, :, :]
    )
    sigma = load * (1.0 + 0.5 * jnp.tanh(0.5 * (minus[..., 0, :, :] + plus[..., 0, :, :])))
    slip = jnp.zeros_like(trial)
    for turn in range(NEWTON):
        scaled = state * slip
        resid = trial - ETA * slip - AFRIC * sigma * inverse_sine(scaled)
        slope = -ETA - AFRIC * sigma * state / jnp.sqrt(1.0 + scaled * scaled)
        slip = slip - resid / slope
    return (trial - ETA * slip, slip)


def per_device(
    dofs,
    star,
    kdiff,
    couple,
    omega,
    flux_minus,
    flux_plus,
    area,
    face_proj,
    face_lift,
    nbr_elem,
    nbr_face,
    weight_class,
    send_rows,
    fault_send_elem,
    fault_send_face,
    fault_minus_elem,
    fault_minus_face,
    fault_live,
    normal_load,
    state,
):
    local_n = dofs.shape[-1]
    rim_n = send_rows.shape[-1]
    integ = predict(dofs, star, kdiff, couple, omega, weight_class)
    faces = jnp.einsum("ibe,fbp->fipe", integ[:NE], face_proj, precision=HIGH)
    elastic_now = integ[:NE]
    picked = jnp.stack([elastic_now[:, :, send_rows[k]] for k in range(4)], 0)
    packed = picked.reshape(4, NE * NB, rim_n)
    strike_out = jnp.stack([packed[1], packed[0]], 1)
    depth_out = jnp.stack([packed[3], packed[2]], 1)
    strike_in = extended(strike_out, (("strike", 1),), 1)
    depth_in = extended(depth_out, (("depth", 1),), 1)
    arrived = jnp.stack([strike_in[:, 0], strike_in[:, 3], depth_in[:, 0], depth_in[:, 3]], 0)
    rim = jnp.einsum("kibn,kbp->kipn", arrived.reshape(4, NE, NB, rim_n), face_proj, precision=HIGH)
    volume = derive(integ, star, kdiff, couple, omega)
    span = local_n + rim_n
    table = jnp.concatenate([faces, rim], -1)
    table = jnp.transpose(table, (1, 2, 0, 3)).reshape(NE, NP, 4 * span)
    flat = nbr_face * span + jnp.where(nbr_elem < local_n, nbr_elem, nbr_elem - nbr_face * rim_n)
    neigh = jnp.transpose(table[:, :, flat], (2, 0, 1, 3))
    mixed = jnp.einsum("ije,fjpe->fipe", flux_minus, faces, precision=HIGH) + jnp.einsum(
        "ije,fjpe->fipe", flux_plus, neigh, precision=HIGH
    )
    flux = jnp.einsum("fe,fipe,fpb->ibe", area, mixed, face_lift, precision=HIGH)
    slots = fault_live.shape[-1]
    sel = faces[:, 0:7:3]
    plus_local = jnp.transpose(sel[fault_send_face[0], :, :, fault_send_elem[0]], (1, 2, 0))
    outgoing = plus_local.reshape(3 * NP, slots)
    incoming = lax.all_to_all(
        outgoing, ("strike", "depth"), split_axis=1, concat_axis=1, tiled=True
    )
    plus = incoming.reshape(3, NP, slots)
    minus = jnp.transpose(sel[fault_minus_face[0], :, :, fault_minus_elem[0]], (1, 2, 0))
    traction, slip = friction(minus, plus, normal_load[0], state[0])
    live = fault_live[0].astype(dofs.dtype)[None, :]
    minus_term = jnp.stack([(traction - minus[1]) * live, -0.5 * slip * live], 0)
    plus_term = jnp.stack([(traction - plus[1]) * live, 0.5 * slip * live], 0).reshape(
        2 * NP, slots
    )
    returned = lax.all_to_all(
        plus_term, ("strike", "depth"), split_axis=1, concat_axis=1, tiled=True
    )
    plus_home = returned.reshape(2, NP, slots)
    minus_add = jnp.einsum(
        "kps,spb->kbs", minus_term, face_lift[fault_minus_face[0]], precision=HIGH
    )
    plus_add = jnp.einsum("kps,spb->kbs", plus_home, face_lift[fault_send_face[0]], precision=HIGH)
    delta = jnp.zeros((2, NB, local_n), dofs.dtype)
    delta = delta.at[:, :, fault_minus_elem[0]].add(minus_add)
    delta = delta.at[:, :, fault_send_elem[0]].add(plus_add)
    elastic = dofs[:NE] + volume[:NE] + flux
    elastic = elastic.at[3].add(delta[0]).at[6].add(delta[1])
    return jnp.concatenate([elastic, dofs[NE:] + volume[NE:]], 0)


def solution(mesh):
    in_specs = (
        P(None, None, ("strike", "depth")),
        P(None, None, None, ("strike", "depth")),
        P(),
        P(None, None, ("strike", "depth")),
        P(None, ("strike", "depth")),
        P(None, None, ("strike", "depth")),
        P(None, None, ("strike", "depth")),
        P(None, ("strike", "depth")),
        P(),
        P(),
        P(None, ("strike", "depth")),
        P(None, ("strike", "depth")),
        P(("strike", "depth")),
        P(None, ("strike", "depth")),
        P(("strike", "depth"), None),
        P(("strike", "depth"), None),
        P(("strike", "depth"), None),
        P(("strike", "depth"), None),
        P(("strike", "depth"), None),
        P(("strike", "depth"), None, None),
        P(("strike", "depth"), None, None),
    )
    out_specs = P(None, None, ("strike", "depth"))
    return jax.shard_map(
        per_device, mesh=mesh, in_specs=in_specs, out_specs=out_specs, check_vma=False
    )
```

profile of v0, /device:TPU:1, one launch (start us, length us, event | category | flops | bytes accessed | tf_op | source)
XLA Modules:
  0.0 657.2 jit_solution(15234381861840563217)
XLA Ops:
  4.4 9.7 %copy.321 = f32[3,9,20,512]{2,1,0,3:T(8,128)} copy(f32[3,9,20,512]{3,2,1,0:T(8,128)} %convolution_bitcast_fusion.7) | data formatting | bytes 2211840 | tf_op jit(solution)/shard_map/jce,dcb->djbe/transpose | solution.py:39
  14.1 7.6 %copy.322 = f32[3,9,9,512]{2,1,0,3:T(8,128)} copy(f32[3,9,9,512]{3,0,2,1:T(4,128)S(1)} %copy-done.10) | data formatting | bytes 995328 | tf_op args[1]
  21.8 20.2 %convolution_bitcast_fusion.3 = f32[512,20,9]{1,2,0:T(8,128)} fusion(f32[3,9,20,512]{2,1,0,3:T(8,128)} %copy.321, f32[3,9,9,512]{2,1,0,3:T(8,128)} %copy.322), kind=kOutput, calls=%fused_computation.17 | convolution fusion | flops 29859840 | bytes 1972224 | tf_op jit(solution)/shard_map/dije,djbe->ibe/dot_general | solution.py:40
  42.0 2.8 copy.323
  45.7 2.3 convolution_bitcast_fusion.6
  48.1 9.7 %copy.326 = f32[3,9,20,512]{2,1,0,3:T(8,128)} copy(f32[3,9,20,512]{3,2,0,1:T(8,128)} %convolution_bitcast_fusion.6) | data formatting | bytes 2211840 | tf_op jit(solution)/shard_map/jce,dcb->djbe/transpose | solution.py:39
  57.7 20.4 %convolution_bitcast_fusion.2 = f32[512,20,9]{1,2,0:T(8,128)} fusion(f32[3,9,20,512]{2,1,0,3:T(8,128)} %copy.326, f32[3,9,9,512]{2,1,0,3:T(8,128)} %copy.322), kind=kOutput, calls=%fused_computation.16 | convolution fusion | flops 29859840 | bytes 1972224 | tf_op jit(solution)/shard_map/dije,djbe->ibe/dot_general | solution.py:40
  78.2 2.8 copy.328
  88.0 8.8 %copy.330 = f32[3,9,20,512]{2,1,0,3:T(8,128)} copy(f32[3,9,20,512]{3,2,0,1:T(8,128)S(1)} %convolution_bitcast_fusion.5) | data formatting | bytes 2211840 | tf_op jit(solution)/shard_map/jce,dcb->djbe/transpose | solution.py:39
  96.9 20.7 %convolution_bitcast_fusion.1 = f32[512,20,9]{1,2,0:T(8,128)} fusion(f32[3,9,20,512]{2,1,0,3:T(8,128)} %copy.330, f32[3,9,9,512]{2,1,0,3:T(8,128)} %copy.322), kind=kOutput, calls=%fused_computation.15 | convolution fusion | flops 29859840 | bytes 1972224 | tf_op jit(solution)/shard_map/dije,djbe->ibe/dot_general | solution.py:40
  117.5 3.6 copy.332
  126.9 3.7 copy.339
  130.5 2.8 gather_fusion.3
  135.7 2.8 gather_fusion.2
  139.6 5.2 collective-permute-start.2
  144.8 2.8 gather_fusion.1
  148.7 3.5 collective-permute-start.1
  152.1 2.8 gather_fusion
  156.0 3.5 collective-permute-start
  161.8 3.1 copy.357
  165.5 20.9 %gather_fusion.7 = f32[2048,3,16]{2,1,0:T(4,128)} fusion(f32[4,3,16,512]{2,1,3,0:T(4,128)} %copy.357, s32[2048]{0:T(1024)S(1)} %bitcast.204), kind=kCustom, calls=%fused_computation.7 | custom fusion | bytes 802816 | tf_op jit(solution)/shard_map/gather | solution.py:122
  186.3 5.2 reshape.507
  191.6 2.9 reshape.509
  194.5 11.2 %all-to-all-start = ((f32[128,1,768]{2,1,0:T(1,128)}), f32[128,1,768]{2,1,0:T(1,128)S(1)}, u32[]{:S(2)}, u32[]{:S(2)}) async-start(f32[128,1,768]{2,1,0:T(1,128)} %reshape.509), calls=%async_computation | async-start | bytes 786432 | tf_op jit(solution)/shard_map/all_to_all | solution.py:124
  205.8 3.3 convolution_bitcast_fusion.4
  209.1 14.0 %copy.337 = f32[4,9,16,512]{1,2,0,3:T(8,128)} copy(f32[4,9,16,512]{3,2,0,1:T(8,128)S(1)} %convolution_bitcast_fusion.8) | data formatting | bytes 2359296 | tf_op jit(solution)/shard_map/ibe,fbp->fipe/transpose | solution.py:100
  224.4 3.7 copy.383
  228.0 9.8 %copy.334 = f32[3,9,20,512]{2,1,0,3:T(8,128)} copy(f32[3,9,20,512]{3,2,0,1:T(8,128)} %convolution_bitcast_fusion.4) | data formatting | bytes 2211840 | tf_op jit(solution)/shard_map/jce,dcb->djbe/transpose | solution.py:39
  237.8 20.3 %convolution_bitcast_fusion = f32[512,20,9]{1,2,0:T(8,128)} fusion(f32[3,9,20,512]{2,1,0,3:T(8,128)} %copy.334, f32[3,9,9,512]{2,1,0,3:T(8,128)} %copy.322), kind=kOutput, calls=%fused_computation.14 | convolution fusion | flops 29859840 | bytes 1972224 | tf_op jit(solution)/shard_map/dije,djbe->ibe/dot_general | solution.py:40
  258.1 3.2 copy.336
  261.3 2.4 fusion.62
  264.7 19.5 %fusion.66 = f32[512,4,16,9]{3,2,1,0:T(8,128)} fusion(f32[4,9,16,512]{1,2,0,3:T(8,128)} %copy.337, f32[9,9,512,1]{1,0,3,2:T(8,128)S(1)} %copy-done.3), kind=kOutput, calls=%fused_computation.145 | convolution fusion | flops 31850496 | bytes 2525184 | tf_op jit(solution)/shard_map/ije,fjpe->fipe/dot_general | solution.py:116
  284.9 4.5 copy.384
  289.5 20.9 %gather_fusion.6 = f32[2048,3,16]{2,1,0:T(4,128)} fusion(f32[4,3,16,512]{2,1,3,0:T(4,128)} %copy.357, s32[2048]{0:T(1024)S(1)} %bitcast.203), kind=kCustom, calls=%fused_computation.6 | custom fusion | bytes 802816 | tf_op jit(solution)/shard_map/gather | solution.py:128
  310.4 4.3 copy.358
  314.7 20.5 %gather_fusion.5 = f32[2048,16,20]{2,1,0:T(8,128)} fusion(f32[4,16,20]{2,1,0:T(8,128)S(1)} %copy-done.2, s32[2048]{0:T(1024)S(1)} %copy-done.20), kind=kCustom, calls=%fused_computation.5 | custom fusion | bytes 5251072 | tf_op jit(solution)/shard_map/gather | solution.py:140
  335.2 20.6 %gather_fusion.8 = f32[2048,16,20]{2,1,0:T(8,128)} fusion(f32[4,16,20]{2,1,0:T(8,128)S(1)} %copy-done.2, s32[2048]{0:T(1024)S(1)} %copy-done.19), kind=kCustom, calls=%fused_computation.8 | custom fusion | bytes 5251072 | tf_op jit(solution)/shard_map/gather | solution.py:142
  364.1 11.1 %copy.397 = f32[9,16,4,640]{1,0,3,2:T(8,128)} copy(f32[9,16,4,640]{3,1,2,0:T(8,128)} %maximum_bitcast_fusion) | data formatting | bytes 2949120 | tf_op jit(solution)/shard_map/reshape | solution.py:113
  375.2 25.8 %gather_fusion.4 = f32[2048,9,16]{2,1,0:T(8,128)} fusion(f32[9,16,2560]{1,0,2:T(8,128)} %bitcast.205, s32[2048]{0:T(1024)S(1)} %broadcast_clamp_fusion.2), kind=kCustom, calls=%fused_computation.4 | custom fusion | bytes 2367488 | tf_op jit(solution)/shard_map/gather | solution.py:115
  401.0 19.4 %copy.353 = f32[4,512,9,16]{2,3,0,1:T(8,128)} copy(f32[4,512,9,16]{3,2,1,0:T(8,128)} %bitcast.206) | data formatting | bytes 2359296 | tf_op jit(solution)/shard_map/gather | solution.py:115
  420.3 25.1 %bitcast_multiply_fusion = f32[4,9,16,512]{1,2,0,3:T(8,128)} fusion(f32[512,4,16,9]{3,2,1,0:T(8,128)} %fusion.66, f32[9,9,512,1]{1,0,3,2:T(8,128)} %copy.384, f32[4,512,9,16]{2,3,0,1:T(8,128)} %copy.353, f32[4,512]{0,1:T(8,128)S(1)} %copy.355), kind=kOutput, calls=%fused_computation.11 | convolution fusion | flops 32440320 | bytes 3713024 | tf_op jit(solution)/shard_map/ije,fjpe->fipe/dot_general | solution.py:116
  445.5 10.1 %copy.356 = f32[4,9,16,512]{3,2,0,1:T(8,128)S(1)} copy(f32[4,9,16,512]{1,2,0,3:T(8,128)} %bitcast_multiply_fusion) | data formatting | bytes 2359296 | tf_op jit(solution)/shard_map/fe,fipe,fpb->ibe/dot_general | solution.py:119
  471.5 10.1 %all-to-all-start.1 = ((f32[128,1,512]{2,1,0:T(1,128)}), f32[128,1,512]{2,1,0:T(1,128)S(1)}, u32[]{:S(2)}, u32[]{:S(2)}) async-start(f32[128,1,512]{2,1,0:T(1,128)} %reshape.511), calls=%async_computation.1 | async-start | bytes 524288 | tf_op jit(solution)/shard_map/all_to_all | solution.py:135
  481.6 17.2 %fusion.67 = f32[2048,2,20]{2,1,0:T(2,128)S(1)} fusion(f32[2,16,2048]{1,0,2:T(2,128)} %copy.365, f32[2048,16,20]{2,1,0:T(8,128)} %gather_fusion.5), kind=kOutput, calls=%fused_computation.146 | convolution fusion | flops 15728640 | bytes 3211264 | tf_op jit(solution)/shard_map/kps,spb->kbs/dot_general | solution.py:139
  498.9 65.1 %scatter_fusion = f32[2,20,512]{1,0,2:T(2,128)S(1)} fusion(f32[2,20,512]{1,0,2:T(2,128)S(1)} %broadcast_in_dim.7, s32[2048]{0:T(1024)S(1)} %bitcast.240, f32[2048,2,20]{2,1,0:T(2,128)S(1)} %fusion.67), kind=kCustom, calls=%fused_computation.9 | custom fusion | flops 81920 | bytes 991232 | tf_op jit(solution)/shard_map/scatter-add | solution.py:144
  565.6 2.6 reshape.508
  568.1 17.2 %fusion.68 = f32[2048,2,20]{2,1,0:T(2,128)S(1)} fusion(f32[2,16,2048]{1,0,2:T(2,128)} %reshape.508, f32[2048,16,20]{2,1,0:T(8,128)} %gather_fusion.8), kind=kOutput, calls=%fused_computation.147 | convolution fusion | flops 15728640 | bytes 3211264 | tf_op jit(solution)/shard_map/kps,spb->kbs/dot_general | solution.py:142
  585.3 65.1 %scatter_fusion.1 = f32[2,20,512]{1,0,2:T(2,128)S(1)} fusion(f32[2,20,512]{1,0,2:T(2,128)S(1)} %scatter_fusion, s32[2048]{0:T(1024)S(1)} %bitcast.239, f32[2048,2,20]{2,1,0:T(2,128)S(1)} %fusion.68), kind=kCustom, calls=%fused_computation.10 | custom fusion | flops 81920 | bytes 991232 | tf_op jit(solution)/shard_map/scatter-add | solution.py:145
  (157 shorter events, 61.3 us)
Async XLA Ops:
  0.0 2.0 copy-start
  4.4 9.8 %copy-start.10 = (f32[3,9,9,512]{3,0,2,1:T(4,128)S(1)}, f32[3,9,9,512]{3,0,2,1:T(4,128)}, u32[]{:S(2)}) copy-start(f32[3,9,9,512]{3,0,2,1:T(4,128)} %param.26) | copy-start | bytes 1492996
  42.0 2.8 copy-start.11
  78.2 3.5 copy-start.32
  78.2 4.2 copy-start.31
  78.2 4.2 copy-start.15
  81.7 4.1 copy-start.7
  117.5 7.1 %copy-start.5 = (f32[27,20,512]{2,0,1:T(8,128)S(1)}, f32[27,20,512]{2,0,1:T(8,128)}, u32[]{:S(2)}) copy-start(f32[27,20,512]{2,0,1:T(8,128)} %param.25) | copy-start | bytes 3317764
  121.1 3.5 copy-start.8
  125.7 1.1 copy-start.4
  126.8 3.7 copy-start.34
  126.8 3.7 copy-start.35
  126.8 18.0 %copy-start.33 = (s32[128]{0:T(128)S(1)}, s32[128]{0:T(128)}, u32[]{:S(2)}) copy-start(s32[128]{0:T(128)} %get-tuple-element.62) | copy-start | bytes 1540
  130.5 29.0 %copy-start.21 = (f32[4,20,16]{1,2,0:T(8,128)S(1)}, f32[4,20,16]{1,2,0:T(8,128)}, u32[]{:S(2)}) copy-start(f32[4,20,16]{1,2,0:T(8,128)} %param.33) | copy-start | bytes 15364
  134.4 221.4 %collective-permute-start.3 = (f32[180,1,128]{2,0,1:T(8,128)}, f32[180,1,128]{2,0,1:T(8,128)}, u32[]{:S(2)}, u32[]{:S(2)}) collective-permute-start(f32[180,1,128]{2,0,1:T(8,128)} %copy.396), channel_id=1, source_target_pairs={{1,0},{2,1},{3,2},{5,4},{6,5},{7,6},{9,8},{10,9},{11,10},{13,12},{... | collective-permute-start | bytes 276488 | tf_op jit(solution)/shard_map/ppermute | solution.py:27
  139.6 217.2 %collective-permute-start.2 = (f32[180,1,128]{2,0,1:T(8,128)}, f32[180,1,128]{2,0,1:T(8,128)}, u32[]{:S(2)}, u32[]{:S(2)}) collective-permute-start(f32[180,1,128]{2,0,1:T(8,128)} %copy.395), channel_id=1, source_target_pairs={{0,1},{1,2},{2,3},{4,5},{5,6},{6,7},{8,9},{9,10},{10,11},{12,13},{... | collective-permute-start | bytes 276488 | tf_op jit(solution)/shard_map/ppermute | solution.py:26
  148.7 209.6 %collective-permute-start.1 = (f32[180,1,128]{2,0,1:T(8,128)}, f32[180,1,128]{2,0,1:T(8,128)}, u32[]{:S(2)}, u32[]{:S(2)}) collective-permute-start(f32[180,1,128]{2,0,1:T(8,128)} %copy.394), channel_id=1, source_target_pairs={{4,0},{8,4},{12,8},{16,12},{20,16},{24,20},{28,24},{32,28},{36,32}... | collective-permute-start | bytes 276488 | tf_op jit(solution)/shard_map/ppermute | solution.py:27
  155.0 9.9 %copy-start.23 = (s32[1,2048]{1,0:T(1,128)S(1)}, s32[1,2048]{1,0:T(1,128)}, u32[]{:S(2)}) copy-start(s32[1,2048]{1,0:T(1,128)} %param.40) | copy-start | bytes 24580
  155.0 9.9 %copy-start.24 = (s32[1,2048]{1,0:T(1,128)S(1)}, s32[1,2048]{1,0:T(1,128)}, u32[]{:S(2)}) copy-start(s32[1,2048]{1,0:T(1,128)} %param.39) | copy-start | bytes 24580
  156.0 203.8 %collective-permute-start = (f32[180,1,128]{2,0,1:T(8,128)}, f32[180,1,128]{2,0,1:T(8,128)}, u32[]{:S(2)}, u32[]{:S(2)}) collective-permute-start(f32[180,1,128]{2,0,1:T(8,128)} %copy.393), channel_id=1, source_target_pairs={{0,4},{4,8},{8,12},{12,16},{16,20},{20,24},{24,28},{28,32},{32,36}... | collective-permute-start | bytes 276488 | tf_op jit(solution)/shard_map/ppermute | solution.py:26
  194.5 262.6 %all-to-all-start = ((f32[128,1,768]{2,1,0:T(1,128)}), f32[128,1,768]{2,1,0:T(1,128)S(1)}, u32[]{:S(2)}, u32[]{:S(2)}) async-start(f32[128,1,768]{2,1,0:T(1,128)} %reshape.509), calls=%async_computation | async-start | bytes 786432 | tf_op jit(solution)/shard_map/all_to_all | solution.py:124
  209.1 14.0 %copy-start.25 = (s32[4,512]{1,0:T(4,128)S(1)}, s32[4,512]{1,0:T(4,128)}, u32[]{:S(2)}) copy-start(s32[4,512]{1,0:T(4,128)} %param.35) | copy-start | bytes 24580
  209.1 14.0 %copy-start.26 = (s32[4,512]{1,0:T(4,128)S(1)}, s32[4,512]{1,0:T(4,128)}, u32[]{:S(2)}) copy-start(s32[4,512]{1,0:T(4,128)} %param.36) | copy-start | bytes 24580
  209.1 14.0 %copy-start.30 = (s32[1,2048]{1,0:T(1,128)S(1)}, s32[1,2048]{1,0:T(1,128)}, u32[]{:S(2)}) copy-start(s32[1,2048]{1,0:T(1,128)} %param.43) | copy-start | bytes 24580
  209.1 15.3 %copy-start.12 = (f32[9,9,512]{2,1,0:T(8,128)S(1)}, f32[9,9,512]{2,1,0:T(8,128)}, u32[]{:S(2)}) copy-start(f32[9,9,512]{2,1,0:T(8,128)} %param.30) | copy-start | bytes 497668
  261.3 3.4 copy-start.27
  261.3 3.4 copy-start.28
  261.3 3.4 copy-start.3
  264.7 20.1 %copy-start.29 = (f32[4,512]{1,0:T(4,128)S(1)}, f32[4,512]{1,0:T(4,128)}, u32[]{:S(2)}) copy-start(f32[4,512]{1,0:T(4,128)} %param.32) | copy-start | bytes 24580
  310.4 4.3 copy-start.2
  310.4 4.3 copy-start.20
  314.7 20.5 %copy-start.19 = (s32[2048]{0:T(1024)S(1)}, s32[2048]{0:T(1024)}, u32[]{:S(2)}) copy-start(s32[2048]{0:T(1024)} %broadcast_clamp_fusion) | copy-start | bytes 24580
  335.2 26.2 %copy-start.22 = (f32[4,20,16]{1,2,0:T(8,128)S(1)}, f32[4,20,16]{1,2,0:T(8,128)}, u32[]{:S(2)}) copy-start(f32[4,20,16]{1,2,0:T(8,128)} %param.33) | copy-start | bytes 15364
  445.5 10.1 %copy-start.9 = (f32[6,20,512]{2,1,0:T(8,128)S(1)}, f32[6,20,512]{2,1,0:T(8,128)}, u32[]{:S(2)}) copy-start(f32[6,20,512]{2,1,0:T(8,128)} %slice_subtract_fusion.1) | copy-start | bytes 737284
  459.7 3.8 copy-start.13
  459.7 3.7 copy-start.14
  459.7 5.4 copy-start.17
  459.7 5.4 copy-start.18
  471.5 92.5 %all-to-all-start.1 = ((f32[128,1,512]{2,1,0:T(1,128)}), f32[128,1,512]{2,1,0:T(1,128)S(1)}, u32[]{:S(2)}, u32[]{:S(2)}) async-start(f32[128,1,512]{2,1,0:T(1,128)} %reshape.511), calls=%async_computation.1 | async-start | bytes 524288 | tf_op jit(solution)/shard_map/all_to_all | solution.py:135
  568.1 17.2 %copy-start.16 = (s32[2048,1]{0,1:T(1,128)S(1)}, s32[2048,1]{0,1:T(1,128)}, u32[]{:S(2)}) copy-start(s32[2048,1]{0,1:T(1,128)} %get-tuple-element.55) | copy-start | bytes 24580
  585.3 68.7 %copy-start.6 = (f32[18,20,512]{2,1,0:T(8,128)S(1)}, f32[18,20,512]{2,1,0:T(8,128)}, u32[]{:S(2)}) copy-start(f32[18,20,512]{2,1,0:T(8,128)} %get-tuple-element.40) | copy-start | bytes 2211844
  585.3 71.5 %copy-start.1 = (f32[3,20,20]{2,1,0:T(8,128)S(1)}, f32[3,20,20]{2,1,0:T(8,128)}, u32[]{:S(2)}) copy-start(f32[3,20,20]{2,1,0:T(8,128)} %param.27) | copy-start | bytes 14404
where the time goes:
time: 668 us; the launch traced here: 657 us
  local copies, waits for them, and re-layouts  292 us (44%)
  matrix products  176 us (26%)
  other arithmetic  154 us (23%)
  starting transfers between devices  34.8 us (5%)
    dot_general x4, matrix products, derive(): stress = jnp.einsum('dije,djbe->ibe', star, grads, precision=HIGH)  81.5 us
    scatter-add x1, other arithmetic, per_device(): delta = delta.at[:, :, fault_minus_elem[0]].add(minus_add)  65.1 us
    scatter-add x1, other arithmetic, per_device(): delta = delta.at[:, :, fault_send_elem[0]].add(plus_add)  65.1 us
    gather x2, local copies, waits for them, and re-layouts, per_device(): neigh = jnp.transpose(table[:, :, flat], (2, 0, 1, 3))  45.1 us
    transpose x4, local copies, waits for them, and re-layouts, derive(): grads = jnp.einsum('jce,dcb->djbe', field[:NE], kdiff, precision=HIGH)  38 us
    gather x2, local copies, waits for them, and re-layouts, per_device(): sel[fault_minus_face[0], :, :, fault_minus_elem[0]]  25.2 us
    dot_general x1, matrix products, per_device(): jnp.einsum('ije,fjpe->fipe', flux_plus, neigh, precision=HIGH)  25.1 us
    unnamed x84, local copies, waits for them, and re-layouts  24.3 us
  transfers between devices with their start and end apart: 6, of which 0 were waited for; matrix products, arithmetic and copies ran while one was open for 58% of the time, Pallas kernels for 0%

commit v1 on v0

v1 whole, which is shorter than its diff:
```python
import jax
import jax.numpy as jnp
from jax import lax
from jax.experimental import pallas as pl
from jax.experimental.pallas import tpu as pltpu
from jax.sharding import PartitionSpec as P

NQ = 27
NE = 9
MECH = 3
NB = 20
NP = 16
ORDER = 4
NEWTON = 4
ETA = 1.0
AFRIC = 0.5
E_DEV = 512
BND = 128
SLOTS = 2048
DEVICES = 128
NBP = 24
LANES = 128
CHUNKS = E_DEV // LANES
ROWS = 224
SC = 512
WIDTH = 12 * 128 + 16
F32 = jnp.float32
BF = jnp.bfloat16
VMEM = 56 * 1024 * 1024
FAULT_ROWS = (0, 3, 6)


def split(x):
    hi = x.astype(BF)
    return hi, (x - hi.astype(F32)).astype(BF)


def pad_rows(x, rows):
    extra = rows - x.shape[0]
    if extra == 0:
        return x
    return jnp.concatenate([x, jnp.zeros((extra,) + x.shape[1:], x.dtype)], axis=0)


def stack3(x):
    hi, lo = split(x)
    return jnp.concatenate([hi, hi, lo], axis=0)


def left3(scratch, parts, depth, rows):
    scratch[...] = jnp.zeros(scratch.shape, F32)
    for row, col, value in parts:
        scratch[row : row + value.shape[0], col : col + value.shape[1]] = value
    whole = scratch[0:depth, :]
    hi = whole.astype(BF).astype(F32)
    lo = whole - hi
    tall = jnp.concatenate([hi, lo, hi], axis=0)
    tall = pad_rows(tall, -(-tall.shape[0] // 128) * 128)
    return jnp.transpose(tall, (1, 0))[0:rows, 0 : 3 * depth].astype(BF)


def dot(a, b):
    return lax.dot_general(a, b, (((1,), (0,)), ((), ())), preferred_element_type=F32)


def dot_nt(a, b):
    return lax.dot_general(a, b, (((1,), (1,)), ((), ())), preferred_element_type=F32)


def one_hot(index, rows, base=0):
    row = lax.broadcasted_iota(jnp.int32, (rows, index.shape[1]), 0) + base
    return jnp.where(row == index, 1.0, 0.0).astype(BF)


def swap_blocks(x):
    x = pltpu.roll(x, 0, 1, stride=16, stride_axis=0)
    lane = lax.broadcasted_iota(jnp.int32, (8, LANES), 1)
    sub = lax.broadcasted_iota(jnp.int32, (8, LANES), 0)
    down = jnp.bitwise_and(lane // 16 - sub, 7)
    across = jnp.bitwise_and(lane + 16 * sub, LANES - 1)
    tiles = []
    for t in range(x.shape[0] // 8):
        y = jnp.take_along_axis(x[8 * t : 8 * t + 8], down, axis=0, mode="promise_in_bounds")
        tiles.append(jnp.take_along_axis(y, across, axis=1, mode="promise_in_bounds"))
    return jnp.concatenate(tiles, axis=0)


def to_blocks(x):
    return swap_blocks(
        jnp.concatenate([x[:, t * LANES : (t + 1) * LANES] for t in range(SC // LANES)], axis=0)
    )


def to_slots(x):
    x = swap_blocks(x)
    return jnp.concatenate([x[8 * t : 8 * t + 8] for t in range(SC // LANES)], axis=1)


def stress_of(get, star_ref, kd, grads):
    right = jnp.concatenate([stack3(pad_rows(get(j), 32)) for j in range(NE)], axis=1)
    grads[...] = dot(kd, right)
    acc = [None] * NE
    for d in range(3):
        for j in range(NE):
            g = grads[d * NBP : (d + 1) * NBP, j * LANES : (j + 1) * LANES]
            for i in range(NE):
                t = star_ref[d, i, j : j + 1, :] * g
                acc[i] = t if acc[i] is None else acc[i] + t
    return acc


def predict_kernel(
    dofs, star, couple, omega, wc, kdiff, proj, srow, fse, fsf, fme, fmf, live, load, state,
    integ, ihl, send0, send1, send2, send3, out, keep,
    term, grads, mat, kdw, fpw, fhl,
):
    c = pl.program_id(0)

    @pl.when(c == 0)
    def _():
        kdw[...] = left3(mat, [(0, d * NBP, kdiff[d]) for d in range(3)], 32, 80)
        fpw[...] = left3(mat, [(0, g * NP, proj[g]) for g in range(4)], 32, 64)
        term[...] = jnp.zeros(term.shape, F32)

    kd = kdw[...]
    step = 1.0 / (1.0 + wc[...].astype(F32))
    for q in range(NQ):
        term[q, 0:NB, :] = dofs[q]
    for q in range(NQ):
        integ[q] = step * term[q]

    def turn(order, power):
        acc = stress_of(lambda j: term[j], star, kd, grads)
        for q in range(6):
            old = [term[NE + 6 * l + q] for l in range(MECH)]
            relax = couple[0, q : q + 1, :] * old[0]
            for l in range(1, MECH):
                relax = relax + couple[l, q : q + 1, :] * old[l]
            term[q] = acc[q] - relax
            for l in range(MECH):
                term[NE + 6 * l + q] = omega[l : l + 1, :] * (acc[q] - old[l])
        for q in range(6, NE):
            term[q] = acc[q]
        power = power * step / (order + 2).astype(F32)
        for q in range(NQ):
            integ[q] += power * term[q]
        return power

    lax.fori_loop(0, ORDER - 1, turn, step)

    here = pl.ds(pl.multiple_of(c * LANES, LANES), LANES)
    flat = pad_rows(integ[0:NE].reshape(NE * NBP, LANES), ROWS)
    hi, lo = split(flat)
    ihl[0:ROWS, here] = hi
    ihl[ROWS : 2 * ROWS, here] = lo
    hi, lo = split(pad_rows(jnp.concatenate([integ[r] for r in FAULT_ROWS], axis=0), 80))
    fhl[0:80, here] = hi
    fhl[80:160, here] = lo

    @pl.when(c == CHUNKS - 1)
    def _():
        rows = jnp.concatenate([srow[k : k + 1, :] for k in range(4)], axis=1)
        got = dot(ihl[...], one_hot(rows, E_DEV))
        got = got[0:ROWS] + got[ROWS : 2 * ROWS]
        for k, ref in enumerate((send0, send1, send2, send3)):
            for j in range(NE):
                ref[j] = got[j * NBP : j * NBP + NB, k * BND : (k + 1) * BND]

        def fault_values(elem, face):
            x = dot(fhl[...], one_hot(elem, E_DEV))
            right = []
            for r in range(3):
                h = pad_rows(x[r * NBP : (r + 1) * NBP], 32).astype(BF)
                l = pad_rows(x[80 + r * NBP : 80 + (r + 1) * NBP], 32).astype(BF)
                right.append(jnp.concatenate([h, h, l], axis=0))
            points = dot(fpw[...], jnp.concatenate(right, axis=1))
            values = []
            for r in range(3):
                cols = slice(r * SC, (r + 1) * SC)
                v = points[0:NP, cols]
                for g in range(1, 4):
                    v = jnp.where(face == g, points[g * NP : (g + 1) * NP, cols], v)
                values.append(v)
            return values

        def chunk(s, carry):
            cols = pl.ds(pl.multiple_of(s * SC, SC), SC)
            lines = pl.ds(pl.multiple_of(s * (SC // 16), SC // 16), SC // 16)
            plus = fault_values(fse[:, cols], fsf[:, cols])
            minus = fault_values(fme[:, cols], fmf[:, cols])
            sent = (
                plus[1] + plus[2], plus[0], minus[1] - minus[2], minus[0],
                load[0, :, cols], state[0, :, cols],
            )
            for n, x in enumerate(sent):
                for g in range(2):
                    at = (2 * n + g) * LANES
                    out[lines, at : at + LANES] = to_blocks(x[8 * g : 8 * g + 8])
            for n, x in enumerate((plus[1], minus[1])):
                for g in range(2):
                    at = (2 * n + g) * LANES
                    keep[lines, at : at + LANES] = to_blocks(x[8 * g : 8 * g + 8])
            alive = jnp.broadcast_to(live[:, cols].astype(F32), (8, SC))
            out[lines, 12 * LANES : WIDTH] = to_blocks(alive)[:, 0:16]
            return carry

        lax.fori_loop(0, SLOTS // SC, chunk, 0)


def element_kernel(
    integ, dofs, star, couple, omega, fminus, fplus, area, nelem, nface, ihl, rim0, rim1, rim2, rim3,
    kdiff, proj, lift, base, grads, mat, kdw, fpw, ltw, plw, rhl, own, near,
):
    c = pl.program_id(0)

    @pl.when(c == 0)
    def _():
        kdw[...] = left3(mat, [(0, d * NBP, kdiff[d]) for d in range(3)], 32, 80)
        fpw[...] = left3(mat, [(0, g * NP, proj[g]) for g in range(4)], 32, 64)
        ltw[...] = left3(mat, [(f * NP, 0, lift[f]) for f in range(4)], 64, 32)
        both = [
            lax.dot_general(
                proj[f], lift[f], (((1,), (0,)), ((), ())),
                precision=lax.Precision.HIGHEST, preferred_element_type=F32,
            )
            for f in range(4)
        ]
        plw[...] = left3(mat, [(0, f * NBP, both[f]) for f in range(4)], 32, 96)
        for k, ref in enumerate((rim0, rim1, rim2, rim3)):
            flat = jnp.concatenate([pad_rows(ref[j], NBP) for j in range(NE)], axis=0)
            hi, lo = split(pad_rows(flat, ROWS))
            rhl[0:ROWS, k * BND : (k + 1) * BND] = hi
            rhl[ROWS : 2 * ROWS, k * BND : (k + 1) * BND] = lo

    elem = jnp.concatenate([nelem[f : f + 1, :] for f in range(4)], axis=1)
    face = jnp.concatenate([nface[f : f + 1, :] for f in range(4)], axis=1)
    scale = jnp.concatenate([area[f : f + 1, :] for f in range(4)], axis=1)
    got = dot(ihl[...], one_hot(elem, E_DEV)) + dot(rhl[...], one_hot(elem, 4 * BND, E_DEV))
    lifted = []
    for j in range(NE):
        h = pad_rows(got[j * NBP : (j + 1) * NBP], 32).astype(BF)
        l = pad_rows(got[ROWS + j * NBP : ROWS + (j + 1) * NBP], 32).astype(BF)
        points = dot(fpw[...], jnp.concatenate([h, h, l], axis=0))
        v = points[0:NP]
        for g in range(1, 4):
            v = jnp.where(face == g, points[g * NP : (g + 1) * NP], v)
        v = v * scale
        v = jnp.concatenate([v[:, f * LANES : (f + 1) * LANES] for f in range(4)], axis=0)
        lifted.append(stack3(v))
    near[...] = dot(ltw[...], jnp.concatenate(lifted, axis=1))

    right = jnp.concatenate([stack3(pad_rows(integ[j], 32)) for j in range(NE)], axis=1)
    folded = dot(plw[...], right)
    for j in range(NE):
        cols = slice(j * LANES, (j + 1) * LANES)
        w = area[0:1, :] * folded[0:NBP, cols]
        for f in range(1, 4):
            w = w + area[f : f + 1, :] * folded[f * NBP : (f + 1) * NBP, cols]
        own[:, cols] = w

    acc = stress_of(lambda j: integ[j], star, kdw[...], grads)
    total = []
    for q in range(6):
        old = [integ[NE + 6 * l + q] for l in range(MECH)]
        relax = couple[0, q : q + 1, :] * old[0]
        for l in range(1, MECH):
            relax = relax + couple[l, q : q + 1, :] * old[l]
        for l in range(MECH):
            at = NE + 6 * l + q
            base[at] = dofs[at] + (omega[l : l + 1, :] * (acc[q] - old[l]))[0:NB]
        total.append(acc[q] - relax)
    total = total + acc[6:]
    for j in range(NE):
        cols = slice(j * LANES, (j + 1) * LANES)
        w, v = own[:, cols], near[0:NBP, cols]
        for i in range(NE):
            total[i] = total[i] + (fminus[i, j : j + 1, :] * w + fplus[i, j : j + 1, :] * v)
    for i in range(NE):
        base[i] = dofs[i] + total[i][0:NB]


def friction(trial, pressure, load, state):
    sigma = load * (1.0 + 0.5 * jnp.tanh(0.5 * pressure))
    half = AFRIC * sigma
    slip = trial / (ETA + half * state)
    for turn in range(NEWTON - 1):
        scaled = state * slip
        size = jnp.abs(scaled)
        root = jnp.sqrt(1.0 + size * size)
        arc = jnp.log(size + root)
        arc = jnp.where(scaled < 0.0, -arc, arc)
        resid = trial - ETA * slip - half * arc
        slip = slip + resid * root / (ETA * root + half * state)
    return trial - ETA * slip, slip


def fault_kernel(
    base_in, mine, theirs, keep, fse, fsf, fme, fmf, live, lift,
    base, mat, lfw, acc, rows, sem,
):
    del base_in
    reads = [
        pltpu.make_async_copy(base.at[FAULT_ROWS[1 + k]], rows.at[k], sem.at[k]) for k in range(2)
    ]
    for copy in reads:
        copy.start()
    lfw[...] = left3(mat, [(0, f * NBP, lift[f]) for f in range(4)], 16, 96)
    acc[...] = jnp.zeros(acc.shape, F32)

    def chunk(s, carry):
        cols = pl.ds(pl.multiple_of(s * SC, SC), SC)
        lines = pl.ds(pl.multiple_of(s * (SC // 16), SC // 16), SC // 16)

        def pair(ref, n):
            return ref[lines, n * 256 : (n + 1) * 256]

        pull, slip = friction(
            0.5 * (pair(theirs, 0) + pair(mine, 2)), pair(mine, 3) + pair(theirs, 1),
            pair(mine, 4), pair(mine, 5),
        )
        terms = [pull - pair(keep, 1), -0.5 * slip]
        pull, slip = friction(
            0.5 * (pair(mine, 0) + pair(theirs, 2)), pair(theirs, 3) + pair(mine, 1),
            pair(theirs, 4), pair(theirs, 5),
        )
        terms += [pull - pair(keep, 0), 0.5 * slip]
        right = []
        for t in terms:
            x = jnp.concatenate([to_slots(t[:, 0:LANES]), to_slots(t[:, LANES:256])], axis=0)
            right.append(stack3(x))
        added = dot(lfw[...], jnp.concatenate(right, axis=1))
        far = jnp.concatenate(
            [theirs[lines, 12 * LANES : WIDTH], jnp.zeros((SC // 16, LANES - 16), F32)], axis=1
        )
        far = to_slots(far)[0:1]
        left = []
        for side, (alive, face) in enumerate(
            ((live[:, cols].astype(F32), fmf[:, cols]), (far, fsf[:, cols]))
        ):
            mask = [jnp.where(face == f, alive, 0.0) for f in range(4)]
            sums = []
            for k in range(2):
                at = slice((2 * side + k) * SC, (2 * side + k + 1) * SC)
                y = mask[0] * added[0:NBP, at]
                for f in range(1, 4):
                    y = y + mask[f] * added[f * NBP : (f + 1) * NBP, at]
                sums.append(y)
            hi, lo = split(jnp.concatenate(sums, axis=0))
            left.append(jnp.concatenate([hi, lo], axis=0))
        spots = jnp.concatenate([one_hot(fme[:, cols], E_DEV), one_hot(fse[:, cols], E_DEV)], axis=1)
        acc[...] += dot_nt(jnp.concatenate(left, axis=1), spots)
        return carry

    lax.fori_loop(0, SLOTS // SC, chunk, 0)
    delta = acc[0:48] + acc[48:96]
    for copy in reads:
        copy.wait()
    for k in range(2):
        rows[k] = rows[k] + delta[k * NBP : k * NBP + NB]
    writes = [
        pltpu.make_async_copy(rows.at[k], base.at[FAULT_ROWS[1 + k]], sem.at[k]) for k in range(2)
    ]
    for copy in writes:
        copy.start()
    for copy in writes:
        copy.wait()


def whole(shape):
    return pl.BlockSpec(shape, lambda *i: (0,) * len(shape))


def lanes(*lead):
    return pl.BlockSpec(lead + (LANES,), lambda c: (0,) * len(lead) + (c,))


def per_device(
    dofs, star, kdiff, couple, omega, flux_minus, flux_plus, area, face_proj, face_lift,
    nbr_elem, nbr_face, weight_class, send_rows, fault_send_elem, fault_send_face,
    fault_minus_elem, fault_minus_face, fault_live, normal_load, state,
):
    shape = jax.ShapeDtypeStruct
    wc = weight_class.reshape(1, E_DEV)
    slot = whole((1, SLOTS))
    point = whole((1, NP, SLOTS))
    rim = whole((NE, NB, BND))
    params = pltpu.CompilerParams(vmem_limit_bytes=VMEM)
    integ, ihl, s0, s1, s2, s3, out, keep = pl.pallas_call(
        predict_kernel,
        grid=(CHUNKS,),
        in_specs=[
            lanes(NQ, NB), lanes(3, NE, NE), lanes(MECH, 6), lanes(MECH), lanes(1),
            whole((3, NB, NB)), whole((4, NB, NP)), whole((4, BND)),
            slot, slot, slot, slot, slot, point, point,
        ],
        out_specs=[
            lanes(NQ, NBP), whole((2 * ROWS, E_DEV)), rim, rim, rim, rim,
            whole((DEVICES, WIDTH)), whole((DEVICES, 4 * LANES)),
        ],
        out_shape=[
            shape((NQ, NBP, E_DEV), F32), shape((2 * ROWS, E_DEV), BF),
            *[shape((NE, NB, BND), F32)] * 4,
            shape((DEVICES, WIDTH), F32), shape((DEVICES, 4 * LANES), F32),
        ],
        scratch_shapes=[
            pltpu.VMEM((NQ, NBP, LANES), F32), pltpu.VMEM((80, NE * LANES), F32),
            pltpu.VMEM((64, LANES), F32), pltpu.VMEM((80, 96), BF), pltpu.VMEM((64, 96), BF),
            pltpu.VMEM((160, E_DEV), BF),
        ],
        compiler_params=params,
        name="predict",
    )(
        dofs, star, couple, omega, wc, kdiff, face_proj, send_rows, fault_send_elem, fault_send_face,
        fault_minus_elem, fault_minus_face, fault_live, normal_load, state,
    )
    ns, nd = lax.axis_size("strike"), lax.axis_size("depth")

    def onward(n):
        return [(i, i + 1) for i in range(n - 1)]

    def back(n):
        return [(i + 1, i) for i in range(n - 1)]

    r0 = lax.ppermute(s0, "strike", onward(ns))
    r1 = lax.ppermute(s1, "strike", back(ns))
    r2 = lax.ppermute(s2, "depth", onward(nd))
    r3 = lax.ppermute(s3, "depth", back(nd))
    theirs = lax.all_to_all(out, ("strike", "depth"), split_axis=0, concat_axis=0, tiled=True)
    base = pl.pallas_call(
        element_kernel,
        grid=(CHUNKS,),
        in_specs=[
            lanes(NQ, NBP), lanes(NQ, NB), lanes(3, NE, NE), lanes(MECH, 6), lanes(MECH),
            lanes(NE, NE), lanes(NE, NE), lanes(4), lanes(4), lanes(4),
            whole((2 * ROWS, E_DEV)), rim, rim, rim, rim,
            whole((3, NB, NB)), whole((4, NB, NP)), whole((4, NP, NB)),
        ],
        out_specs=lanes(NQ, NB),
        out_shape=shape((NQ, NB, E_DEV), F32),
        scratch_shapes=[
            pltpu.VMEM((80, NE * LANES), F32), pltpu.VMEM((64, LANES), F32),
            pltpu.VMEM((80, 96), BF), pltpu.VMEM((64, 96), BF), pltpu.VMEM((32, 192), BF),
            pltpu.VMEM((96, 96), BF), pltpu.VMEM((2 * ROWS, 4 * BND), BF),
            pltpu.VMEM((NBP, NE * LANES), F32), pltpu.VMEM((32, NE * LANES), F32),
        ],
        compiler_params=params,
        name="elements",
    )(
        integ, dofs, star, couple, omega, flux_minus, flux_plus, area, nbr_elem, nbr_face,
        ihl, r0, r1, r2, r3, kdiff, face_proj, face_lift,
    )
    anywhere = pl.BlockSpec(memory_space=pl.ANY)
    local = pl.BlockSpec(memory_space=pltpu.VMEM)
    return pl.pallas_call(
        fault_kernel,
        in_specs=[anywhere] + [local] * 9,
        out_specs=anywhere,
        out_shape=shape((NQ, NB, E_DEV), F32),
        input_output_aliases={0: 0},
        scratch_shapes=[
            pltpu.VMEM((64, LANES), F32), pltpu.VMEM((96, 48), BF), pltpu.VMEM((96, E_DEV), F32),
            pltpu.VMEM((2, NB, E_DEV), F32), pltpu.SemaphoreType.DMA((2,)),
        ],
        compiler_params=params,
        name="fault",
    )(
        base, out, theirs, keep, fault_send_elem, fault_send_face, fault_minus_elem,
        fault_minus_face, fault_live, face_lift,
    )


def solution(mesh):
    both = ("strike", "depth")
    split_1, split_2, split_3 = P(None, both), P(None, None, both), P(None, None, None, both)
    in_specs = (
        split_2, split_3, P(), split_2, split_1, split_2, split_2, split_1, P(), P(),
        split_1, split_1, P(both), split_1,
        *[P(both, None)] * 5, P(both, None, None), P(both, None, None),
    )
    return jax.shard_map(
        per_device, mesh=mesh, in_specs=in_specs, out_specs=split_2, check_vma=False
    )
```

time: 668 us -> 69.7 us (0.10)
  the two profiles are of different devices: /device:TPU:1 before, /device:TPU:8 now
where the time goes in v1:
time: 69.7 us; the launch traced here: 69.2 us
  Pallas kernels  27.8 us (40%)
  starting transfers between devices  22.8 us (33%)
  local copies, waits for them, and re-layouts  13.1 us (19%)
  waiting for transfers between devices  5.34 us (8%)
    pallas_call x1, Pallas kernels, per_device(): pl.pallas_call(predict_kernel, grid=(CHUNKS,), in_specs=[lanes(NQ, NB), l...  12.7 us
    all_to_all x1, starting transfers between devices, per_device(): lax.all_to_all(out, ('strike', 'depth'), split_axis=0, concat_axis=0, til...  10.4 us
    pallas_call x1, Pallas kernels, per_device(): pl.pallas_call(element_kernel, grid=(CHUNKS,), in_specs=[lanes(NQ, NBP),...  9.18 us
    unnamed x21, local copies, waits for them, and re-layouts  6.14 us
    pallas_call x1, Pallas kernels, per_device(): pl.pallas_call(fault_kernel, in_specs=[anywhere] + [local] * 9, out_specs...  5.9 us
    ppermute x1, starting transfers between devices, per_device(): r1 = lax.ppermute(s1, 'strike', back(ns))  5.61 us
    ppermute x1, waiting for transfers between devices, per_device(): r3 = lax.ppermute(s3, 'depth', back(nd))  4.34 us
    all_to_all x2, local copies, waits for them, and re-layouts, per_device(): lax.all_to_all(out, ('strike', 'depth'), split_axis=0, concat_axis=0, til...  3.97 us
  transfers between devices with their start and end apart: 5, of which 3 were waited for; matrix products, arithmetic and copies ran while one was open for 0% of the time, Pallas kernels for 13%

profile of v1, /device:TPU:8, one launch (start us, length us, event | category | flops | bytes accessed | tf_op | source)
XLA Modules:
  0.0 69.2 jit_solution(10572736029017129747)
XLA Ops:
  0.0 0.0 copy-start
  0.0 1.6 %copy.40.proj = f32[4,20,16]{2,1,0:T(8,128)} copy(f32[4,20,16]{1,2,0:T(8,128)} %param.29) | data formatting | bytes 10240 | tf_op args[8]
  1.6 2.2 %copy.39.star = f32[3,9,9,512]{3,2,1,0:T(8,128)} copy(f32[3,9,9,512]{3,0,2,1:T(4,128)} %param.22) | data formatting | bytes 995328 | tf_op args[1]
  3.8 0.0 copy-done
  3.8 1.7 %copy.38.dofs = f32[27,20,512]{2,1,0:T(8,128)} copy(f32[27,20,512]{2,0,1:T(8,128)S(1)} %copy-done) | data formatting | bytes 2211840 | tf_op args[0]
  5.5 12.7 %predict.1 = (f32[27,24,512]{2,1,0:T(8,128)}, bf16[448,512]{1,0:T(8,128)(2,1)}, f32[9,20,128]{2,1,0:T(8,128)}, f32[9,20,128]{2,1,0:T(8,128)}, f32[9,20,128]{2,1,...) custom-call(f32[27,20,512]{2,1,0:T(8,128)} %copy.38.dofs, ...), custom_call_target="tpu_custom_call" | custom-call | tf_op jit(solution)/shard_map/predict/pallas_call | solution.py:388
  18.2 0.0 copy-start.8
  18.3 0.0 copy-start.7
  18.3 0.0 copy-start.6
  18.3 0.0 copy-start.5
  18.3 3.0 %copy.44 = f32[128,1,1552]{2,1,0:T(1,128)} copy(f32[128,1,1552]{2,0,1:T(8,128)} %bitcast.6) | data formatting | bytes 1589248 | tf_op jit(solution)/shard_map/all_to_all | solution.py:428
  21.3 10.4 %all-to-all-start = ((f32[128,1,1552]{2,1,0:T(1,128)}), f32[128,1,1552]{2,1,0:T(1,128)S(1)}, u32[]{:S(2)}, u32[]{:S(2)}) async-start(f32[128,1,1552]{2,1,0:T(1,128)} %copy.44), calls=%async_computation | async-start | bytes 1703936 | tf_op jit(solution)/shard_map/all_to_all | solution.py:428
  31.8 0.0 copy-done.8
  31.8 2.1 %collective-permute-start = (f32[9,20,128]{2,1,0:T(8,128)S(1)}, f32[9,20,128]{2,1,0:T(8,128)S(1)}, u32[]{:S(2)}, u32[]{:S(2)}) collective-permute-start(f32[9,20,128]{2,1,0:T(8,128)S(1)} %copy-done.8), channel_id=1, source_target_pairs={{0,4},{4,8},{8,12},{12,16},{16,20},{20,24},{24,28},{28,32},{32,36}... | collective-permute-start | bytes 276488 | tf_op jit(solution)/shard_map/ppermute | solution.py:424
  33.8 0.0 copy-done.7
  33.8 5.6 %collective-permute-start.1 = (f32[9,20,128]{2,1,0:T(8,128)S(1)}, f32[9,20,128]{2,1,0:T(8,128)S(1)}, u32[]{:S(2)}, u32[]{:S(2)}) collective-permute-start(f32[9,20,128]{2,1,0:T(8,128)S(1)} %copy-done.7), channel_id=1, source_target_pairs={{4,0},{8,4},{12,8},{16,12},{20,16},{24,20},{28,24},{32,28},{36,32}... | collective-permute-start | bytes 276488 | tf_op jit(solution)/shard_map/ppermute | solution.py:425
  39.5 0.0 copy-done.6
  39.5 3.4 %collective-permute-start.2 = (f32[9,20,128]{2,1,0:T(8,128)S(1)}, f32[9,20,128]{2,1,0:T(8,128)S(1)}, u32[]{:S(2)}, u32[]{:S(2)}) collective-permute-start(f32[9,20,128]{2,1,0:T(8,128)S(1)} %copy-done.6), channel_id=1, source_target_pairs={{0,1},{1,2},{2,3},{4,5},{5,6},{6,7},{8,9},{9,10},{10,11},{12,13},{... | collective-permute-start | bytes 276488 | tf_op jit(solution)/shard_map/ppermute | solution.py:426
  42.9 0.0 copy-done.5
  42.9 1.3 %collective-permute-start.3 = (f32[9,20,128]{2,1,0:T(8,128)S(1)}, f32[9,20,128]{2,1,0:T(8,128)S(1)}, u32[]{:S(2)}, u32[]{:S(2)}) collective-permute-start(f32[9,20,128]{2,1,0:T(8,128)S(1)} %copy-done.5), channel_id=1, source_target_pairs={{1,0},{2,1},{3,2},{5,4},{6,5},{7,6},{9,8},{10,9},{11,10},{13,12},{... | collective-permute-start | bytes 276488 | tf_op jit(solution)/shard_map/ppermute | solution.py:427
  44.2 0.1 collective-permute-done.rim0
  44.2 0.0 copy-start.1
  44.2 0.0 collective-permute-done.1.rim1
  44.3 0.0 copy-start.2
  44.3 0.9 %collective-permute-done.2.rim2 = f32[9,20,128]{2,1,0:T(8,128)S(1)} collective-permute-done((f32[9,20,128]{2,1,0:T(8,128)S(1)}, f32[9,20,128]{2,1,0:T(8,128)S(1)}, u32[]{:S(2)}, u32[]{:S(2)}) %collective-permute-start.2) | collective-permute-done | bytes 92192 | tf_op jit(solution)/shard_map/ppermute | solution.py:426
  45.2 0.0 copy-start.3
  45.2 4.3 %collective-permute-done.3.rim3 = f32[9,20,128]{2,1,0:T(8,128)S(1)} collective-permute-done((f32[9,20,128]{2,1,0:T(8,128)S(1)}, f32[9,20,128]{2,1,0:T(8,128)S(1)}, u32[]{:S(2)}, u32[]{:S(2)}) %collective-permute-start.3) | collective-permute-done | bytes 92192 | tf_op jit(solution)/shard_map/ppermute | solution.py:427
  49.5 0.0 copy-start.4
  49.5 0.0 copy-done.1
  49.5 0.0 copy-done.2
  49.5 0.0 copy-done.3
  49.5 0.6 copy-done.4
  50.1 9.2 %elements.1.base_in = f32[27,20,512]{2,1,0:T(8,128)} custom-call(f32[27,24,512]{2,1,0:T(8,128)} %get-tuple-element.13.integ, f32[27,20,512]{2,1,0:T(8,128)} %copy.38.dofs, f32[3,9,9,512]{3,2,1,0:T(8,128)} %copy.39.star, f32[3,6,512]{2,1,0:T(8,128)} %couple.3, f32[3,512]{1,0:T(4,128)} %omega.3, f32[9,9,512]{2,1,0:T(8,128)} %fminus.1, f32[9,9,512]{2,1,0:T(8,128)} %fplus.1, ...), custom_call_target="tpu_custom_call" | custom-call | tf_op jit(solution)/shard_map/elements/pallas_call | solution.py:429
  59.3 0.0 all-to-all-done
  59.3 1.0 %copy.50 = f32[128,1,1552]{2,0,1:T(8,128)} copy(f32[128,1,1552]{2,1,0:T(1,128)S(1)} %all-to-all-done) | data formatting | bytes 1589248 | tf_op jit(solution)/shard_map/all_to_all | solution.py:428
  60.3 5.9 %fault.1 = f32[27,20,512]{2,1,0:T(8,128)} custom-call(f32[27,20,512]{2,1,0:T(8,128)} %elements.1.base_in, f32[128,1552]{1,0:T(8,128)} %get-tuple-element.19.mine, f32[128,1552]{1,0:T(8,128)} %bitcast.7, f32[128,512]{1,0:T(8,128)} %get-tuple-element.20.keep, s32[1,2048]{1,0:T(1,128)} %fse.3, s32[1,2048]{1,0:T(1,128)} %fsf.3, ...), custom_call_target="tpu_custom_call", output_to_operand_aliasing={{}: (0, {})} | custom-call | tf_op jit(solution)/shard_map/fault/pallas_call | solution.py:454
  66.2 3.0 %copy.47 = f32[27,20,512]{2,0,1:T(8,128)} copy(f32[27,20,512]{2,1,0:T(8,128)} %fault.1) | data formatting | bytes 2211840 | tf_op jit(solution)/shard_map/fault/pallas_call | solution.py:454
Async XLA Ops:
  0.0 3.8 %copy-start = (f32[27,20,512]{2,0,1:T(8,128)S(1)}, f32[27,20,512]{2,0,1:T(8,128)}, u32[]{:S(2)}) copy-start(f32[27,20,512]{2,0,1:T(8,128)} %param.21) | copy-start | bytes 3317764
  18.2 13.5 %copy-start.8 = (f32[9,20,128]{2,1,0:T(8,128)S(1)}, f32[9,20,128]{2,1,0:T(8,128)}, u32[]{:S(2)}) copy-start(f32[9,20,128]{2,1,0:T(8,128)} %get-tuple-element.15) | copy-start | bytes 276484
  18.3 15.6 %copy-start.7 = (f32[9,20,128]{2,1,0:T(8,128)S(1)}, f32[9,20,128]{2,1,0:T(8,128)}, u32[]{:S(2)}) copy-start(f32[9,20,128]{2,1,0:T(8,128)} %get-tuple-element.16) | copy-start | bytes 276484
  18.3 21.2 %copy-start.6 = (f32[9,20,128]{2,1,0:T(8,128)S(1)}, f32[9,20,128]{2,1,0:T(8,128)}, u32[]{:S(2)}) copy-start(f32[9,20,128]{2,1,0:T(8,128)} %get-tuple-element.17) | copy-start | bytes 276484
  18.3 24.6 %copy-start.5 = (f32[9,20,128]{2,1,0:T(8,128)S(1)}, f32[9,20,128]{2,1,0:T(8,128)}, u32[]{:S(2)}) copy-start(f32[9,20,128]{2,1,0:T(8,128)} %get-tuple-element.18) | copy-start | bytes 276484
  21.3 38.0 %all-to-all-start = ((f32[128,1,1552]{2,1,0:T(1,128)}), f32[128,1,1552]{2,1,0:T(1,128)S(1)}, u32[]{:S(2)}, u32[]{:S(2)}) async-start(f32[128,1,1552]{2,1,0:T(1,128)} %copy.44), calls=%async_computation | async-start | bytes 1703936 | tf_op jit(solution)/shard_map/all_to_all | solution.py:428
  31.8 12.5 %collective-permute-start = (f32[9,20,128]{2,1,0:T(8,128)S(1)}, f32[9,20,128]{2,1,0:T(8,128)S(1)}, u32[]{:S(2)}, u32[]{:S(2)}) collective-permute-start(f32[9,20,128]{2,1,0:T(8,128)S(1)} %copy-done.8), channel_id=1, source_target_pairs={{0,4},{4,8},{8,12},{12,16},{16,20},{20,24},{24,28},{28,32},{32,36}... | collective-permute-start | bytes 276488 | tf_op jit(solution)/shard_map/ppermute | solution.py:424
  33.8 10.4 %collective-permute-start.1 = (f32[9,20,128]{2,1,0:T(8,128)S(1)}, f32[9,20,128]{2,1,0:T(8,128)S(1)}, u32[]{:S(2)}, u32[]{:S(2)}) collective-permute-start(f32[9,20,128]{2,1,0:T(8,128)S(1)} %copy-done.7), channel_id=1, source_target_pairs={{4,0},{8,4},{12,8},{16,12},{20,16},{24,20},{28,24},{32,28},{36,32}... | collective-permute-start | bytes 276488 | tf_op jit(solution)/shard_map/ppermute | solution.py:425
  39.5 5.7 %collective-permute-start.2 = (f32[9,20,128]{2,1,0:T(8,128)S(1)}, f32[9,20,128]{2,1,0:T(8,128)S(1)}, u32[]{:S(2)}, u32[]{:S(2)}) collective-permute-start(f32[9,20,128]{2,1,0:T(8,128)S(1)} %copy-done.6), channel_id=1, source_target_pairs={{0,1},{1,2},{2,3},{4,5},{5,6},{6,7},{8,9},{9,10},{10,11},{12,13},{... | collective-permute-start | bytes 276488 | tf_op jit(solution)/shard_map/ppermute | solution.py:426
  42.9 6.6 %collective-permute-start.3 = (f32[9,20,128]{2,1,0:T(8,128)S(1)}, f32[9,20,128]{2,1,0:T(8,128)S(1)}, u32[]{:S(2)}, u32[]{:S(2)}) collective-permute-start(f32[9,20,128]{2,1,0:T(8,128)S(1)} %copy-done.5), channel_id=1, source_target_pairs={{1,0},{2,1},{3,2},{5,4},{6,5},{7,6},{9,8},{10,9},{11,10},{13,12},{... | collective-permute-start | bytes 276488 | tf_op jit(solution)/shard_map/ppermute | solution.py:427
  44.2 5.3 %copy-start.1 = (f32[9,20,128]{2,1,0:T(8,128)}, f32[9,20,128]{2,1,0:T(8,128)S(1)}, u32[]{:S(2)}) copy-start(f32[9,20,128]{2,1,0:T(8,128)S(1)} %collective-permute-done.rim0) | copy-start | bytes 276484
  44.3 5.3 %copy-start.2 = (f32[9,20,128]{2,1,0:T(8,128)}, f32[9,20,128]{2,1,0:T(8,128)S(1)}, u32[]{:S(2)}) copy-start(f32[9,20,128]{2,1,0:T(8,128)S(1)} %collective-permute-done.1.rim1) | copy-start | bytes 276484
  45.2 4.4 %copy-start.3 = (f32[9,20,128]{2,1,0:T(8,128)}, f32[9,20,128]{2,1,0:T(8,128)S(1)}, u32[]{:S(2)}) copy-start(f32[9,20,128]{2,1,0:T(8,128)S(1)} %collective-permute-done.2.rim2) | copy-start | bytes 276484
  49.5 0.6 copy-start.4

commit v2 on v1

v2 whole, which is shorter than its diff:
```python
import jax
import jax.numpy as jnp
from jax import lax
from jax.experimental import pallas as pl
from jax.experimental.pallas import tpu as pltpu
from jax.sharding import PartitionSpec as P

NQ = 27
NE = 9
MECH = 3
NB = 20
NP = 16
ORDER = 4
NEWTON = 4
ETA = 1.0
AFRIC = 0.5
E_DEV = 512
BND = 128
SLOTS = 2048
DEVICES = 128
NBP = 24
LANES = 128
CHUNKS = E_DEV // LANES
ROWS = 224
SC = 512
TILES = 13
F32 = jnp.float32
BF = jnp.bfloat16
VMEM = 56 * 1024 * 1024
FAULT_ROWS = (0, 3, 6)


def split(x):
    hi = x.astype(BF)
    return hi, (x - hi.astype(F32)).astype(BF)


def pad_rows(x, rows):
    extra = rows - x.shape[0]
    if extra == 0:
        return x
    return jnp.concatenate([x, jnp.zeros((extra,) + x.shape[1:], x.dtype)], axis=0)


def stack3(x):
    hi, lo = split(x)
    return jnp.concatenate([hi, hi, lo], axis=0)


def left3(scratch, parts, depth, rows):
    scratch[...] = jnp.zeros(scratch.shape, F32)
    for row, col, value in parts:
        scratch[row : row + value.shape[0], col : col + value.shape[1]] = value
    whole = scratch[0:depth, :]
    hi = whole.astype(BF).astype(F32)
    lo = whole - hi
    tall = jnp.concatenate([hi, lo, hi], axis=0)
    tall = pad_rows(tall, -(-tall.shape[0] // 128) * 128)
    return jnp.transpose(tall, (1, 0))[0:rows, 0 : 3 * depth].astype(BF)


def dot(a, b):
    return lax.dot_general(a, b, (((1,), (0,)), ((), ())), preferred_element_type=F32)


def dot_nt(a, b):
    return lax.dot_general(a, b, (((1,), (1,)), ((), ())), preferred_element_type=F32)


def one_hot(index, rows, base=0):
    row = lax.broadcasted_iota(jnp.int32, (rows, index.shape[1]), 0) + base
    return jnp.where(row == index, 1.0, 0.0).astype(BF)


def swap_blocks(x):
    x = pltpu.roll(x, 0, 1, stride=16, stride_axis=0)
    lane = lax.broadcasted_iota(jnp.int32, (8, LANES), 1)
    sub = lax.broadcasted_iota(jnp.int32, (8, LANES), 0)
    down = jnp.bitwise_and(lane // 16 - sub, 7)
    across = jnp.bitwise_and(lane + 16 * sub, LANES - 1)
    tiles = []
    for t in range(x.shape[0] // 8):
        y = jnp.take_along_axis(x[8 * t : 8 * t + 8], down, axis=0, mode="promise_in_bounds")
        tiles.append(jnp.take_along_axis(y, across, axis=1, mode="promise_in_bounds"))
    return jnp.concatenate(tiles, axis=0)


def to_blocks(x):
    return swap_blocks(
        jnp.concatenate([x[:, t * LANES : (t + 1) * LANES] for t in range(SC // LANES)], axis=0)
    )


def to_slots(x):
    x = swap_blocks(x)
    return jnp.concatenate([x[8 * t : 8 * t + 8] for t in range(SC // LANES)], axis=1)


def stress_of(get, star_ref, kd, grads):
    right = jnp.concatenate([stack3(pad_rows(get(j), 32)) for j in range(NE)], axis=1)
    grads[...] = dot(kd, right)
    acc = [None] * NE
    for d in range(3):
        for j in range(NE):
            g = grads[d * NBP : (d + 1) * NBP, j * LANES : (j + 1) * LANES]
            for i in range(NE):
                t = star_ref[i, j, d : d + 1, :] * g
                acc[i] = t if acc[i] is None else acc[i] + t
    return acc


def predict_kernel(
    dofs, star, couple, omega, wc, kdiff, srow,
    integ, ihl, fhl, send0, send1, send2, send3,
    term, grads, mat, kdw,
):
    c = pl.program_id(0)

    @pl.when(c == 0)
    def _():
        kdw[...] = left3(mat, [(0, d * NBP, kdiff[d]) for d in range(3)], 32, 80)
        term[...] = jnp.zeros(term.shape, F32)

    kd = kdw[...]
    step = 1.0 / (1.0 + wc[...].astype(F32))
    term[:, 0:NB, :] = jnp.transpose(dofs[...], (1, 0, 2))
    for q in range(NQ):
        integ[q] = step * term[q]

    def turn(order, power):
        acc = stress_of(lambda j: term[j], star, kd, grads)
        for q in range(6):
            old = [term[NE + 6 * l + q] for l in range(MECH)]
            relax = couple[0, q : q + 1, :] * old[0]
            for l in range(1, MECH):
                relax = relax + couple[l, q : q + 1, :] * old[l]
            term[q] = acc[q] - relax
            for l in range(MECH):
                term[NE + 6 * l + q] = omega[l : l + 1, :] * (acc[q] - old[l])
        for q in range(6, NE):
            term[q] = acc[q]
        power = power * step / (order + 2).astype(F32)
        for q in range(NQ):
            integ[q] += power * term[q]
        return power

    lax.fori_loop(0, ORDER - 1, turn, step)

    here = pl.ds(pl.multiple_of(c * LANES, LANES), LANES)
    flat = pad_rows(integ[0:NE].reshape(NE * NBP, LANES), ROWS)
    hi, lo = split(flat)
    ihl[0:ROWS, here] = hi
    ihl[ROWS : 2 * ROWS, here] = lo
    hi, lo = split(pad_rows(jnp.concatenate([integ[r] for r in FAULT_ROWS], axis=0), 80))
    fhl[0:80, here] = hi
    fhl[80:160, here] = lo

    @pl.when(c == CHUNKS - 1)
    def _():
        rows = []
        for axis, k in (("strike", 0), ("depth", 2)):
            even = lax.axis_index(axis) % 2 == 0
            ahead, behind = srow[k : k + 1, :], srow[k + 1 : k + 2, :]
            rows += [jnp.where(even, ahead, behind), jnp.where(even, behind, ahead)]
        rows = jnp.concatenate(rows, axis=1)
        got = dot(ihl[...], one_hot(rows, E_DEV))
        got = got[0:ROWS] + got[ROWS : 2 * ROWS]
        for k, ref in enumerate((send0, send1, send2, send3)):
            for j in range(NE):
                ref[j] = got[j * NBP : j * NBP + NB, k * BND : (k + 1) * BND]


def fault_values(fhl, fpw, elem, face):
    x = dot(fhl[...], one_hot(elem, E_DEV))
    right = []
    for r in range(3):
        h = pad_rows(x[r * NBP : (r + 1) * NBP], 32).astype(BF)
        l = pad_rows(x[80 + r * NBP : 80 + (r + 1) * NBP], 32).astype(BF)
        right.append(jnp.concatenate([h, h, l], axis=0))
    points = dot(fpw[...], jnp.concatenate(right, axis=1))
    values = []
    for r in range(3):
        cols = slice(r * SC, (r + 1) * SC)
        v = points[0:NP, cols]
        for g in range(1, 4):
            v = jnp.where(face == g, points[g * NP : (g + 1) * NP, cols], v)
        values.append(v)
    return values


def slot_kernel(fhl, proj, fse, fsf, fme, fmf, live, load, state, out, keep, mat, fpw):
    @pl.when(pl.program_id(0) == 0)
    def _():
        fpw[...] = left3(mat, [(0, g * NP, proj[g].T) for g in range(4)], 32, 64)

    def place(tile, x):
        out[pl.ds(tile, SC // 16, stride=TILES), :] = to_blocks(x)

    place(12, jnp.broadcast_to(live[...].astype(F32), (8, SC)))
    plus = fault_values(fhl, fpw, fse[...], fsf[...])
    minus = fault_values(fhl, fpw, fme[...], fmf[...])
    sent = (
        plus[1] + plus[2], plus[0], minus[1] - minus[2], minus[0], load[0], state[0],
    )
    for n, x in enumerate(sent):
        for g in range(2):
            place(2 * n + g, x[8 * g : 8 * g + 8])
    for n, x in enumerate((plus[1], minus[1])):
        for g in range(2):
            at = (2 * n + g) * LANES
            keep[:, at : at + LANES] = to_blocks(x[8 * g : 8 * g + 8])


def element_kernel(
    integ, dofs, star, couple, omega, fminus, fplus, area, nelem, nface, ihl, rim0, rim1, rim2, rim3,
    kdiff, proj, lift, base, grads, mat, kdw, fpw, ltw, plw, rhl, own, near, change,
):
    c = pl.program_id(0)

    def put_rim(k, fields):
        flat = jnp.concatenate([pad_rows(x, NBP) for x in fields], axis=0)
        hi, lo = split(pad_rows(flat, ROWS))
        rhl[0:ROWS, k * BND : (k + 1) * BND] = hi
        rhl[ROWS : 2 * ROWS, k * BND : (k + 1) * BND] = lo

    @pl.when(c == 0)
    def _():
        kdw[...] = left3(mat, [(0, d * NBP, kdiff[d]) for d in range(3)], 32, 80)
        fpw[...] = left3(mat, [(0, g * NP, proj[g].T) for g in range(4)], 32, 64)
        ltw[...] = left3(mat, [(f * NP, 0, lift[f]) for f in range(4)], 64, 32)
        both = [
            lax.dot_general(
                proj[f], lift[f], (((0,), (0,)), ((), ())),
                precision=lax.Precision.HIGHEST, preferred_element_type=F32,
            )
            for f in range(4)
        ]
        plw[...] = left3(mat, [(0, f * NBP, both[f]) for f in range(4)], 32, 96)
        for k, first, second, axis in ((0, rim0, rim1, "strike"), (2, rim2, rim3, "depth")):
            at = lax.axis_index(axis)
            even = (at % 2 == 0).astype(F32)
            odd = 1.0 - even
            before = (at > 0).astype(F32)
            after = (at < lax.axis_size(axis) - 1).astype(F32)
            for side, one, two in ((k, odd * before, even * before), (k + 1, even * after, odd * after)):
                put_rim(side, [one * first[j] + two * second[j] for j in range(NE)])
    elem = jnp.concatenate([nelem[f : f + 1, :] for f in range(4)], axis=1)
    face = jnp.concatenate([nface[f : f + 1, :] for f in range(4)], axis=1)
    scale = jnp.concatenate([area[f : f + 1, :] for f in range(4)], axis=1)
    got = dot(ihl[...], one_hot(elem, E_DEV)) + dot(rhl[...], one_hot(elem, 4 * BND, E_DEV))
    lifted = []
    for j in range(NE):
        h = pad_rows(got[j * NBP : (j + 1) * NBP], 32).astype(BF)
        l = pad_rows(got[ROWS + j * NBP : ROWS + (j + 1) * NBP], 32).astype(BF)
        points = dot(fpw[...], jnp.concatenate([h, h, l], axis=0))
        v = points[0:NP]
        for g in range(1, 4):
            v = jnp.where(face == g, points[g * NP : (g + 1) * NP], v)
        v = v * scale
        v = jnp.concatenate([v[:, f * LANES : (f + 1) * LANES] for f in range(4)], axis=0)
        lifted.append(stack3(v))
    near[...] = dot(ltw[...], jnp.concatenate(lifted, axis=1))

    right = jnp.concatenate([stack3(pad_rows(integ[j], 32)) for j in range(NE)], axis=1)
    folded = dot(plw[...], right)
    for j in range(NE):
        cols = slice(j * LANES, (j + 1) * LANES)
        w = area[0:1, :] * folded[0:NBP, cols]
        for f in range(1, 4):
            w = w + area[f : f + 1, :] * folded[f * NBP : (f + 1) * NBP, cols]
        own[:, cols] = w

    acc = stress_of(lambda j: integ[j], star, kdw[...], grads)
    total = []
    for q in range(6):
        old = [integ[NE + 6 * l + q] for l in range(MECH)]
        relax = couple[0, q : q + 1, :] * old[0]
        for l in range(1, MECH):
            relax = relax + couple[l, q : q + 1, :] * old[l]
        for l in range(MECH):
            at = NE + 6 * l + q
            change[at] = omega[l : l + 1, :] * (acc[q] - old[l])
        total.append(acc[q] - relax)
    total = total + acc[6:]
    for j in range(NE):
        cols = slice(j * LANES, (j + 1) * LANES)
        w, v = own[:, cols], near[0:NBP, cols]
        for i in range(NE):
            total[i] = total[i] + (fminus[i, j : j + 1, :] * w + fplus[i, j : j + 1, :] * v)
    for i in range(NE):
        change[i] = total[i]
    base[...] = dofs[...] + jnp.transpose(change[:, 0:NB, :], (1, 0, 2))


def friction(trial, pressure, load, state):
    sigma = load * (1.0 + 0.5 * jnp.tanh(0.5 * pressure))
    half = AFRIC * sigma
    steep = half * state
    size = jnp.abs(trial)
    slip = size / (ETA + steep)
    for turn in range(NEWTON - 1):
        scaled = state * slip
        square = 1.0 + scaled * scaled
        inverse = lax.rsqrt(square)
        resid = size - ETA * slip - half * jnp.log(scaled + square * inverse)
        slope = ETA + steep * inverse
        guess = pl.reciprocal(slope, approx=True)
        slip = slip + resid * (guess * (2.0 - slope * guess))
    slip = jnp.where(trial < 0.0, -slip, slip)
    return trial - ETA * slip, slip


def fault_kernel(
    base_in, mine, theirs, keep, fse, fsf, fme, fmf, live, lift,
    base, mat, lfw, acc, slab, sem,
):
    del base_in
    s = pl.program_id(0)
    window = base.at[:, 0:8, :]

    @pl.when(s == 0)
    def _():
        pltpu.make_async_copy(window, slab, sem).start()
        lfw[...] = left3(mat, [(0, f * NBP, lift[f]) for f in range(4)], 16, 96)

    def tile(ref, n):
        return ref[pl.ds(n, SC // 16, stride=TILES), :]

    def pair(ref, n):
        return jnp.concatenate([tile(ref, 2 * n), tile(ref, 2 * n + 1)], axis=1)

    pull, slip = friction(
        0.5 * (pair(theirs, 0) + pair(mine, 2)), pair(mine, 3) + pair(theirs, 1),
        pair(mine, 4), pair(mine, 5),
    )
    terms = [pull - keep[:, 256:512], -0.5 * slip]
    pull, slip = friction(
        0.5 * (pair(mine, 0) + pair(theirs, 2)), pair(theirs, 3) + pair(mine, 1),
        pair(theirs, 4), pair(theirs, 5),
    )
    terms += [pull - keep[:, 0:256], 0.5 * slip]
    right = []
    for t in terms:
        x = jnp.concatenate([to_slots(t[:, 0:LANES]), to_slots(t[:, LANES:256])], axis=0)
        right.append(stack3(x))
    added = dot(lfw[...], jnp.concatenate(right, axis=1))
    far = to_slots(tile(theirs, 12))[0:1]
    left = []
    for side, (alive, face) in enumerate(((live[...].astype(F32), fmf[...]), (far, fsf[...]))):
        mask = [jnp.where(face == f, alive, 0.0) for f in range(4)]
        sums = []
        for k in range(2):
            at = slice((2 * side + k) * SC, (2 * side + k + 1) * SC)
            y = mask[0] * added[0:NBP, at]
            for f in range(1, 4):
                y = y + mask[f] * added[f * NBP : (f + 1) * NBP, at]
            sums.append(y)
        hi, lo = split(jnp.concatenate(sums, axis=0))
        left.append(jnp.concatenate([hi, lo], axis=0))
    spots = jnp.concatenate([one_hot(fme[...], E_DEV), one_hot(fse[...], E_DEV)], axis=1)
    acc[s] = dot_nt(jnp.concatenate(left, axis=1), spots)

    @pl.when(s == SLOTS // SC - 1)
    def _():
        total = acc[0]
        for part in range(1, SLOTS // SC):
            total = total + acc[part]
        acc[0, 0:48, :] = total[0:48] + total[48:96]
        pltpu.make_async_copy(window, slab, sem).wait()
        for b in range(NB):
            for k in range(2):
                row = slice(FAULT_ROWS[1 + k], FAULT_ROWS[1 + k] + 1)
                slab[b, row, :] = slab[b, row, :] + acc[0, k * NBP + b : k * NBP + b + 1, :]
        copy = pltpu.make_async_copy(slab, window, sem)
        copy.start()
        copy.wait()


def whole(shape):
    return pl.BlockSpec(shape, lambda *i: (0,) * len(shape))


def lanes(*lead):
    return pl.BlockSpec(lead + (LANES,), lambda c: (0,) * len(lead) + (c,))


def per_device(
    dofs, star, kdiff, couple, omega, flux_minus, flux_plus, area, face_proj, face_lift,
    nbr_elem, nbr_face, weight_class, send_rows, fault_send_elem, fault_send_face,
    fault_minus_elem, fault_minus_face, fault_live, normal_load, state,
):
    shape = jax.ShapeDtypeStruct
    wc = weight_class.reshape(1, E_DEV)
    dofs = jnp.transpose(dofs, (1, 0, 2))
    star = jnp.transpose(star, (1, 2, 0, 3))
    face_proj = jnp.transpose(face_proj, (0, 2, 1))
    rim = whole((NE, NB, BND))
    lines = pl.BlockSpec((SC // 16 * TILES, LANES), lambda c: (c, 0))
    kept = pl.BlockSpec((SC // 16, 4 * LANES), lambda c: (c, 0))
    slots = pl.BlockSpec((1, SC), lambda c: (0, c))
    points = pl.BlockSpec((1, NP, SC), lambda c: (0, 0, c))
    params = pltpu.CompilerParams(vmem_limit_bytes=VMEM)
    integ, ihl, fhl, s0, s1, s2, s3 = pl.pallas_call(
        predict_kernel,
        grid=(CHUNKS,),
        in_specs=[
            lanes(NB, NQ), lanes(NE, NE, 3), lanes(MECH, 6), lanes(MECH), lanes(1),
            whole((3, NB, NB)), whole((4, BND)),
        ],
        out_specs=[
            lanes(NQ, NBP), whole((2 * ROWS, E_DEV)), whole((160, E_DEV)), rim, rim, rim, rim,
        ],
        out_shape=[
            shape((NQ, NBP, E_DEV), F32), shape((2 * ROWS, E_DEV), BF), shape((160, E_DEV), BF),
            *[shape((NE, NB, BND), F32)] * 4,
        ],
        scratch_shapes=[
            pltpu.VMEM((NQ, NBP, LANES), F32), pltpu.VMEM((80, NE * LANES), F32),
            pltpu.VMEM((64, LANES), F32), pltpu.VMEM((80, 96), BF),
        ],
        compiler_params=params,
        name="predict",
    )(dofs, star, couple, omega, wc, kdiff, send_rows)
    out, keep = pl.pallas_call(
        slot_kernel,
        grid=(SLOTS // SC,),
        in_specs=[whole((160, E_DEV)), whole((4, NP, NB)), *[slots] * 5, points, points],
        out_specs=[lines, kept],
        out_shape=[shape((DEVICES * TILES, LANES), F32), shape((DEVICES, 4 * LANES), F32)],
        scratch_shapes=[pltpu.VMEM((64, LANES), F32), pltpu.VMEM((64, 96), BF)],
        compiler_params=params,
        name="slots",
    )(
        fhl, face_proj, fault_send_elem, fault_send_face, fault_minus_elem, fault_minus_face,
        fault_live, normal_load, state,
    )
    ns, nd = lax.axis_size("strike"), lax.axis_size("depth")

    def swap(x, axis, n, first):
        ends = [(i, (i + 1) % n) for i in range(first, n, 2)]
        return lax.ppermute(x, axis, ends + [(j, i) for i, j in ends])

    r0 = swap(s0, "strike", ns, 0)
    r1 = swap(s1, "strike", ns, 1)
    r2 = swap(s2, "depth", nd, 0)
    r3 = swap(s3, "depth", nd, 1)
    theirs = lax.all_to_all(
        out.reshape(DEVICES, 1, TILES * LANES), ("strike", "depth"), split_axis=0, concat_axis=0, tiled=True
    ).reshape(DEVICES * TILES, LANES)
    base = pl.pallas_call(
        element_kernel,
        grid=(CHUNKS,),
        in_specs=[
            lanes(NQ, NBP), lanes(NB, NQ), lanes(NE, NE, 3), lanes(MECH, 6), lanes(MECH),
            lanes(NE, NE), lanes(NE, NE), lanes(4), lanes(4), lanes(4),
            whole((2 * ROWS, E_DEV)), rim, rim, rim, rim,
            whole((3, NB, NB)), whole((4, NP, NB)), whole((4, NP, NB)),
        ],
        out_specs=lanes(NB, NQ),
        out_shape=shape((NB, NQ, E_DEV), F32),
        scratch_shapes=[
            pltpu.VMEM((80, NE * LANES), F32), pltpu.VMEM((64, LANES), F32),
            pltpu.VMEM((80, 96), BF), pltpu.VMEM((64, 96), BF), pltpu.VMEM((32, 192), BF),
            pltpu.VMEM((96, 96), BF), pltpu.VMEM((2 * ROWS, 4 * BND), BF),
            pltpu.VMEM((NBP, NE * LANES), F32), pltpu.VMEM((32, NE * LANES), F32),
            pltpu.VMEM((NQ, NBP, LANES), F32),
        ],
        compiler_params=params,
        name="elements",
    )(
        integ, dofs, star, couple, omega, flux_minus, flux_plus, area, nbr_elem, nbr_face,
        ihl, r0, r1, r2, r3, kdiff, face_proj, face_lift,
    )
    anywhere = pl.BlockSpec(memory_space=pl.ANY)
    result = pl.pallas_call(
        fault_kernel,
        grid=(SLOTS // SC,),
        in_specs=[
            anywhere, lines, lines, kept,
            slots, slots, slots, slots, slots, whole((4, NP, NB)),
        ],
        out_specs=anywhere,
        out_shape=shape((NB, NQ, E_DEV), F32),
        input_output_aliases={0: 0},
        scratch_shapes=[
            pltpu.VMEM((64, LANES), F32), pltpu.VMEM((96, 48), BF), pltpu.VMEM((SLOTS // SC, 96, E_DEV), F32),
            pltpu.VMEM((NB, 8, E_DEV), F32), pltpu.SemaphoreType.DMA,
        ],
        compiler_params=params,
        name="fault",
    )(
        base, out, theirs, keep, fault_send_elem, fault_send_face, fault_minus_elem,
        fault_minus_face, fault_live, face_lift,
    )
    return jnp.transpose(result, (1, 0, 2))


def solution(mesh):
    both = ("strike", "depth")
    split_1, split_2, split_3 = P(None, both), P(None, None, both), P(None, None, None, both)
    in_specs = (
        split_2, split_3, P(), split_2, split_1, split_2, split_2, split_1, P(), P(),
        split_1, split_1, P(both), split_1,
        *[P(both, None)] * 5, P(both, None, None), P(both, None, None),
    )
    return jax.shard_map(
        per_device, mesh=mesh, in_specs=in_specs, out_specs=split_2, check_vma=False
    )
```

time: 69.7 us -> 58.9 us (0.85)
  the two profiles are of different devices: /device:TPU:8 before, /device:TPU:4 now
where the time goes in v2:
time: 58.9 us; the launch traced here: 58.4 us
  Pallas kernels  29.8 us (51%)
  starting transfers between devices  17.6 us (30%)
  waiting for transfers between devices  9.29 us (16%)
  local copies, waits for them, and re-layouts  1.61 us (3%)
    all_to_all x1, starting transfers between devices, per_device(): lax.all_to_all(out.reshape(DEVICES, 1, TILES * LANES), ('strike', 'depth'...  10.5 us
    pallas_call x1, Pallas kernels, per_device(): pl.pallas_call(element_kernel, grid=(CHUNKS,), in_specs=[lanes(NQ, NBP),...  9.42 us
    ppermute x4, waiting for transfers between devices, swap(): return lax.ppermute(x, axis, ends + [(j, i) for i, j in ends])  9.29 us
    pallas_call x1, Pallas kernels, per_device(): pl.pallas_call(predict_kernel, grid=(CHUNKS,), in_specs=[lanes(NB, NQ), l...  8.71 us
    ppermute x4, starting transfers between devices, swap(): return lax.ppermute(x, axis, ends + [(j, i) for i, j in ends])  7.06 us
    pallas_call x1, Pallas kernels, per_device(): pl.pallas_call(fault_kernel, grid=(SLOTS // SC,), in_specs=[anywhere, lin...  5.84 us
    pallas_call x1, Pallas kernels, per_device(): pl.pallas_call(slot_kernel, grid=(SLOTS // SC,), in_specs=[whole((160, E_...  5.81 us
    unnamed x18, local copies, waits for them, and re-layouts  1.61 us
  transfers between devices with their start and end apart: 5, of which 1 were waited for; matrix products, arithmetic and copies ran while one was open for 0% of the time, Pallas kernels for 16%

profile of v2, /device:TPU:4, one launch (start us, length us, event | category | flops | bytes accessed | tf_op | source)
XLA Modules:
  0.0 58.4 jit_solution(11480101732350852221)
XLA Ops:
  0.0 8.7 %predict.1 = (f32[27,24,512]{2,1,0:T(8,128)}, bf16[448,512]{1,0:T(8,128)(2,1)}, bf16[160,512]{1,0:T(8,128)(2,1)}, f32[9,20,128]{2,1,0:T(8,128)}, f32[9,20,128]{2...) custom-call(f32[20,27,512]{2,1,0:T(8,128)} %bitcast.7, f32[9,9,3,512]{3,2,1,0:T(4,128)} %bitcast.11, ...), custom_call_target="tpu_custom_call" | custom-call | tf_op jit(solution)/shard_map/predict/pallas_call | solution.py:403
  8.7 0.0 copy-start.8
  8.7 0.0 copy-start.7
  8.7 0.0 copy-start.6
  8.7 0.0 copy-start.5
  8.8 5.8 %slots.1 = (f32[1664,128]{1,0:T(8,128)}, f32[128,512]{1,0:T(8,128)}) custom-call(bf16[160,512]{1,0:T(8,128)(2,1)} %get-tuple-element.20.fhl, f32[4,16,20]{2,1,0:T(8,128)} %bitcast.13, s32[1,2048]{1,0:T(1,128)} %fse.3, s32[1,2048]{1,0:T(1,128)} %fsf.3, s32[1,2048]{1,0:T(1,128)} %fme.3, s32[1,2048]{1,0:T(1,128)} %fmf.3, s32[1,2048]{1,0:T(1,128)} %live.3, ...), custom_call_target="tpu_custom_call" | custom-call | tf_op jit(solution)/shard_map/slots/pallas_call | solution.py:424
  14.6 10.5 %all-to-all-start = ((f32[128,1,1664]{2,1,0:T(1,128)}), f32[128,1,1664]{2,1,0:T(1,128)S(1)}, u32[]{:S(2)}, u32[]{:S(2)}) async-start(f32[128,1,1664]{2,1,0:T(1,128)} %bitcast.9), calls=%async_computation | async-start | bytes 1703936 | tf_op jit(solution)/shard_map/all_to_all | solution.py:447
  25.1 0.0 copy-done.8
  25.1 0.2 collective-permute-start
  25.3 0.0 copy-done.7
  25.3 5.6 %collective-permute-start.1 = (f32[9,20,128]{2,1,0:T(8,128)S(1)}, f32[9,20,128]{2,1,0:T(8,128)S(1)}, u32[]{:S(2)}, u32[]{:S(2)}) collective-permute-start(f32[9,20,128]{2,1,0:T(8,128)S(1)} %copy-done.7), channel_id=1, source_target_pairs={{4,8},{12,16},{20,24},{28,32},{36,40},{44,48},{52,56},{60,64},{68,... | collective-permute-start | bytes 276488 | tf_op jit(solution)/shard_map/ppermute | solution.py:441
  31.0 0.0 copy-done.6
  31.0 1.2 %collective-permute-start.2 = (f32[9,20,128]{2,1,0:T(8,128)S(1)}, f32[9,20,128]{2,1,0:T(8,128)S(1)}, u32[]{:S(2)}, u32[]{:S(2)}) collective-permute-start(f32[9,20,128]{2,1,0:T(8,128)S(1)} %copy-done.6), channel_id=1, source_target_pairs={{0,1},{2,3},{1,0},{3,2},{4,5},{6,7},{5,4},{7,6},{8,9},{10,11},{9,8... | collective-permute-start | bytes 276488 | tf_op jit(solution)/shard_map/ppermute | solution.py:441
  32.1 0.0 copy-done.5
  32.1 0.0 collective-permute-start.3
  32.2 0.0 collective-permute-done.rim0
  32.2 0.0 copy-start.1
  32.2 9.3 %collective-permute-done.1.rim1 = f32[9,20,128]{2,1,0:T(8,128)S(1)} collective-permute-done((f32[9,20,128]{2,1,0:T(8,128)S(1)}, f32[9,20,128]{2,1,0:T(8,128)S(1)}, u32[]{:S(2)}, u32[]{:S(2)}) %collective-permute-start.1) | collective-permute-done | bytes 92192 | tf_op jit(solution)/shard_map/ppermute | solution.py:441
  41.5 0.0 copy-start.2
  41.5 0.0 collective-permute-done.2.rim2
  41.5 0.0 copy-start.3
  41.5 0.0 collective-permute-done.3.rim3
  41.5 0.0 copy-start.4
  41.5 0.0 copy-done.1
  41.5 0.6 %copy-done.2 = f32[9,20,128]{2,1,0:T(8,128)} copy-done((f32[9,20,128]{2,1,0:T(8,128)}, f32[9,20,128]{2,1,0:T(8,128)S(1)}, u32[]{:S(2)}) %copy-start.2) | copy-done | bytes 92184
  42.1 0.0 copy-done.3
  42.1 0.0 copy-done.4
  42.2 9.4 %elements.1.base_in = f32[20,27,512]{2,1,0:T(8,128)} custom-call(f32[27,24,512]{2,1,0:T(8,128)} %get-tuple-element.14.integ, f32[20,27,512]{2,1,0:T(8,128)} %bitcast.8, f32[9,9,3,512]{3,2,1,0:T(4,128)} %bitcast.12, f32[3,6,512]{2,1,0:T(8,128)} %couple.3, f32[3,512]{1,0:T(4,128)} %omega.3, f32[9,9,512]{2,1,0:T(8,128)} %fminus.1, f32[9,9,512]{2,1,0:T(8,128)} %fplus.1, ...), custom_call_target="tpu_custom_call" | custom-call | tf_op jit(solution)/shard_map/elements/pallas_call | solution.py:450
  51.6 0.0 all-to-all-done
  51.6 0.0 copy-start
  51.6 0.9 %copy-done = f32[128,1,1664]{2,1,0:T(1,128)} copy-done((f32[128,1,1664]{2,1,0:T(1,128)}, f32[128,1,1664]{2,1,0:T(1,128)S(1)}, u32[]{:S(2)}) %copy-start) | copy-done | bytes 851992
  52.5 5.8 %fault.1 = f32[20,27,512]{2,1,0:T(8,128)} custom-call(f32[20,27,512]{2,1,0:T(8,128)} %elements.1.base_in, f32[1664,128]{1,0:T(8,128)} %get-tuple-element.21.mine, f32[1664,128]{1,0:T(8,128)} %bitcast.10, f32[128,512]{1,0:T(8,128)} %get-tuple-element.22.keep, s32[1,2048]{1,0:T(1,128)} %fse.3, s32[1,2048]{1,0:T(1,128)} %fsf.3, ...), custom_call_target="tpu_custom_call", output_to_operand_aliasing={{}: (0, {})} | custom-call | tf_op jit(solution)/shard_map/fault/pallas_call | solution.py:475
Async XLA Ops:
  8.7 16.4 %copy-start.8 = (f32[9,20,128]{2,1,0:T(8,128)S(1)}, f32[9,20,128]{2,1,0:T(8,128)}, u32[]{:S(2)}) copy-start(f32[9,20,128]{2,1,0:T(8,128)} %get-tuple-element.16) | copy-start | bytes 276484
  8.7 16.6 %copy-start.7 = (f32[9,20,128]{2,1,0:T(8,128)S(1)}, f32[9,20,128]{2,1,0:T(8,128)}, u32[]{:S(2)}) copy-start(f32[9,20,128]{2,1,0:T(8,128)} %get-tuple-element.17) | copy-start | bytes 276484
  8.7 22.2 %copy-start.6 = (f32[9,20,128]{2,1,0:T(8,128)S(1)}, f32[9,20,128]{2,1,0:T(8,128)}, u32[]{:S(2)}) copy-start(f32[9,20,128]{2,1,0:T(8,128)} %get-tuple-element.18) | copy-start | bytes 276484
  8.7 23.4 %copy-start.5 = (f32[9,20,128]{2,1,0:T(8,128)S(1)}, f32[9,20,128]{2,1,0:T(8,128)}, u32[]{:S(2)}) copy-start(f32[9,20,128]{2,1,0:T(8,128)} %get-tuple-element.19) | copy-start | bytes 276484
  14.6 37.0 %all-to-all-start = ((f32[128,1,1664]{2,1,0:T(1,128)}), f32[128,1,1664]{2,1,0:T(1,128)S(1)}, u32[]{:S(2)}, u32[]{:S(2)}) async-start(f32[128,1,1664]{2,1,0:T(1,128)} %bitcast.9), calls=%async_computation | async-start | bytes 1703936 | tf_op jit(solution)/shard_map/all_to_all | solution.py:447
  25.1 7.1 %collective-permute-start = (f32[9,20,128]{2,1,0:T(8,128)S(1)}, f32[9,20,128]{2,1,0:T(8,128)S(1)}, u32[]{:S(2)}, u32[]{:S(2)}) collective-permute-start(f32[9,20,128]{2,1,0:T(8,128)S(1)} %copy-done.8), channel_id=1, source_target_pairs={{0,4},{8,12},{16,20},{24,28},{32,36},{40,44},{48,52},{56,60},{64,6... | collective-permute-start | bytes 276488 | tf_op jit(solution)/shard_map/ppermute | solution.py:441
  25.3 16.1 %collective-permute-start.1 = (f32[9,20,128]{2,1,0:T(8,128)S(1)}, f32[9,20,128]{2,1,0:T(8,128)S(1)}, u32[]{:S(2)}, u32[]{:S(2)}) collective-permute-start(f32[9,20,128]{2,1,0:T(8,128)S(1)} %copy-done.7), channel_id=1, source_target_pairs={{4,8},{12,16},{20,24},{28,32},{36,40},{44,48},{52,56},{60,64},{68,... | collective-permute-start | bytes 276488 | tf_op jit(solution)/shard_map/ppermute | solution.py:441
  31.0 10.5 %collective-permute-start.2 = (f32[9,20,128]{2,1,0:T(8,128)S(1)}, f32[9,20,128]{2,1,0:T(8,128)S(1)}, u32[]{:S(2)}, u32[]{:S(2)}) collective-permute-start(f32[9,20,128]{2,1,0:T(8,128)S(1)} %copy-done.6), channel_id=1, source_target_pairs={{0,1},{2,3},{1,0},{3,2},{4,5},{6,7},{5,4},{7,6},{8,9},{10,11},{9,8... | collective-permute-start | bytes 276488 | tf_op jit(solution)/shard_map/ppermute | solution.py:441
  32.1 9.3 %collective-permute-start.3 = (f32[9,20,128]{2,1,0:T(8,128)S(1)}, f32[9,20,128]{2,1,0:T(8,128)S(1)}, u32[]{:S(2)}, u32[]{:S(2)}) collective-permute-start(f32[9,20,128]{2,1,0:T(8,128)S(1)} %copy-done.5), channel_id=1, source_target_pairs={{1,2},{3,0},{2,1},{0,3},{5,6},{7,4},{6,5},{4,7},{9,10},{11,8},{10,... | collective-permute-start | bytes 276488 | tf_op jit(solution)/shard_map/ppermute | solution.py:441
  32.2 9.3 %copy-start.1 = (f32[9,20,128]{2,1,0:T(8,128)}, f32[9,20,128]{2,1,0:T(8,128)S(1)}, u32[]{:S(2)}) copy-start(f32[9,20,128]{2,1,0:T(8,128)S(1)} %collective-permute-done.rim0) | copy-start | bytes 276484
  41.5 0.6 %copy-start.2 = (f32[9,20,128]{2,1,0:T(8,128)}, f32[9,20,128]{2,1,0:T(8,128)S(1)}, u32[]{:S(2)}) copy-start(f32[9,20,128]{2,1,0:T(8,128)S(1)} %collective-permute-done.1.rim1) | copy-start | bytes 276484
  41.5 0.7 %copy-start.3 = (f32[9,20,128]{2,1,0:T(8,128)}, f32[9,20,128]{2,1,0:T(8,128)S(1)}, u32[]{:S(2)}) copy-start(f32[9,20,128]{2,1,0:T(8,128)S(1)} %collective-permute-done.2.rim2) | copy-start | bytes 276484
  41.5 0.7 %copy-start.4 = (f32[9,20,128]{2,1,0:T(8,128)}, f32[9,20,128]{2,1,0:T(8,128)S(1)}, u32[]{:S(2)}) copy-start(f32[9,20,128]{2,1,0:T(8,128)S(1)} %collective-permute-done.3.rim3) | copy-start | bytes 276484
  51.6 0.9 %copy-start = (f32[128,1,1664]{2,1,0:T(1,128)}, f32[128,1,1664]{2,1,0:T(1,128)S(1)}, u32[]{:S(2)}) copy-start(f32[128,1,1664]{2,1,0:T(1,128)S(1)} %all-to-all-done) | copy-start | bytes 2555908

commit v3 on v2

--- a/solution.py
+++ b/solution.py
@@ -68,8 +68,13 @@
 
 
 def one_hot(index, rows, base=0):
-    row = lax.broadcasted_iota(jnp.int32, (rows, index.shape[1]), 0) + base
-    return jnp.where(row == index, 1.0, 0.0).astype(BF)
+    row = lax.broadcasted_iota(jnp.int32, (rows, LANES), 0).astype(jnp.int16)
+    index = jnp.broadcast_to(index - base, (16, index.shape[1])).astype(jnp.int16)
+    out = []
+    for t in range(index.shape[1] // LANES):
+        here = jnp.concatenate([index[:, t * LANES : (t + 1) * LANES]] * (rows // 16), axis=0)
+        out.append(jnp.where(row == here, jnp.ones((), BF), jnp.zeros((), BF)))
+    return jnp.concatenate(out, axis=1)
 
 
 def swap_blocks(x):
@@ -96,29 +101,30 @@
     return jnp.concatenate([x[8 * t : 8 * t + 8] for t in range(SC // LANES)], axis=1)
 
 
-def stress_of(get, star_ref, kd, grads):
-    right = jnp.concatenate([stack3(pad_rows(get(j), 32)) for j in range(NE)], axis=1)
-    grads[...] = dot(kd, right)
-    acc = [None] * NE
-    for d in range(3):
-        for j in range(NE):
-            g = grads[d * NBP : (d + 1) * NBP, j * LANES : (j + 1) * LANES]
-            for i in range(NE):
-                t = star_ref[i, j, d : d + 1, :] * g
-                acc[i] = t if acc[i] is None else acc[i] + t
-    return acc
+def stress_of(get, star_ref, kd, rows=range(NE)):
+    fields = [get(j) for j in range(NE)]
+    out = []
+    for i in rows:
+        mixed = []
+        for d in range(3):
+            t = star_ref[i, 0, d : d + 1, :] * fields[0]
+            for j in range(1, NE):
+                t = t + star_ref[i, j, d : d + 1, :] * fields[j]
+            mixed.append(t)
+        out.append(dot(kd, stack3(pad_rows(jnp.concatenate(mixed, axis=0), 80)))[0:NBP])
+    return out
 
 
 def predict_kernel(
     dofs, star, couple, omega, wc, kdiff, srow,
     integ, ihl, fhl, send0, send1, send2, send3,
-    term, grads, mat, kdw,
+    term, mat, kdw,
 ):
     c = pl.program_id(0)
 
     @pl.when(c == 0)
     def _():
-        kdw[...] = left3(mat, [(0, d * NBP, kdiff[d]) for d in range(3)], 32, 80)
+        kdw[...] = left3(mat, [(d * NBP, 0, kdiff[d]) for d in range(3)], 80, 32)
         term[...] = jnp.zeros(term.shape, F32)
 
     kd = kdw[...]
@@ -128,7 +134,7 @@
         integ[q] = step * term[q]
 
     def turn(order, power):
-        acc = stress_of(lambda j: term[j], star, kd, grads)
+        acc = stress_of(lambda j: term[j], star, kd)
         for q in range(6):
             old = [term[NE + 6 * l + q] for l in range(MECH)]
             relax = couple[0, q : q + 1, :] * old[0]
@@ -213,7 +219,7 @@
 
 def element_kernel(
     integ, dofs, star, couple, omega, fminus, fplus, area, nelem, nface, ihl, rim0, rim1, rim2, rim3,
-    kdiff, proj, lift, base, grads, mat, kdw, fpw, ltw, plw, rhl, own, near, change,
+    kdiff, proj, lift, base, mat, kdw, fpw, ltw, plw, rhl, change,
 ):
     c = pl.program_id(0)
 
@@ -225,7 +231,7 @@
 
     @pl.when(c == 0)
     def _():
-        kdw[...] = left3(mat, [(0, d * NBP, kdiff[d]) for d in range(3)], 32, 80)
+        kdw[...] = left3(mat, [(d * NBP, 0, kdiff[d]) for d in range(3)], 80, 32)
         fpw[...] = left3(mat, [(0, g * NP, proj[g].T) for g in range(4)], 32, 64)
         ltw[...] = left3(mat, [(f * NP, 0, lift[f]) for f in range(4)], 64, 32)
         both = [
@@ -244,51 +250,65 @@
             after = (at < lax.axis_size(axis) - 1).astype(F32)
             for side, one, two in ((k, odd * before, even * before), (k + 1, even * after, odd * after)):
                 put_rim(side, [one * first[j] + two * second[j] for j in range(NE)])
-    elem = jnp.concatenate([nelem[f : f + 1, :] for f in range(4)], axis=1)
-    face = jnp.concatenate([nface[f : f + 1, :] for f in range(4)], axis=1)
-    scale = jnp.concatenate([area[f : f + 1, :] for f in range(4)], axis=1)
-    got = dot(ihl[...], one_hot(elem, E_DEV)) + dot(rhl[...], one_hot(elem, 4 * BND, E_DEV))
-    lifted = []
-    for j in range(NE):
-        h = pad_rows(got[j * NBP : (j + 1) * NBP], 32).astype(BF)
-        l = pad_rows(got[ROWS + j * NBP : ROWS + (j + 1) * NBP], 32).astype(BF)
-        points = dot(fpw[...], jnp.concatenate([h, h, l], axis=0))
-        v = points[0:NP]
-        for g in range(1, 4):
-            v = jnp.where(face == g, points[g * NP : (g + 1) * NP], v)
-        v = v * scale
-        v = jnp.concatenate([v[:, f * LANES : (f + 1) * LANES] for f in range(4)], axis=0)
-        lifted.append(stack3(v))
-    near[...] = dot(ltw[...], jnp.concatenate(lifted, axis=1))
-
-    right = jnp.concatenate([stack3(pad_rows(integ[j], 32)) for j in range(NE)], axis=1)
-    folded = dot(plw[...], right)
-    for j in range(NE):
-        cols = slice(j * LANES, (j + 1) * LANES)
-        w = area[0:1, :] * folded[0:NBP, cols]
-        for f in range(1, 4):
-            w = w + area[f : f + 1, :] * folded[f * NBP : (f + 1) * NBP, cols]
-        own[:, cols] = w
-
-    acc = stress_of(lambda j: integ[j], star, kdw[...], grads)
-    total = []
+    def spread(ref):
+        return jnp.concatenate([ref[f : f + 1, :] for f in range(4)], axis=1)
+
+    def gather():
+        elem = spread(nelem)
+        return dot(ihl[...], one_hot(elem, E_DEV)) + dot(rhl[...], one_hot(elem, 4 * BND, E_DEV))
+
+    def project(got):
+        right = []
+        for j in range(NE):
+            hi = pad_rows(got[j * NBP : (j + 1) * NBP], 32).astype(BF)
+            lo = pad_rows(got[ROWS + j * NBP : ROWS + (j + 1) * NBP], 32).astype(BF)
+            right.append(jnp.concatenate([hi, hi, lo], axis=0))
+        return dot(fpw[...], jnp.concatenate(right, axis=1))
+
+    def choose(points):
+        face, scale = spread(nface), spread(area)
+        out = []
+        for j in range(NE):
+            cols = slice(j * E_DEV, (j + 1) * E_DEV)
+            v = points[0:NP, cols]
+            for g in range(1, 4):
+                v = jnp.where(face == g, points[g * NP : (g + 1) * NP, cols], v)
+            v = v * scale
+            out.append(jnp.concatenate([v[:, f * LANES : (f + 1) * LANES] for f in range(4)], axis=0))
+        return out
+
+    kd = kdw[...]
+    got = gather()
+    acc = stress_of(lambda j: integ[j], star, kd)
+    folded = dot(plw[...], jnp.concatenate([stack3(pad_rows(integ[j], 32)) for j in range(NE)], axis=1))
+    points = project(got)
     for q in range(6):
         old = [integ[NE + 6 * l + q] for l in range(MECH)]
         relax = couple[0, q : q + 1, :] * old[0]
         for l in range(1, MECH):
             relax = relax + couple[l, q : q + 1, :] * old[l]
         for l in range(MECH):
-            at = NE + 6 * l + q
-            change[at] = omega[l : l + 1, :] * (acc[q] - old[l])
-        total.append(acc[q] - relax)
-    total = total + acc[6:]
+            change[NE + 6 * l + q] = omega[l : l + 1, :] * (acc[q] - old[l])
+        change[q] = acc[q] - relax
+    for q in range(6, NE):
+        change[q] = acc[q]
+    total = [None] * NE
     for j in range(NE):
         cols = slice(j * LANES, (j + 1) * LANES)
-        w, v = own[:, cols], near[0:NBP, cols]
+        w = area[0:1, :] * folded[0:NBP, cols]
+        for f in range(1, 4):
+            w = w + area[f : f + 1, :] * folded[f * NBP : (f + 1) * NBP, cols]
         for i in range(NE):
-            total[i] = total[i] + (fminus[i, j : j + 1, :] * w + fplus[i, j : j + 1, :] * v)
+            t = fminus[i, j : j + 1, :] * w
+            total[i] = t if j == 0 else total[i] + t
     for i in range(NE):
-        change[i] = total[i]
+        change[i] += total[i]
+    lifted = dot(ltw[...], jnp.concatenate([stack3(v) for v in choose(points)], axis=1))
+    for i in range(NE):
+        t = change[i]
+        for j in range(NE):
+            t = t + fplus[i, j : j + 1, :] * lifted[0:NBP, j * LANES : (j + 1) * LANES]
+        change[i] = t
     base[...] = dofs[...] + jnp.transpose(change[:, 0:NB, :], (1, 0, 2))
 
 
@@ -412,11 +432,11 @@
         ],
         out_shape=[
             shape((NQ, NBP, E_DEV), F32), shape((2 * ROWS, E_DEV), BF), shape((160, E_DEV), BF),
-            *[shape((NE, NB, BND), F32)] * 4,
+            *[pltpu.HBM((NE, NB, BND), F32)] * 4,
         ],
         scratch_shapes=[
-            pltpu.VMEM((NQ, NBP, LANES), F32), pltpu.VMEM((80, NE * LANES), F32),
-            pltpu.VMEM((64, LANES), F32), pltpu.VMEM((80, 96), BF),
+            pltpu.VMEM((NQ, NBP, LANES), F32), pltpu.VMEM((80, LANES), F32),
+            pltpu.VMEM((32, 240), BF),
         ],
         compiler_params=params,
         name="predict",
@@ -444,8 +464,9 @@
     r1 = swap(s1, "strike", ns, 1)
     r2 = swap(s2, "depth", nd, 0)
     r3 = swap(s3, "depth", nd, 1)
+    r0, r1, r2, r3, sent = lax.optimization_barrier((r0, r1, r2, r3, out))
     theirs = lax.all_to_all(
-        out.reshape(DEVICES, 1, TILES * LANES), ("strike", "depth"), split_axis=0, concat_axis=0, tiled=True
+        sent.reshape(DEVICES, 1, TILES * LANES), ("strike", "depth"), split_axis=0, concat_axis=0, tiled=True
     ).reshape(DEVICES * TILES, LANES)
     base = pl.pallas_call(
         element_kernel,
@@ -457,12 +478,11 @@
             whole((3, NB, NB)), whole((4, NP, NB)), whole((4, NP, NB)),
         ],
         out_specs=lanes(NB, NQ),
-        out_shape=shape((NB, NQ, E_DEV), F32),
+        out_shape=pltpu.HBM((NB, NQ, E_DEV), F32),
         scratch_shapes=[
-            pltpu.VMEM((80, NE * LANES), F32), pltpu.VMEM((64, LANES), F32),
-            pltpu.VMEM((80, 96), BF), pltpu.VMEM((64, 96), BF), pltpu.VMEM((32, 192), BF),
+            pltpu.VMEM((80, LANES), F32),
+            pltpu.VMEM((32, 240), BF), pltpu.VMEM((64, 96), BF), pltpu.VMEM((32, 192), BF),
             pltpu.VMEM((96, 96), BF), pltpu.VMEM((2 * ROWS, 4 * BND), BF),
-            pltpu.VMEM((NBP, NE * LANES), F32), pltpu.VMEM((32, NE * LANES), F32),
             pltpu.VMEM((NQ, NBP, LANES), F32),
         ],
         compiler_params=params,
@@ -489,7 +509,7 @@
         compiler_params=params,
         name="fault",
     )(
-        base, out, theirs, keep, fault_send_elem, fault_send_face, fault_minus_elem,
+        base, sent, theirs, keep, fault_send_elem, fault_send_face, fault_minus_elem,
         fault_minus_face, fault_live, face_lift,
     )
     return jnp.transpose(result, (1, 0, 2))

time: 58.9 us -> 54.3 us (0.922)
  the two profiles are of different devices: /device:TPU:4 before, /device:TPU:1 now
where the time goes in v3:
time: 54.3 us; the launch traced here: 53.8 us
  Pallas kernels  28 us (52%)
  starting transfers between devices  15.2 us (28%)
  waiting for transfers between devices  9.49 us (17%)
  local copies, waits for them, and re-layouts  0.94 us (2%)
    all_to_all x1, waiting for transfers between devices, per_device(): lax.all_to_all(sent.reshape(DEVICES, 1, TILES * LANES), ('strike', 'depth...  9.48 us
    all_to_all x1, starting transfers between devices, per_device(): lax.all_to_all(sent.reshape(DEVICES, 1, TILES * LANES), ('strike', 'depth...  8.98 us
    pallas_call x1, Pallas kernels, per_device(): pl.pallas_call(element_kernel, grid=(CHUNKS,), in_specs=[lanes(NQ, NBP),...  8.26 us
    pallas_call x1, Pallas kernels, per_device(): pl.pallas_call(predict_kernel, grid=(CHUNKS,), in_specs=[lanes(NB, NQ), l...  8.23 us
    ppermute x4, starting transfers between devices, swap(): return lax.ppermute(x, axis, ends + [(j, i) for i, j in ends])  6.23 us
    pallas_call x1, Pallas kernels, per_device(): pl.pallas_call(fault_kernel, grid=(SLOTS // SC,), in_specs=[anywhere, lin...  5.84 us
    pallas_call x1, Pallas kernels, per_device(): pl.pallas_call(slot_kernel, grid=(SLOTS // SC,), in_specs=[whole((160, E_...  5.69 us
  transfers between devices with their start and end apart: 5, of which 1 were waited for; matrix products, arithmetic and copies ran while one was open for 0% of the time, Pallas kernels for 26%

profile of v3, /device:TPU:1, one launch (start us, length us, event | category | flops | bytes accessed | tf_op | source)
XLA Modules:
  0.0 53.8 jit_solution(16940640545254595111)
XLA Ops:
  0.0 8.2 %predict.1 = (f32[27,24,512]{2,1,0:T(8,128)}, bf16[448,512]{1,0:T(8,128)(2,1)}, bf16[160,512]{1,0:T(8,128)(2,1)}, f32[9,20,128]{2,1,0:T(8,128)}, f32[9,20,128]{2...) custom-call(f32[20,27,512]{2,1,0:T(8,128)} %bitcast.7, f32[9,9,3,512]{3,2,1,0:T(4,128)} %bitcast.11, ...), custom_call_target="tpu_custom_call" | custom-call | tf_op jit(solution)/shard_map/predict/pallas_call | solution.py:423
  8.2 1.5 %collective-permute-start = (f32[9,20,128]{2,1,0:T(8,128)}, f32[9,20,128]{2,1,0:T(8,128)S(1)}, u32[]{:S(2)}, u32[]{:S(2)}) collective-permute-start(f32[9,20,128]{2,1,0:T(8,128)} %get-tuple-element.21), channel_id=1, source_target_pairs={{0,4},{8,12},{16,20},{24,28},{32,36},{40,44},{48,52},{56,60},{64,6... | collective-permute-start | bytes 276488 | tf_op jit(solution)/shard_map/ppermute | solution.py:461
  9.7 1.7 %collective-permute-start.1 = (f32[9,20,128]{2,1,0:T(8,128)}, f32[9,20,128]{2,1,0:T(8,128)S(1)}, u32[]{:S(2)}, u32[]{:S(2)}) collective-permute-start(f32[9,20,128]{2,1,0:T(8,128)} %get-tuple-element.22), channel_id=1, source_target_pairs={{4,8},{12,16},{20,24},{28,32},{36,40},{44,48},{52,56},{60,64},{68,... | collective-permute-start | bytes 276488 | tf_op jit(solution)/shard_map/ppermute | solution.py:461
  11.4 1.2 %collective-permute-start.2 = (f32[9,20,128]{2,1,0:T(8,128)}, f32[9,20,128]{2,1,0:T(8,128)S(1)}, u32[]{:S(2)}, u32[]{:S(2)}) collective-permute-start(f32[9,20,128]{2,1,0:T(8,128)} %get-tuple-element.23), channel_id=1, source_target_pairs={{0,1},{2,3},{1,0},{3,2},{4,5},{6,7},{5,4},{7,6},{8,9},{10,11},{9,8... | collective-permute-start | bytes 276488 | tf_op jit(solution)/shard_map/ppermute | solution.py:461
  12.6 1.8 %collective-permute-start.3 = (f32[9,20,128]{2,1,0:T(8,128)}, f32[9,20,128]{2,1,0:T(8,128)S(1)}, u32[]{:S(2)}, u32[]{:S(2)}) collective-permute-start(f32[9,20,128]{2,1,0:T(8,128)} %get-tuple-element.24), channel_id=1, source_target_pairs={{1,2},{3,0},{2,1},{0,3},{5,6},{7,4},{6,5},{4,7},{9,10},{11,8},{10,... | collective-permute-start | bytes 276488 | tf_op jit(solution)/shard_map/ppermute | solution.py:461
  14.5 5.7 %slots.1 = (f32[1664,128]{1,0:T(8,128)}, f32[128,512]{1,0:T(8,128)}) custom-call(bf16[160,512]{1,0:T(8,128)(2,1)} %get-tuple-element.25.fhl, f32[4,16,20]{2,1,0:T(8,128)} %bitcast.13, s32[1,2048]{1,0:T(1,128)} %fse.3, s32[1,2048]{1,0:T(1,128)} %fsf.3, s32[1,2048]{1,0:T(1,128)} %fme.3, s32[1,2048]{1,0:T(1,128)} %fmf.3, s32[1,2048]{1,0:T(1,128)} %live.3, ...), custom_call_target="tpu_custom_call" | custom-call | tf_op jit(solution)/shard_map/slots/pallas_call | solution.py:444
  20.1 0.0 collective-permute-done.rim0
  20.2 0.0 copy-start.1
  20.2 0.0 collective-permute-done.1.rim1
  20.2 0.0 copy-start.2
  20.2 0.0 collective-permute-done.2.rim2
  20.2 0.0 copy-start.3
  20.2 0.0 collective-permute-done.3.rim3
  20.2 0.0 copy-start.4
  20.2 9.0 %all-to-all-start = ((f32[128,1,1664]{2,1,0:T(1,128)}), f32[128,1,1664]{2,1,0:T(1,128)S(1)}, u32[]{:S(2)}, u32[]{:S(2)}) async-start(f32[128,1,1664]{2,1,0:T(1,128)} %bitcast.9), calls=%async_computation | async-start | bytes 1703936 | tf_op jit(solution)/shard_map/all_to_all | solution.py:468
  29.2 0.0 copy-done.1
  29.2 0.0 copy-done.2
  29.2 0.0 copy-done.3
  29.2 0.0 copy-done.4
  29.3 8.3 %elements.1.base_in = f32[20,27,512]{2,1,0:T(8,128)} custom-call(f32[27,24,512]{2,1,0:T(8,128)} %get-tuple-element.19.integ, f32[20,27,512]{2,1,0:T(8,128)} %bitcast.8, f32[9,9,3,512]{3,2,1,0:T(4,128)} %bitcast.12, f32[3,6,512]{2,1,0:T(8,128)} %couple.3, f32[3,512]{1,0:T(4,128)} %omega.3, f32[9,9,512]{2,1,0:T(8,128)} %fminus.1, f32[9,9,512]{2,1,0:T(8,128)} %fplus.1, ...), custom_call_target="tpu_custom_call" | custom-call | tf_op jit(solution)/shard_map/elements/pallas_call | solution.py:471
  37.5 9.5 %all-to-all-done = f32[128,1,1664]{2,1,0:T(1,128)S(1)} async-done(((f32[128,1,1664]{2,1,0:T(1,128)}), f32[128,1,1664]{2,1,0:T(1,128)S(1)}, u32[]{:S(2)}, u32[]{:S(2)}) %all-to-all-start) | async-done | bytes 852000 | tf_op jit(solution)/shard_map/all_to_all | solution.py:468
  47.0 0.0 copy-start
  47.0 0.9 %copy-done = f32[128,1,1664]{2,1,0:T(1,128)} copy-done((f32[128,1,1664]{2,1,0:T(1,128)}, f32[128,1,1664]{2,1,0:T(1,128)S(1)}, u32[]{:S(2)}) %copy-start) | copy-done | bytes 851992
  47.9 5.8 %fault.1 = f32[20,27,512]{2,1,0:T(8,128)} custom-call(f32[20,27,512]{2,1,0:T(8,128)} %elements.1.base_in, f32[1664,128]{1,0:T(8,128)} %get-tuple-element.31.mine, f32[1664,128]{1,0:T(8,128)} %bitcast.10, f32[128,512]{1,0:T(8,128)} %get-tuple-element.32.keep, s32[1,2048]{1,0:T(1,128)} %fse.3, s32[1,2048]{1,0:T(1,128)} %fsf.3, ...), custom_call_target="tpu_custom_call", output_to_operand_aliasing={{}: (0, {})} | custom-call | tf_op jit(solution)/shard_map/fault/pallas_call | solution.py:495
Async XLA Ops:
  8.2 11.9 %collective-permute-start = (f32[9,20,128]{2,1,0:T(8,128)}, f32[9,20,128]{2,1,0:T(8,128)S(1)}, u32[]{:S(2)}, u32[]{:S(2)}) collective-permute-start(f32[9,20,128]{2,1,0:T(8,128)} %get-tuple-element.21), channel_id=1, source_target_pairs={{0,4},{8,12},{16,20},{24,28},{32,36},{40,44},{48,52},{56,60},{64,6... | collective-permute-start | bytes 276488 | tf_op jit(solution)/shard_map/ppermute | solution.py:461
  9.7 10.4 %collective-permute-start.1 = (f32[9,20,128]{2,1,0:T(8,128)}, f32[9,20,128]{2,1,0:T(8,128)S(1)}, u32[]{:S(2)}, u32[]{:S(2)}) collective-permute-start(f32[9,20,128]{2,1,0:T(8,128)} %get-tuple-element.22), channel_id=1, source_target_pairs={{4,8},{12,16},{20,24},{28,32},{36,40},{44,48},{52,56},{60,64},{68,... | collective-permute-start | bytes 276488 | tf_op jit(solution)/shard_map/ppermute | solution.py:461
  11.4 8.8 %collective-permute-start.2 = (f32[9,20,128]{2,1,0:T(8,128)}, f32[9,20,128]{2,1,0:T(8,128)S(1)}, u32[]{:S(2)}, u32[]{:S(2)}) collective-permute-start(f32[9,20,128]{2,1,0:T(8,128)} %get-tuple-element.23), channel_id=1, source_target_pairs={{0,1},{2,3},{1,0},{3,2},{4,5},{6,7},{5,4},{7,6},{8,9},{10,11},{9,8... | collective-permute-start | bytes 276488 | tf_op jit(solution)/shard_map/ppermute | solution.py:461
  12.6 7.6 %collective-permute-start.3 = (f32[9,20,128]{2,1,0:T(8,128)}, f32[9,20,128]{2,1,0:T(8,128)S(1)}, u32[]{:S(2)}, u32[]{:S(2)}) collective-permute-start(f32[9,20,128]{2,1,0:T(8,128)} %get-tuple-element.24), channel_id=1, source_target_pairs={{1,2},{3,0},{2,1},{0,3},{5,6},{7,4},{6,5},{4,7},{9,10},{11,8},{10,... | collective-permute-start | bytes 276488 | tf_op jit(solution)/shard_map/ppermute | solution.py:461
  20.2 9.1 %copy-start.1 = (f32[9,20,128]{2,1,0:T(8,128)}, f32[9,20,128]{2,1,0:T(8,128)S(1)}, u32[]{:S(2)}) copy-start(f32[9,20,128]{2,1,0:T(8,128)S(1)} %collective-permute-done.rim0) | copy-start | bytes 276484
  20.2 9.0 %copy-start.2 = (f32[9,20,128]{2,1,0:T(8,128)}, f32[9,20,128]{2,1,0:T(8,128)S(1)}, u32[]{:S(2)}) copy-start(f32[9,20,128]{2,1,0:T(8,128)S(1)} %collective-permute-done.1.rim1) | copy-start | bytes 276484
  20.2 9.0 %copy-start.3 = (f32[9,20,128]{2,1,0:T(8,128)}, f32[9,20,128]{2,1,0:T(8,128)S(1)}, u32[]{:S(2)}) copy-start(f32[9,20,128]{2,1,0:T(8,128)S(1)} %collective-permute-done.2.rim2) | copy-start | bytes 276484
  20.2 9.0 %copy-start.4 = (f32[9,20,128]{2,1,0:T(8,128)}, f32[9,20,128]{2,1,0:T(8,128)S(1)}, u32[]{:S(2)}) copy-start(f32[9,20,128]{2,1,0:T(8,128)S(1)} %collective-permute-done.3.rim3) | copy-start | bytes 276484
  20.2 26.8 %all-to-all-start = ((f32[128,1,1664]{2,1,0:T(1,128)}), f32[128,1,1664]{2,1,0:T(1,128)S(1)}, u32[]{:S(2)}, u32[]{:S(2)}) async-start(f32[128,1,1664]{2,1,0:T(1,128)} %bitcast.9), calls=%async_computation | async-start | bytes 1703936 | tf_op jit(solution)/shard_map/all_to_all | solution.py:468
  47.0 0.9 %copy-start = (f32[128,1,1664]{2,1,0:T(1,128)}, f32[128,1,1664]{2,1,0:T(1,128)S(1)}, u32[]{:S(2)}) copy-start(f32[128,1,1664]{2,1,0:T(1,128)S(1)} %all-to-all-done) | copy-start | bytes 2555908

commit v4 on v3

--- a/solution.py
+++ b/solution.py
@@ -21,8 +21,10 @@
 NBP = 24
 LANES = 128
 CHUNKS = E_DEV // LANES
+PAIR = 2
+WIDE = PAIR * LANES
 ROWS = 224
-SC = 512
+SC = 2048
 TILES = 13
 F32 = jnp.float32
 BF = jnp.bfloat16
@@ -133,27 +135,35 @@
     for q in range(NQ):
         integ[q] = step * term[q]
 
+    def derive(cols, power):
+        acc = stress_of(lambda j: term[j, :, cols], star.at[:, :, :, cols], kd)
+        for q in range(6):
+            old = [term[NE + 6 * l + q, :, cols] for l in range(MECH)]
+            relax = couple[0, q : q + 1, cols] * old[0]
+            for l in range(1, MECH):
+                relax = relax + couple[l, q : q + 1, cols] * old[l]
+            new = acc[q] - relax
+            term[q, :, cols] = new
+            integ[q, :, cols] += power * new
+            for l in range(MECH):
+                new = omega[l : l + 1, cols] * (acc[q] - old[l])
+                term[NE + 6 * l + q, :, cols] = new
+                integ[NE + 6 * l + q, :, cols] += power * new
+        for q in range(6, NE):
+            term[q, :, cols] = acc[q]
+            integ[q, :, cols] += power * acc[q]
+
     def turn(order, power):
-        acc = stress_of(lambda j: term[j], star, kd)
-        for q in range(6):
-            old = [term[NE + 6 * l + q] for l in range(MECH)]
-            relax = couple[0, q : q + 1, :] * old[0]
-            for l in range(1, MECH):
-                relax = relax + couple[l, q : q + 1, :] * old[l]
-            term[q] = acc[q] - relax
-            for l in range(MECH):
-                term[NE + 6 * l + q] = omega[l : l + 1, :] * (acc[q] - old[l])
-        for q in range(6, NE):
-            term[q] = acc[q]
         power = power * step / (order + 2).astype(F32)
-        for q in range(NQ):
-            integ[q] += power * term[q]
+        for half in range(PAIR):
+            cols = slice(half * LANES, (half + 1) * LANES)
+            derive(cols, power[:, cols])
         return power
 
     lax.fori_loop(0, ORDER - 1, turn, step)
 
-    here = pl.ds(pl.multiple_of(c * LANES, LANES), LANES)
-    flat = pad_rows(integ[0:NE].reshape(NE * NBP, LANES), ROWS)
+    here = pl.ds(pl.multiple_of(c * WIDE, WIDE), WIDE)
+    flat = pad_rows(integ[0:NE].reshape(NE * NBP, WIDE), ROWS)
     hi, lo = split(flat)
     ihl[0:ROWS, here] = hi
     ihl[ROWS : 2 * ROWS, here] = lo
@@ -161,7 +171,7 @@
     fhl[0:80, here] = hi
     fhl[80:160, here] = lo
 
-    @pl.when(c == CHUNKS - 1)
+    @pl.when(c == CHUNKS // PAIR - 1)
     def _():
         rows = []
         for axis, k in (("strike", 0), ("depth", 2)):
@@ -177,6 +187,7 @@
 
 
 def fault_values(fhl, fpw, elem, face):
+    count = elem.shape[1]
     x = dot(fhl[...], one_hot(elem, E_DEV))
     right = []
     for r in range(3):
@@ -186,7 +197,7 @@
     points = dot(fpw[...], jnp.concatenate(right, axis=1))
     values = []
     for r in range(3):
-        cols = slice(r * SC, (r + 1) * SC)
+        cols = slice(r * count, (r + 1) * count)
         v = points[0:NP, cols]
         for g in range(1, 4):
             v = jnp.where(face == g, points[g * NP : (g + 1) * NP, cols], v)
@@ -202,15 +213,19 @@
     def place(tile, x):
         out[pl.ds(tile, SC // 16, stride=TILES), :] = to_blocks(x)
 
-    place(12, jnp.broadcast_to(live[...].astype(F32), (8, SC)))
-    plus = fault_values(fhl, fpw, fse[...], fsf[...])
-    minus = fault_values(fhl, fpw, fme[...], fmf[...])
-    sent = (
-        plus[1] + plus[2], plus[0], minus[1] - minus[2], minus[0], load[0], state[0],
-    )
-    for n, x in enumerate(sent):
+    def place_points(n, x):
         for g in range(2):
             place(2 * n + g, x[8 * g : 8 * g + 8])
+
+    place(12, jnp.broadcast_to(live[...].astype(F32), (8, SC)))
+    place_points(4, load[0])
+    place_points(5, state[0])
+    values = fault_values(
+        fhl, fpw, jnp.concatenate([fse[...], fme[...]], axis=1), jnp.concatenate([fsf[...], fmf[...]], axis=1)
+    )
+    plus, minus = [v[:, 0:SC] for v in values], [v[:, SC : 2 * SC] for v in values]
+    for n, x in enumerate((plus[1] + plus[2], plus[0], minus[1] - minus[2], minus[0])):
+        place_points(n, x)
     for n, x in enumerate((plus[1], minus[1])):
         for g in range(2):
             at = (2 * n + g) * LANES
@@ -344,7 +359,7 @@
         lfw[...] = left3(mat, [(0, f * NBP, lift[f]) for f in range(4)], 16, 96)
 
     def tile(ref, n):
-        return ref[pl.ds(n, SC // 16, stride=TILES), :]
+        return ref[pl.ds(s * (SC // 16 * TILES) + n, SC // 16, stride=TILES), :]
 
     def pair(ref, n):
         return jnp.concatenate([tile(ref, 2 * n), tile(ref, 2 * n + 1)], axis=1)
@@ -367,14 +382,13 @@
     far = to_slots(tile(theirs, 12))[0:1]
     left = []
     for side, (alive, face) in enumerate(((live[...].astype(F32), fmf[...]), (far, fsf[...]))):
-        mask = [jnp.where(face == f, alive, 0.0) for f in range(4)]
         sums = []
         for k in range(2):
             at = slice((2 * side + k) * SC, (2 * side + k + 1) * SC)
-            y = mask[0] * added[0:NBP, at]
+            y = added[0:NBP, at]
             for f in range(1, 4):
-                y = y + mask[f] * added[f * NBP : (f + 1) * NBP, at]
-            sums.append(y)
+                y = jnp.where(face == f, added[f * NBP : (f + 1) * NBP, at], y)
+            sums.append(y * alive)
         hi, lo = split(jnp.concatenate(sums, axis=0))
         left.append(jnp.concatenate([hi, lo], axis=0))
     spots = jnp.concatenate([one_hot(fme[...], E_DEV), one_hot(fse[...], E_DEV)], axis=1)
@@ -400,8 +414,12 @@
     return pl.BlockSpec(shape, lambda *i: (0,) * len(shape))
 
 
-def lanes(*lead):
-    return pl.BlockSpec(lead + (LANES,), lambda c: (0,) * len(lead) + (c,))
+def lanes(*lead, width=LANES):
+    return pl.BlockSpec(lead + (width,), lambda c: (0,) * len(lead) + (c,))
+
+
+def wide(*lead):
+    return lanes(*lead, width=WIDE)
 
 
 def per_device(
@@ -422,20 +440,20 @@
     params = pltpu.CompilerParams(vmem_limit_bytes=VMEM)
     integ, ihl, fhl, s0, s1, s2, s3 = pl.pallas_call(
         predict_kernel,
-        grid=(CHUNKS,),
+        grid=(CHUNKS // PAIR,),
         in_specs=[
-            lanes(NB, NQ), lanes(NE, NE, 3), lanes(MECH, 6), lanes(MECH), lanes(1),
+            wide(NB, NQ), wide(NE, NE, 3), wide(MECH, 6), wide(MECH), wide(1),
             whole((3, NB, NB)), whole((4, BND)),
         ],
         out_specs=[
-            lanes(NQ, NBP), whole((2 * ROWS, E_DEV)), whole((160, E_DEV)), rim, rim, rim, rim,
+            wide(NQ, NBP), whole((2 * ROWS, E_DEV)), whole((160, E_DEV)), rim, rim, rim, rim,
         ],
         out_shape=[
             shape((NQ, NBP, E_DEV), F32), shape((2 * ROWS, E_DEV), BF), shape((160, E_DEV), BF),
             *[pltpu.HBM((NE, NB, BND), F32)] * 4,
         ],
         scratch_shapes=[
-            pltpu.VMEM((NQ, NBP, LANES), F32), pltpu.VMEM((80, LANES), F32),
+            pltpu.VMEM((NQ, NBP, WIDE), F32), pltpu.VMEM((80, LANES), F32),
             pltpu.VMEM((32, 240), BF),
         ],
         compiler_params=params,
@@ -492,11 +510,12 @@
         ihl, r0, r1, r2, r3, kdiff, face_proj, face_lift,
     )
     anywhere = pl.BlockSpec(memory_space=pl.ANY)
+    resident = pl.BlockSpec(memory_space=pltpu.VMEM)
     result = pl.pallas_call(
         fault_kernel,
         grid=(SLOTS // SC,),
         in_specs=[
-            anywhere, lines, lines, kept,
+            anywhere, resident, resident, kept,
             slots, slots, slots, slots, slots, whole((4, NP, NB)),
         ],
         out_specs=anywhere,

time: 54.3 us -> 51.4 us (0.947)
  Pallas kernels: 28 us -> 25 us
    pallas_call x1, Pallas kernels: 5.69 us -> 3.6 us  [per_device(): pl.pallas_call(slot_kernel, grid=(SLOTS // SC,), in_specs=[whole((160, E_...]
    pallas_call x2, Pallas kernels: 14.1 us -> 13.1 us  [the longest x1 8.12 us: per_device(): pl.pallas_call(predict_kernel, grid=(CHUNKS // PAIR,), in_specs=[wide(NB,...]
  transfers between devices with their start and end apart: 5 -> 5, of which waited for: 1 -> 1; matrix products, arithmetic and copies ran while one was open for 0% -> 0% of each run, Pallas kernels for 26% -> 23%
where the time goes in v4:
time: 51.4 us; the launch traced here: 51.1 us
  Pallas kernels  25 us (49%)
  starting transfers between devices  15.6 us (30%)
  waiting for transfers between devices  9.47 us (18%)
  local copies, waits for them, and re-layouts  0.94 us (2%)
    all_to_all x1, waiting for transfers between devices, per_device(): lax.all_to_all(sent.reshape(DEVICES, 1, TILES * LANES), ('strike', 'depth...  9.46 us
    all_to_all x1, starting transfers between devices, per_device(): lax.all_to_all(sent.reshape(DEVICES, 1, TILES * LANES), ('strike', 'depth...  9.39 us
    pallas_call x1, Pallas kernels, per_device(): pl.pallas_call(element_kernel, grid=(CHUNKS,), in_specs=[lanes(NQ, NBP),...  8.26 us
    pallas_call x1, Pallas kernels, per_device(): pl.pallas_call(predict_kernel, grid=(CHUNKS // PAIR,), in_specs=[wide(NB,...  8.12 us
    ppermute x4, starting transfers between devices, swap(): return lax.ppermute(x, axis, ends + [(j, i) for i, j in ends])  6.23 us
    pallas_call x1, Pallas kernels, per_device(): pl.pallas_call(fault_kernel, grid=(SLOTS // SC,), in_specs=[anywhere, res...  4.99 us
    pallas_call x1, Pallas kernels, per_device(): pl.pallas_call(slot_kernel, grid=(SLOTS // SC,), in_specs=[whole((160, E_...  3.6 us
  transfers between devices with their start and end apart: 5, of which 1 were waited for; matrix products, arithmetic and copies ran while one was open for 0% of the time, Pallas kernels for 23%

profile of v4, /device:TPU:1, one launch (start us, length us, event | category | flops | bytes accessed | tf_op | source)
XLA Modules:
  0.0 51.1 jit_solution(2423861612976330295)
XLA Ops:
  0.0 8.1 %predict.1 = (f32[27,24,512]{2,1,0:T(8,128)}, bf16[448,512]{1,0:T(8,128)(2,1)}, bf16[160,512]{1,0:T(8,128)(2,1)}, f32[9,20,128]{2,1,0:T(8,128)}, f32[9,20,128]{2...) custom-call(f32[20,27,512]{2,1,0:T(8,128)} %bitcast.7, f32[9,9,3,512]{3,2,1,0:T(4,128)} %bitcast.11, ...), custom_call_target="tpu_custom_call" | custom-call | tf_op jit(solution)/shard_map/predict/pallas_call | solution.py:441
  8.1 1.5 %collective-permute-start = (f32[9,20,128]{2,1,0:T(8,128)}, f32[9,20,128]{2,1,0:T(8,128)S(1)}, u32[]{:S(2)}, u32[]{:S(2)}) collective-permute-start(f32[9,20,128]{2,1,0:T(8,128)} %get-tuple-element.21), channel_id=1, source_target_pairs={{0,4},{8,12},{16,20},{24,28},{32,36},{40,44},{48,52},{56,60},{64,6... | collective-permute-start | bytes 276488 | tf_op jit(solution)/shard_map/ppermute | solution.py:479
  9.6 1.7 %collective-permute-start.1 = (f32[9,20,128]{2,1,0:T(8,128)}, f32[9,20,128]{2,1,0:T(8,128)S(1)}, u32[]{:S(2)}, u32[]{:S(2)}) collective-permute-start(f32[9,20,128]{2,1,0:T(8,128)} %get-tuple-element.22), channel_id=1, source_target_pairs={{4,8},{12,16},{20,24},{28,32},{36,40},{44,48},{52,56},{60,64},{68,... | collective-permute-start | bytes 276488 | tf_op jit(solution)/shard_map/ppermute | solution.py:479
  11.3 1.2 %collective-permute-start.2 = (f32[9,20,128]{2,1,0:T(8,128)}, f32[9,20,128]{2,1,0:T(8,128)S(1)}, u32[]{:S(2)}, u32[]{:S(2)}) collective-permute-start(f32[9,20,128]{2,1,0:T(8,128)} %get-tuple-element.23), channel_id=1, source_target_pairs={{0,1},{2,3},{1,0},{3,2},{4,5},{6,7},{5,4},{7,6},{8,9},{10,11},{9,8... | collective-permute-start | bytes 276488 | tf_op jit(solution)/shard_map/ppermute | solution.py:479
  12.5 1.8 %collective-permute-start.3 = (f32[9,20,128]{2,1,0:T(8,128)}, f32[9,20,128]{2,1,0:T(8,128)S(1)}, u32[]{:S(2)}, u32[]{:S(2)}) collective-permute-start(f32[9,20,128]{2,1,0:T(8,128)} %get-tuple-element.24), channel_id=1, source_target_pairs={{1,2},{3,0},{2,1},{0,3},{5,6},{7,4},{6,5},{4,7},{9,10},{11,8},{10,... | collective-permute-start | bytes 276488 | tf_op jit(solution)/shard_map/ppermute | solution.py:479
  14.3 3.6 %slots.1 = (f32[1664,128]{1,0:T(8,128)}, f32[128,512]{1,0:T(8,128)}) custom-call(bf16[160,512]{1,0:T(8,128)(2,1)} %get-tuple-element.25.fhl, f32[4,16,20]{2,1,0:T(8,128)} %bitcast.13, s32[1,2048]{1,0:T(1,128)} %fse.3, s32[1,2048]{1,0:T(1,128)} %fsf.3, s32[1,2048]{1,0:T(1,128)} %fme.3, s32[1,2048]{1,0:T(1,128)} %fmf.3, s32[1,2048]{1,0:T(1,128)} %live.3, ...), custom_call_target="tpu_custom_call" | custom-call | tf_op jit(solution)/shard_map/slots/pallas_call | solution.py:462
  18.0 0.0 collective-permute-done.rim0
  18.0 0.0 copy-start.1
  18.0 0.0 collective-permute-done.1.rim1
  18.0 0.0 copy-start.2
  18.0 0.0 collective-permute-done.2.rim2
  18.0 0.0 copy-start.3
  18.0 0.0 collective-permute-done.3.rim3
  18.0 0.0 copy-start.4
  18.0 9.4 %all-to-all-start = ((f32[128,1,1664]{2,1,0:T(1,128)}), f32[128,1,1664]{2,1,0:T(1,128)S(1)}, u32[]{:S(2)}, u32[]{:S(2)}) async-start(f32[128,1,1664]{2,1,0:T(1,128)} %bitcast.9), calls=%async_computation | async-start | bytes 1703936 | tf_op jit(solution)/shard_map/all_to_all | solution.py:486
  27.4 0.0 copy-done.1
  27.4 0.0 copy-done.2
  27.4 0.0 copy-done.3
  27.5 0.0 copy-done.4
  27.5 8.3 %elements.1.base_in = f32[20,27,512]{2,1,0:T(8,128)} custom-call(f32[27,24,512]{2,1,0:T(8,128)} %get-tuple-element.19.integ, f32[20,27,512]{2,1,0:T(8,128)} %bitcast.8, f32[9,9,3,512]{3,2,1,0:T(4,128)} %bitcast.12, f32[3,6,512]{2,1,0:T(8,128)} %couple.3, f32[3,512]{1,0:T(4,128)} %omega.3, f32[9,9,512]{2,1,0:T(8,128)} %fminus.1, f32[9,9,512]{2,1,0:T(8,128)} %fplus.1, ...), custom_call_target="tpu_custom_call" | custom-call | tf_op jit(solution)/shard_map/elements/pallas_call | solution.py:489
  35.7 9.5 %all-to-all-done = f32[128,1,1664]{2,1,0:T(1,128)S(1)} async-done(((f32[128,1,1664]{2,1,0:T(1,128)}), f32[128,1,1664]{2,1,0:T(1,128)S(1)}, u32[]{:S(2)}, u32[]{:S(2)}) %all-to-all-start) | async-done | bytes 852000 | tf_op jit(solution)/shard_map/all_to_all | solution.py:486
  45.2 0.0 copy-start
  45.2 0.9 %copy-done = f32[128,1,1664]{2,1,0:T(1,128)} copy-done((f32[128,1,1664]{2,1,0:T(1,128)}, f32[128,1,1664]{2,1,0:T(1,128)S(1)}, u32[]{:S(2)}) %copy-start) | copy-done | bytes 851992
  46.1 5.0 %fault.1 = f32[20,27,512]{2,1,0:T(8,128)} custom-call(f32[20,27,512]{2,1,0:T(8,128)} %elements.1.base_in, f32[1664,128]{1,0:T(8,128)} %get-tuple-element.31.mine, f32[1664,128]{1,0:T(8,128)} %bitcast.10, f32[128,512]{1,0:T(8,128)} %get-tuple-element.32.keep, s32[1,2048]{1,0:T(1,128)} %fse.3, s32[1,2048]{1,0:T(1,128)} %fsf.3, ...), custom_call_target="tpu_custom_call", output_to_operand_aliasing={{}: (0, {})} | custom-call | tf_op jit(solution)/shard_map/fault/pallas_call | solution.py:514
Async XLA Ops:
  8.1 9.8 %collective-permute-start = (f32[9,20,128]{2,1,0:T(8,128)}, f32[9,20,128]{2,1,0:T(8,128)S(1)}, u32[]{:S(2)}, u32[]{:S(2)}) collective-permute-start(f32[9,20,128]{2,1,0:T(8,128)} %get-tuple-element.21), channel_id=1, source_target_pairs={{0,4},{8,12},{16,20},{24,28},{32,36},{40,44},{48,52},{56,60},{64,6... | collective-permute-start | bytes 276488 | tf_op jit(solution)/shard_map/ppermute | solution.py:479
  9.6 8.3 %collective-permute-start.1 = (f32[9,20,128]{2,1,0:T(8,128)}, f32[9,20,128]{2,1,0:T(8,128)S(1)}, u32[]{:S(2)}, u32[]{:S(2)}) collective-permute-start(f32[9,20,128]{2,1,0:T(8,128)} %get-tuple-element.22), channel_id=1, source_target_pairs={{4,8},{12,16},{20,24},{28,32},{36,40},{44,48},{52,56},{60,64},{68,... | collective-permute-start | bytes 276488 | tf_op jit(solution)/shard_map/ppermute | solution.py:479
  11.3 6.7 %collective-permute-start.2 = (f32[9,20,128]{2,1,0:T(8,128)}, f32[9,20,128]{2,1,0:T(8,128)S(1)}, u32[]{:S(2)}, u32[]{:S(2)}) collective-permute-start(f32[9,20,128]{2,1,0:T(8,128)} %get-tuple-element.23), channel_id=1, source_target_pairs={{0,1},{2,3},{1,0},{3,2},{4,5},{6,7},{5,4},{7,6},{8,9},{10,11},{9,8... | collective-permute-start | bytes 276488 | tf_op jit(solution)/shard_map/ppermute | solution.py:479
  12.5 5.5 %collective-permute-start.3 = (f32[9,20,128]{2,1,0:T(8,128)}, f32[9,20,128]{2,1,0:T(8,128)S(1)}, u32[]{:S(2)}, u32[]{:S(2)}) collective-permute-start(f32[9,20,128]{2,1,0:T(8,128)} %get-tuple-element.24), channel_id=1, source_target_pairs={{1,2},{3,0},{2,1},{0,3},{5,6},{7,4},{6,5},{4,7},{9,10},{11,8},{10,... | collective-permute-start | bytes 276488 | tf_op jit(solution)/shard_map/ppermute | solution.py:479
  18.0 9.5 %copy-start.1 = (f32[9,20,128]{2,1,0:T(8,128)}, f32[9,20,128]{2,1,0:T(8,128)S(1)}, u32[]{:S(2)}) copy-start(f32[9,20,128]{2,1,0:T(8,128)S(1)} %collective-permute-done.rim0) | copy-start | bytes 276484
  18.0 9.5 %copy-start.2 = (f32[9,20,128]{2,1,0:T(8,128)}, f32[9,20,128]{2,1,0:T(8,128)S(1)}, u32[]{:S(2)}) copy-start(f32[9,20,128]{2,1,0:T(8,128)S(1)} %collective-permute-done.1.rim1) | copy-start | bytes 276484
  18.0 9.5 %copy-start.3 = (f32[9,20,128]{2,1,0:T(8,128)}, f32[9,20,128]{2,1,0:T(8,128)S(1)}, u32[]{:S(2)}) copy-start(f32[9,20,128]{2,1,0:T(8,128)S(1)} %collective-permute-done.2.rim2) | copy-start | bytes 276484
  18.0 9.4 %copy-start.4 = (f32[9,20,128]{2,1,0:T(8,128)}, f32[9,20,128]{2,1,0:T(8,128)S(1)}, u32[]{:S(2)}) copy-start(f32[9,20,128]{2,1,0:T(8,128)S(1)} %collective-permute-done.3.rim3) | copy-start | bytes 276484
  18.0 27.2 %all-to-all-start = ((f32[128,1,1664]{2,1,0:T(1,128)}), f32[128,1,1664]{2,1,0:T(1,128)S(1)}, u32[]{:S(2)}, u32[]{:S(2)}) async-start(f32[128,1,1664]{2,1,0:T(1,128)} %bitcast.9), calls=%async_computation | async-start | bytes 1703936 | tf_op jit(solution)/shard_map/all_to_all | solution.py:486
  45.2 0.9 %copy-start = (f32[128,1,1664]{2,1,0:T(1,128)}, f32[128,1,1664]{2,1,0:T(1,128)S(1)}, u32[]{:S(2)}) copy-start(f32[128,1,1664]{2,1,0:T(1,128)S(1)} %all-to-all-done) | copy-start | bytes 2555908

commit v5 on v4

--- a/solution.py
+++ b/solution.py
@@ -24,11 +24,11 @@
 PAIR = 2
 WIDE = PAIR * LANES
 ROWS = 224
-SC = 2048
 TILES = 13
 F32 = jnp.float32
 BF = jnp.bfloat16
 VMEM = 56 * 1024 * 1024
+VMEM_SMALL = 40 * 1024 * 1024
 FAULT_ROWS = (0, 3, 6)
 
 
@@ -94,13 +94,13 @@
 
 def to_blocks(x):
     return swap_blocks(
-        jnp.concatenate([x[:, t * LANES : (t + 1) * LANES] for t in range(SC // LANES)], axis=0)
+        jnp.concatenate([x[:, t * LANES : (t + 1) * LANES] for t in range(SLOTS // LANES)], axis=0)
     )
 
 
 def to_slots(x):
     x = swap_blocks(x)
-    return jnp.concatenate([x[8 * t : 8 * t + 8] for t in range(SC // LANES)], axis=1)
+    return jnp.concatenate([x[8 * t : 8 * t + 8] for t in range(SLOTS // LANES)], axis=1)
 
 
 def stress_of(get, star_ref, kd, rows=range(NE)):
@@ -206,24 +206,22 @@
 
 
 def slot_kernel(fhl, proj, fse, fsf, fme, fmf, live, load, state, out, keep, mat, fpw):
-    @pl.when(pl.program_id(0) == 0)
-    def _():
-        fpw[...] = left3(mat, [(0, g * NP, proj[g].T) for g in range(4)], 32, 64)
+    fpw[...] = left3(mat, [(0, g * NP, proj[g].T) for g in range(4)], 32, 64)
 
     def place(tile, x):
-        out[pl.ds(tile, SC // 16, stride=TILES), :] = to_blocks(x)
+        out[pl.ds(tile, DEVICES, stride=TILES), :] = to_blocks(x)
 
     def place_points(n, x):
         for g in range(2):
             place(2 * n + g, x[8 * g : 8 * g + 8])
 
-    place(12, jnp.broadcast_to(live[...].astype(F32), (8, SC)))
+    place(12, jnp.broadcast_to(live[...].astype(F32), (8, SLOTS)))
     place_points(4, load[0])
     place_points(5, state[0])
     values = fault_values(
         fhl, fpw, jnp.concatenate([fse[...], fme[...]], axis=1), jnp.concatenate([fsf[...], fmf[...]], axis=1)
     )
-    plus, minus = [v[:, 0:SC] for v in values], [v[:, SC : 2 * SC] for v in values]
+    plus, minus = [v[:, 0:SLOTS] for v in values], [v[:, SLOTS : 2 * SLOTS] for v in values]
     for n, x in enumerate((plus[1] + plus[2], plus[0], minus[1] - minus[2], minus[0])):
         place_points(n, x)
     for n, x in enumerate((plus[1], minus[1])):
@@ -327,87 +325,79 @@
     base[...] = dofs[...] + jnp.transpose(change[:, 0:NB, :], (1, 0, 2))
 
 
+def inverse_of(x):
+    guess = pl.reciprocal(x, approx=True)
+    return guess * (2.0 - x * guess)
+
+
 def friction(trial, pressure, load, state):
     sigma = load * (1.0 + 0.5 * jnp.tanh(0.5 * pressure))
     half = AFRIC * sigma
     steep = half * state
     size = jnp.abs(trial)
-    slip = size / (ETA + steep)
+    slip = size * inverse_of(ETA + steep)
     for turn in range(NEWTON - 1):
         scaled = state * slip
         square = 1.0 + scaled * scaled
         inverse = lax.rsqrt(square)
         resid = size - ETA * slip - half * jnp.log(scaled + square * inverse)
-        slope = ETA + steep * inverse
-        guess = pl.reciprocal(slope, approx=True)
-        slip = slip + resid * (guess * (2.0 - slope * guess))
+        slip = slip + resid * inverse_of(ETA + steep * inverse)
     slip = jnp.where(trial < 0.0, -slip, slip)
     return trial - ETA * slip, slip
 
 
 def fault_kernel(
     base_in, mine, theirs, keep, fse, fsf, fme, fmf, live, lift,
-    base, mat, lfw, acc, slab, sem,
+    base, mat, lfw, slab, sem,
 ):
     del base_in
-    s = pl.program_id(0)
     window = base.at[:, 0:8, :]
-
-    @pl.when(s == 0)
-    def _():
-        pltpu.make_async_copy(window, slab, sem).start()
-        lfw[...] = left3(mat, [(0, f * NBP, lift[f]) for f in range(4)], 16, 96)
+    read_slab = pltpu.make_async_copy(window, slab, sem)
+    read_slab.start()
+    lfw[...] = left3(mat, [(0, f * NBP, lift[f]) for f in range(4)], 16, 96)
 
     def tile(ref, n):
-        return ref[pl.ds(s * (SC // 16 * TILES) + n, SC // 16, stride=TILES), :]
+        return ref[pl.ds(n, DEVICES, stride=TILES), :]
 
     def pair(ref, n):
         return jnp.concatenate([tile(ref, 2 * n), tile(ref, 2 * n + 1)], axis=1)
 
-    pull, slip = friction(
-        0.5 * (pair(theirs, 0) + pair(mine, 2)), pair(mine, 3) + pair(theirs, 1),
-        pair(mine, 4), pair(mine, 5),
-    )
-    terms = [pull - keep[:, 256:512], -0.5 * slip]
-    pull, slip = friction(
-        0.5 * (pair(mine, 0) + pair(theirs, 2)), pair(theirs, 3) + pair(mine, 1),
-        pair(theirs, 4), pair(theirs, 5),
-    )
-    terms += [pull - keep[:, 0:256], 0.5 * slip]
-    right = []
-    for t in terms:
-        x = jnp.concatenate([to_slots(t[:, 0:LANES]), to_slots(t[:, LANES:256])], axis=0)
-        right.append(stack3(x))
-    added = dot(lfw[...], jnp.concatenate(right, axis=1))
-    far = to_slots(tile(theirs, 12))[0:1]
-    left = []
-    for side, (alive, face) in enumerate(((live[...].astype(F32), fmf[...]), (far, fsf[...]))):
+    def side(one, other, load, state, kept, sign, alive, face, elem):
+        pull, slip = friction(0.5 * (pair(theirs, other[0]) + pair(mine, one[0])), pair(mine, one[1]) + pair(theirs, other[1]), load, state)
+        right = []
+        for t in (pull - kept, sign * slip):
+            x = jnp.concatenate([to_slots(t[:, 0:LANES]), to_slots(t[:, LANES:256])], axis=0)
+            right.append(stack3(x))
+        added = dot(lfw[...], jnp.concatenate(right, axis=1))
         sums = []
         for k in range(2):
-            at = slice((2 * side + k) * SC, (2 * side + k + 1) * SC)
+            at = slice(k * SLOTS, (k + 1) * SLOTS)
             y = added[0:NBP, at]
             for f in range(1, 4):
                 y = jnp.where(face == f, added[f * NBP : (f + 1) * NBP, at], y)
             sums.append(y * alive)
         hi, lo = split(jnp.concatenate(sums, axis=0))
-        left.append(jnp.concatenate([hi, lo], axis=0))
-    spots = jnp.concatenate([one_hot(fme[...], E_DEV), one_hot(fse[...], E_DEV)], axis=1)
-    acc[s] = dot_nt(jnp.concatenate(left, axis=1), spots)
-
-    @pl.when(s == SLOTS // SC - 1)
-    def _():
-        total = acc[0]
-        for part in range(1, SLOTS // SC):
-            total = total + acc[part]
-        acc[0, 0:48, :] = total[0:48] + total[48:96]
-        pltpu.make_async_copy(window, slab, sem).wait()
-        for b in range(NB):
-            for k in range(2):
-                row = slice(FAULT_ROWS[1 + k], FAULT_ROWS[1 + k] + 1)
-                slab[b, row, :] = slab[b, row, :] + acc[0, k * NBP + b : k * NBP + b + 1, :]
-        copy = pltpu.make_async_copy(slab, window, sem)
-        copy.start()
-        copy.wait()
+        return dot_nt(jnp.concatenate([hi, lo], axis=0), one_hot(elem, E_DEV))
+
+    minus = side(
+        (2, 3), (0, 1), pair(mine, 4), pair(mine, 5), keep[:, 256:512], -0.5,
+        live[...].astype(F32), fmf[...], fme[...],
+    )
+    far = to_slots(tile(theirs, 12))[0:1]
+    plus = side(
+        (0, 1), (2, 3), pair(theirs, 4), pair(theirs, 5), keep[:, 0:256], 0.5,
+        far, fsf[...], fse[...],
+    )
+    both = minus + plus
+    delta = both[0:48] + both[48:96]
+    read_slab.wait()
+    for b in range(NB):
+        for k in range(2):
+            row = slice(FAULT_ROWS[1 + k], FAULT_ROWS[1 + k] + 1)
+            slab[b, row, :] = slab[b, row, :] + delta[k * NBP + b : k * NBP + b + 1, :]
+    write = pltpu.make_async_copy(slab, window, sem)
+    write.start()
+    write.wait()
 
 
 def whole(shape):
@@ -433,11 +423,9 @@
     star = jnp.transpose(star, (1, 2, 0, 3))
     face_proj = jnp.transpose(face_proj, (0, 2, 1))
     rim = whole((NE, NB, BND))
-    lines = pl.BlockSpec((SC // 16 * TILES, LANES), lambda c: (c, 0))
-    kept = pl.BlockSpec((SC // 16, 4 * LANES), lambda c: (c, 0))
-    slots = pl.BlockSpec((1, SC), lambda c: (0, c))
-    points = pl.BlockSpec((1, NP, SC), lambda c: (0, 0, c))
+    resident = pl.BlockSpec(memory_space=pltpu.VMEM)
     params = pltpu.CompilerParams(vmem_limit_bytes=VMEM)
+    small = pltpu.CompilerParams(vmem_limit_bytes=VMEM_SMALL)
     integ, ihl, fhl, s0, s1, s2, s3 = pl.pallas_call(
         predict_kernel,
         grid=(CHUNKS // PAIR,),
@@ -461,12 +449,11 @@
     )(dofs, star, couple, omega, wc, kdiff, send_rows)
     out, keep = pl.pallas_call(
         slot_kernel,
-        grid=(SLOTS // SC,),
-        in_specs=[whole((160, E_DEV)), whole((4, NP, NB)), *[slots] * 5, points, points],
-        out_specs=[lines, kept],
+        in_specs=[resident] * 9,
+        out_specs=[resident] * 2,
         out_shape=[shape((DEVICES * TILES, LANES), F32), shape((DEVICES, 4 * LANES), F32)],
         scratch_shapes=[pltpu.VMEM((64, LANES), F32), pltpu.VMEM((64, 96), BF)],
-        compiler_params=params,
+        compiler_params=small,
         name="slots",
     )(
         fhl, face_proj, fault_send_elem, fault_send_face, fault_minus_elem, fault_minus_face,
@@ -503,33 +490,28 @@
             pltpu.VMEM((96, 96), BF), pltpu.VMEM((2 * ROWS, 4 * BND), BF),
             pltpu.VMEM((NQ, NBP, LANES), F32),
         ],
-        compiler_params=params,
+        compiler_params=small,
         name="elements",
     )(
         integ, dofs, star, couple, omega, flux_minus, flux_plus, area, nbr_elem, nbr_face,
         ihl, r0, r1, r2, r3, kdiff, face_proj, face_lift,
     )
     anywhere = pl.BlockSpec(memory_space=pl.ANY)
-    resident = pl.BlockSpec(memory_space=pltpu.VMEM)
     result = pl.pallas_call(
         fault_kernel,
-        grid=(SLOTS // SC,),
-        in_specs=[
-            anywhere, resident, resident, kept,
-            slots, slots, slots, slots, slots, whole((4, NP, NB)),
-        ],
+        in_specs=[anywhere] + [resident] * 9,
         out_specs=anywhere,
         out_shape=shape((NB, NQ, E_DEV), F32),
         input_output_aliases={0: 0},
         scratch_shapes=[
-            pltpu.VMEM((64, LANES), F32), pltpu.VMEM((96, 48), BF), pltpu.VMEM((SLOTS // SC, 96, E_DEV), F32),
+            pltpu.VMEM((64, LANES), F32), pltpu.VMEM((96, 48), BF),
             pltpu.VMEM((NB, 8, E_DEV), F32), pltpu.SemaphoreType.DMA,
         ],
-        compiler_params=params,
+        compiler_params=small,
         name="fault",
     )(
-        base, sent, theirs, keep, fault_send_elem, fault_send_face, fault_minus_elem,
-        fault_minus_face, fault_live, face_lift,
+        base, sent, theirs, keep, fault_send_elem, fault_send_face, fault_minus_elem, fault_minus_face,
+        fault_live, face_lift,
     )
     return jnp.transpose(result, (1, 0, 2))
 

time: 51.4 us -> 58.1 us (1.13); the launches traced: 51.1 us -> 57.2 us
  local copies, waits for them, and re-layouts: 0.94 us -> 16.8 us
  waiting for transfers between devices: 9.47 us -> 1.83 us
  Pallas kernels: 25 us -> 23.1 us
    unnamed x10 -> x74, local copies, waits for them, and re-layouts: 0.94 us -> 16.8 us
    all_to_all x1, waiting for transfers between devices: 9.46 us -> 1.82 us  [per_device(): lax.all_to_all(sent.reshape(DEVICES, 1, TILES * LANES), ('strike', 'depth...]
    pallas_call x1, Pallas kernels: 8.26 us -> 7.1 us  [per_device(): pl.pallas_call(element_kernel, grid=(CHUNKS,), in_specs=[lanes(NQ, NBP),...]
    pallas_call x2, Pallas kernels: 8.59 us -> 7.81 us  [the longest x1 5.44 us: per_device(): pl.pallas_call(fault_kernel, in_specs=[anywhere] + [resident] * 9, out_sp...]
  transfers between devices with their start and end apart: 5 -> 5, of which waited for: 1 -> 1; matrix products, arithmetic and copies ran while one was open for 0% -> 0% of each run, Pallas kernels for 23% -> 17%
where the time goes in v5:
time: 58.1 us; the launch traced here: 57.2 us
  Pallas kernels  23.1 us (40%)
  local copies, waits for them, and re-layouts  16.8 us (29%)
  starting transfers between devices  15.2 us (26%)
  waiting for transfers between devices  1.83 us (3%)
    unnamed x74, local copies, waits for them, and re-layouts  16.8 us
    all_to_all x1, starting transfers between devices, per_device(): lax.all_to_all(sent.reshape(DEVICES, 1, TILES * LANES), ('strike', 'depth...  8.97 us
    pallas_call x1, Pallas kernels, per_device(): pl.pallas_call(predict_kernel, grid=(CHUNKS // PAIR,), in_specs=[wide(NB,...  8.23 us
    pallas_call x1, Pallas kernels, per_device(): pl.pallas_call(element_kernel, grid=(CHUNKS,), in_specs=[lanes(NQ, NBP),...  7.1 us
    ppermute x4, starting transfers between devices, swap(): return lax.ppermute(x, axis, ends + [(j, i) for i, j in ends])  6.22 us
    pallas_call x1, Pallas kernels, per_device(): pl.pallas_call(fault_kernel, in_specs=[anywhere] + [resident] * 9, out_sp...  5.44 us
    pallas_call x1, Pallas kernels, per_device(): pl.pallas_call(slot_kernel, in_specs=[resident] * 9, out_specs=[resident]...  2.37 us
    all_to_all x1, waiting for transfers between devices, per_device(): lax.all_to_all(sent.reshape(DEVICES, 1, TILES * LANES), ('strike', 'depth...  1.82 us
  transfers between devices with their start and end apart: 5, of which 1 were waited for; matrix products, arithmetic and copies ran while one was open for 0% of the time, Pallas kernels for 17%

profile of v5, /device:TPU:1, one launch (start us, length us, event | category | flops | bytes accessed | tf_op | source)
XLA Modules:
  0.0 57.2 jit_solution(10672185172615950582)
XLA Ops:
  0.0 0.0 copy-start.26
  0.0 0.0 copy-start.25
  0.0 0.0 copy-start.15
  0.0 0.0 copy-start.14
  0.1 0.0 copy-start.12
  0.1 0.0 copy-start.4
  0.1 0.0 copy-start.5
  0.1 0.0 copy-start.10
  0.1 8.2 %predict.1 = (f32[27,24,512]{2,1,0:T(8,128)}, bf16[448,512]{1,0:T(8,128)(2,1)}, bf16[160,512]{1,0:T(8,128)(2,1)}, f32[9,20,128]{2,1,0:T(8,128)}, f32[9,20,128]{2...) custom-call(f32[20,27,512]{2,1,0:T(8,128)} %bitcast.7, f32[9,9,3,512]{3,2,1,0:T(4,128)} %bitcast.10, ...), custom_call_target="tpu_custom_call" | custom-call | tf_op jit(solution)/shard_map/predict/pallas_call | solution.py:429
  8.4 0.0 copy-start
  8.4 0.0 copy-start.1
  8.4 0.0 copy-start.8
  8.4 1.5 %collective-permute-start = (f32[9,20,128]{2,1,0:T(8,128)}, f32[9,20,128]{2,1,0:T(8,128)S(1)}, u32[]{:S(2)}, u32[]{:S(2)}) collective-permute-start(f32[9,20,128]{2,1,0:T(8,128)} %get-tuple-element.21), channel_id=1, source_target_pairs={{0,4},{8,12},{16,20},{24,28},{32,36},{40,44},{48,52},{56,60},{64,6... | collective-permute-start | bytes 276488 | tf_op jit(solution)/shard_map/ppermute | solution.py:466
  9.9 1.7 %collective-permute-start.1 = (f32[9,20,128]{2,1,0:T(8,128)}, f32[9,20,128]{2,1,0:T(8,128)S(1)}, u32[]{:S(2)}, u32[]{:S(2)}) collective-permute-start(f32[9,20,128]{2,1,0:T(8,128)} %get-tuple-element.22), channel_id=1, source_target_pairs={{4,8},{12,16},{20,24},{28,32},{36,40},{44,48},{52,56},{60,64},{68,... | collective-permute-start | bytes 276488 | tf_op jit(solution)/shard_map/ppermute | solution.py:466
  11.6 1.2 %collective-permute-start.2 = (f32[9,20,128]{2,1,0:T(8,128)}, f32[9,20,128]{2,1,0:T(8,128)S(1)}, u32[]{:S(2)}, u32[]{:S(2)}) collective-permute-start(f32[9,20,128]{2,1,0:T(8,128)} %get-tuple-element.23), channel_id=1, source_target_pairs={{0,1},{2,3},{1,0},{3,2},{4,5},{6,7},{5,4},{7,6},{8,9},{10,11},{9,8... | collective-permute-start | bytes 276488 | tf_op jit(solution)/shard_map/ppermute | solution.py:466
  12.8 1.8 %collective-permute-start.3 = (f32[9,20,128]{2,1,0:T(8,128)}, f32[9,20,128]{2,1,0:T(8,128)S(1)}, u32[]{:S(2)}, u32[]{:S(2)}) collective-permute-start(f32[9,20,128]{2,1,0:T(8,128)} %get-tuple-element.24), channel_id=1, source_target_pairs={{1,2},{3,0},{2,1},{0,3},{5,6},{7,4},{6,5},{4,7},{9,10},{11,8},{10,... | collective-permute-start | bytes 276488 | tf_op jit(solution)/shard_map/ppermute | solution.py:466
  14.6 0.0 copy-done.32
  14.6 0.0 copy-done.28
  14.7 0.9 %copy-done.9 = bf16[160,512]{1,0:T(8,128)(2,1)S(1)} copy-done((bf16[160,512]{1,0:T(8,128)(2,1)S(1)}, bf16[160,512]{1,0:T(8,128)(2,1)}, u32[]{:S(2)}) %copy-start.9) | copy-done | bytes 163864
  15.6 2.4 %slots.1 = (f32[1664,128]{1,0:T(8,128)}, f32[128,512]{1,0:T(8,128)S(1)}) custom-call(bf16[160,512]{1,0:T(8,128)(2,1)S(1)} %copy-done.9, f32[4,16,20]{2,1,0:T(8,128)S(1)} %bitcast.12, s32[1,2048]{1,0:T(1,128)S(1)} %copy-done.25, s32[1,2048]{1,0:T(1,128)S(1)} %copy-done.26, s32[1,2048]{1,0:T(1,128)S(1)} %copy-done.28, s32[1,2048]{1,0:T(1,128)S(1)} %copy-done.30, ...), custom_call_target="tpu_custom_call" | custom-call | tf_op jit(solution)/shard_map/slots/pallas_call | solution.py:450
  17.9 0.7 %copy-done.6 = f32[128,512]{1,0:T(8,128)} copy-done((f32[128,512]{1,0:T(8,128)}, f32[128,512]{1,0:T(8,128)S(1)}, u32[]{:S(2)}) %copy-start.6) | copy-done | bytes 262168
  18.7 0.0 collective-permute-done.rim0
  18.7 0.6 %copy-done.16 = f32[9,20,128]{2,1,0:T(8,128)} copy-done((f32[9,20,128]{2,1,0:T(8,128)}, f32[9,20,128]{2,1,0:T(8,128)S(1)}, u32[]{:S(2)}) %copy-start.16) | copy-done | bytes 92184
  19.3 0.0 collective-permute-done.1.rim1
  19.3 0.7 %copy-done.18 = f32[9,20,128]{2,1,0:T(8,128)} copy-done((f32[9,20,128]{2,1,0:T(8,128)}, f32[9,20,128]{2,1,0:T(8,128)S(1)}, u32[]{:S(2)}) %copy-start.18) | copy-done | bytes 92184
  20.0 0.0 collective-permute-done.2.rim2
  20.0 0.6 %copy-done.20 = f32[9,20,128]{2,1,0:T(8,128)} copy-done((f32[9,20,128]{2,1,0:T(8,128)}, f32[9,20,128]{2,1,0:T(8,128)S(1)}, u32[]{:S(2)}) %copy-start.20) | copy-done | bytes 92184
  20.6 0.0 collective-permute-done.3.rim3
  20.6 0.6 %copy-done.22 = f32[9,20,128]{2,1,0:T(8,128)} copy-done((f32[9,20,128]{2,1,0:T(8,128)}, f32[9,20,128]{2,1,0:T(8,128)S(1)}, u32[]{:S(2)}) %copy-start.22) | copy-done | bytes 92184
  21.3 9.0 %all-to-all-start = ((f32[128,1,1664]{2,1,0:T(1,128)}), f32[128,1,1664]{2,1,0:T(1,128)S(1)}, u32[]{:S(2)}, u32[]{:S(2)}) async-start(f32[128,1,1664]{2,1,0:T(1,128)} %bitcast.4), calls=%async_computation | async-start | bytes 1703936 | tf_op jit(solution)/shard_map/all_to_all | solution.py:473
  30.3 1.3 %copy-done.2 = f32[27,24,512]{2,1,0:T(8,128)S(1)} copy-done((f32[27,24,512]{2,1,0:T(8,128)S(1)}, f32[27,24,512]{2,1,0:T(8,128)}, u32[]{:S(2)}) %copy-start.2) | copy-done | bytes 1327128
  31.6 1.0 %copy-done.3 = bf16[448,512]{1,0:T(8,128)(2,1)S(1)} copy-done((bf16[448,512]{1,0:T(8,128)(2,1)S(1)}, bf16[448,512]{1,0:T(8,128)(2,1)}, u32[]{:S(2)}) %copy-start.3) | copy-done | bytes 458776
  32.7 0.8 %copy-done.13 = f32[4,20,16]{1,2,0:T(8,128)S(1)} copy-done((f32[4,20,16]{1,2,0:T(8,128)S(1)}, f32[4,20,16]{1,2,0:T(8,128)}, u32[]{:S(2)}) %copy-start.13) | copy-done | bytes 5144
  33.4 0.9 %copy-done.17 = f32[9,20,128]{2,1,0:T(8,128)S(1)} copy-done((f32[9,20,128]{2,1,0:T(8,128)S(1)}, f32[9,20,128]{2,1,0:T(8,128)}, u32[]{:S(2)}) %copy-start.17) | copy-done | bytes 92184
  34.3 0.9 %copy-done.19 = f32[9,20,128]{2,1,0:T(8,128)S(1)} copy-done((f32[9,20,128]{2,1,0:T(8,128)S(1)}, f32[9,20,128]{2,1,0:T(8,128)}, u32[]{:S(2)}) %copy-start.19) | copy-done | bytes 92184
  35.2 0.9 %copy-done.21 = f32[9,20,128]{2,1,0:T(8,128)S(1)} copy-done((f32[9,20,128]{2,1,0:T(8,128)S(1)}, f32[9,20,128]{2,1,0:T(8,128)}, u32[]{:S(2)}) %copy-start.21) | copy-done | bytes 92184
  36.1 0.9 %copy-done.23 = f32[9,20,128]{2,1,0:T(8,128)S(1)} copy-done((f32[9,20,128]{2,1,0:T(8,128)S(1)}, f32[9,20,128]{2,1,0:T(8,128)}, u32[]{:S(2)}) %copy-start.23) | copy-done | bytes 92184
  37.0 0.7 %copy-done.34 = f32[4,512]{1,0:T(4,128)S(1)} copy-done((f32[4,512]{1,0:T(4,128)S(1)}, f32[4,512]{1,0:T(4,128)}, u32[]{:S(2)}) %copy-start.34) | copy-done | bytes 8216
  37.7 0.7 %copy-done.35 = s32[4,512]{1,0:T(4,128)S(1)} copy-done((s32[4,512]{1,0:T(4,128)S(1)}, s32[4,512]{1,0:T(4,128)}, u32[]{:S(2)}) %copy-start.35) | copy-done | bytes 8216
  38.4 0.7 %copy-done.36 = s32[4,512]{1,0:T(4,128)S(1)} copy-done((s32[4,512]{1,0:T(4,128)S(1)}, s32[4,512]{1,0:T(4,128)}, u32[]{:S(2)}) %copy-start.36) | copy-done | bytes 8216
  39.1 7.1 %elements.1.base_in = f32[20,27,512]{2,1,0:T(8,128)} custom-call(f32[27,24,512]{2,1,0:T(8,128)S(1)} %copy-done.2, f32[20,27,512]{2,1,0:T(8,128)S(1)} %bitcast.8, f32[9,9,3,512]{3,2,1,0:T(4,128)S(1)} %bitcast.11, f32[3,6,512]{2,1,0:T(8,128)S(1)} %copy-done.8, f32[3,512]{1,0:T(4,128)S(1)} %copy-done.24, f32[9,9,512]{2,1,0:T(8,128)S(1)} %copy-done.4, ...), custom_call_target="tpu_custom_call" | custom-call | tf_op jit(solution)/shard_map/elements/pallas_call | solution.py:476
  46.2 1.8 %all-to-all-done = f32[128,1,1664]{2,1,0:T(1,128)S(1)} async-done(((f32[128,1,1664]{2,1,0:T(1,128)}), f32[128,1,1664]{2,1,0:T(1,128)S(1)}, u32[]{:S(2)}, u32[]{:S(2)}) %all-to-all-start) | async-done | bytes 852000 | tf_op jit(solution)/shard_map/all_to_all | solution.py:473
  48.0 0.9 %copy-done.7 = f32[128,512]{1,0:T(8,128)S(1)} copy-done((f32[128,512]{1,0:T(8,128)S(1)}, f32[128,512]{1,0:T(8,128)}, u32[]{:S(2)}) %copy-start.7) | copy-done | bytes 262168
  49.0 0.7 %copy-done.27 = s32[1,2048]{1,0:T(1,128)S(1)} copy-done((s32[1,2048]{1,0:T(1,128)S(1)}, s32[1,2048]{1,0:T(1,128)}, u32[]{:S(2)}) %copy-start.27) | copy-done | bytes 8216
  49.7 0.7 %copy-done.29 = s32[1,2048]{1,0:T(1,128)S(1)} copy-done((s32[1,2048]{1,0:T(1,128)S(1)}, s32[1,2048]{1,0:T(1,128)}, u32[]{:S(2)}) %copy-start.29) | copy-done | bytes 8216
  50.4 0.7 %copy-done.31 = s32[1,2048]{1,0:T(1,128)S(1)} copy-done((s32[1,2048]{1,0:T(1,128)S(1)}, s32[1,2048]{1,0:T(1,128)}, u32[]{:S(2)}) %copy-start.31) | copy-done | bytes 8216
  51.1 0.7 %copy-done.33 = s32[1,2048]{1,0:T(1,128)S(1)} copy-done((s32[1,2048]{1,0:T(1,128)S(1)}, s32[1,2048]{1,0:T(1,128)}, u32[]{:S(2)}) %copy-start.33) | copy-done | bytes 8216
  51.8 5.4 %fault.1 = f32[20,27,512]{2,1,0:T(8,128)} custom-call(f32[20,27,512]{2,1,0:T(8,128)} %elements.1.base_in, f32[1664,128]{1,0:T(8,128)} %get-tuple-element.31.mine, f32[1664,128]{1,0:T(8,128)S(1)} %bitcast.9, f32[128,512]{1,0:T(8,128)S(1)} %copy-done.7, s32[1,2048]{1,0:T(1,128)S(1)} %copy-done.25, ...), custom_call_target="tpu_custom_call", output_to_operand_aliasing={{}: (0, {})} | custom-call | tf_op jit(solution)/shard_map/fault/pallas_call | solution.py:500
  (40 shorter events, 0.1 us)
Async XLA Ops:
  0.0 14.6 %copy-start.32 = (s32[1,2048]{1,0:T(1,128)S(1)}, s32[1,2048]{1,0:T(1,128)}, u32[]{:S(2)}) copy-start(s32[1,2048]{1,0:T(1,128)} %live.3) | copy-start | bytes 24580
  0.0 14.6 %copy-start.30 = (s32[1,2048]{1,0:T(1,128)S(1)}, s32[1,2048]{1,0:T(1,128)}, u32[]{:S(2)}) copy-start(s32[1,2048]{1,0:T(1,128)} %fmf.3) | copy-start | bytes 24580
  0.0 14.6 %copy-start.28 = (s32[1,2048]{1,0:T(1,128)S(1)}, s32[1,2048]{1,0:T(1,128)}, u32[]{:S(2)}) copy-start(s32[1,2048]{1,0:T(1,128)} %fme.3) | copy-start | bytes 24580
  0.0 14.6 %copy-start.26 = (s32[1,2048]{1,0:T(1,128)S(1)}, s32[1,2048]{1,0:T(1,128)}, u32[]{:S(2)}) copy-start(s32[1,2048]{1,0:T(1,128)} %fsf.3) | copy-start | bytes 24580
  0.0 14.6 %copy-start.25 = (s32[1,2048]{1,0:T(1,128)S(1)}, s32[1,2048]{1,0:T(1,128)}, u32[]{:S(2)}) copy-start(s32[1,2048]{1,0:T(1,128)} %fse.3) | copy-start | bytes 24580
  0.0 14.6 %copy-start.15 = (f32[1,16,2048]{2,1,0:T(8,128)S(1)}, f32[1,16,2048]{2,1,0:T(8,128)}, u32[]{:S(2)}) copy-start(f32[1,16,2048]{2,1,0:T(8,128)} %state.1) | copy-start | bytes 393220
  0.0 14.6 %copy-start.14 = (f32[1,16,2048]{2,1,0:T(8,128)S(1)}, f32[1,16,2048]{2,1,0:T(8,128)}, u32[]{:S(2)}) copy-start(f32[1,16,2048]{2,1,0:T(8,128)} %load.1) | copy-start | bytes 393220
  0.1 14.6 %copy-start.12 = (f32[4,20,16]{1,2,0:T(8,128)S(1)}, f32[4,20,16]{1,2,0:T(8,128)}, u32[]{:S(2)}) copy-start(f32[4,20,16]{1,2,0:T(8,128)} %param.29) | copy-start | bytes 15364
  0.1 30.2 %copy-start.4 = (f32[9,9,512]{2,1,0:T(8,128)S(1)}, f32[9,9,512]{2,1,0:T(8,128)}, u32[]{:S(2)}) copy-start(f32[9,9,512]{2,1,0:T(8,128)} %fminus.1) | copy-start | bytes 497668
  0.1 30.2 %copy-start.5 = (f32[9,9,512]{2,1,0:T(8,128)S(1)}, f32[9,9,512]{2,1,0:T(8,128)}, u32[]{:S(2)}) copy-start(f32[9,9,512]{2,1,0:T(8,128)} %fplus.1) | copy-start | bytes 497668
  0.1 30.2 %copy-start.10 = (f32[3,20,20]{2,1,0:T(8,128)S(1)}, f32[3,20,20]{2,1,0:T(8,128)}, u32[]{:S(2)}) copy-start(f32[3,20,20]{2,1,0:T(8,128)} %kdiff.3) | copy-start | bytes 14404
  0.1 30.2 %copy-start.11 = (f32[4,16,20]{2,1,0:T(8,128)S(1)}, f32[4,16,20]{2,1,0:T(8,128)}, u32[]{:S(2)}) copy-start(f32[4,16,20]{2,1,0:T(8,128)} %lift.3) | copy-start | bytes 15364
  0.1 30.2 %copy-start.24 = (f32[3,512]{1,0:T(4,128)S(1)}, f32[3,512]{1,0:T(4,128)}, u32[]{:S(2)}) copy-start(f32[3,512]{1,0:T(4,128)} %omega.3) | copy-start | bytes 18436
  8.4 21.9 %copy-start = (f32[27,20,512]{2,0,1:T(8,128)S(1)}, f32[27,20,512]{2,0,1:T(8,128)}, u32[]{:S(2)}) copy-start(f32[27,20,512]{2,0,1:T(8,128)} %param.21) | copy-start | bytes 3317764
  8.4 21.9 %copy-start.1 = (f32[3,9,9,512]{3,0,2,1:T(4,128)S(1)}, f32[3,9,9,512]{3,0,2,1:T(4,128)}, u32[]{:S(2)}) copy-start(f32[3,9,9,512]{3,0,2,1:T(4,128)} %param.22) | copy-start | bytes 1492996
  8.4 21.9 %copy-start.8 = (f32[3,6,512]{2,1,0:T(8,128)S(1)}, f32[3,6,512]{2,1,0:T(8,128)}, u32[]{:S(2)}) copy-start(f32[3,6,512]{2,1,0:T(8,128)} %couple.3) | copy-start | bytes 110596
  8.4 10.3 %collective-permute-start = (f32[9,20,128]{2,1,0:T(8,128)}, f32[9,20,128]{2,1,0:T(8,128)S(1)}, u32[]{:S(2)}, u32[]{:S(2)}) collective-permute-start(f32[9,20,128]{2,1,0:T(8,128)} %get-tuple-element.21), channel_id=1, source_target_pairs={{0,4},{8,12},{16,20},{24,28},{32,36},{40,44},{48,52},{56,60},{64,6... | collective-permute-start | bytes 276488 | tf_op jit(solution)/shard_map/ppermute | solution.py:466
  9.9 9.4 %collective-permute-start.1 = (f32[9,20,128]{2,1,0:T(8,128)}, f32[9,20,128]{2,1,0:T(8,128)S(1)}, u32[]{:S(2)}, u32[]{:S(2)}) collective-permute-start(f32[9,20,128]{2,1,0:T(8,128)} %get-tuple-element.22), channel_id=1, source_target_pairs={{4,8},{12,16},{20,24},{28,32},{36,40},{44,48},{52,56},{60,64},{68,... | collective-permute-start | bytes 276488 | tf_op jit(solution)/shard_map/ppermute | solution.py:466
  11.6 8.4 %collective-permute-start.2 = (f32[9,20,128]{2,1,0:T(8,128)}, f32[9,20,128]{2,1,0:T(8,128)S(1)}, u32[]{:S(2)}, u32[]{:S(2)}) collective-permute-start(f32[9,20,128]{2,1,0:T(8,128)} %get-tuple-element.23), channel_id=1, source_target_pairs={{0,1},{2,3},{1,0},{3,2},{4,5},{6,7},{5,4},{7,6},{8,9},{10,11},{9,8... | collective-permute-start | bytes 276488 | tf_op jit(solution)/shard_map/ppermute | solution.py:466
  12.8 7.8 %collective-permute-start.3 = (f32[9,20,128]{2,1,0:T(8,128)}, f32[9,20,128]{2,1,0:T(8,128)S(1)}, u32[]{:S(2)}, u32[]{:S(2)}) collective-permute-start(f32[9,20,128]{2,1,0:T(8,128)} %get-tuple-element.24), channel_id=1, source_target_pairs={{1,2},{3,0},{2,1},{0,3},{5,6},{7,4},{6,5},{4,7},{9,10},{11,8},{10,... | collective-permute-start | bytes 276488 | tf_op jit(solution)/shard_map/ppermute | solution.py:466
  14.7 0.9 %copy-start.9 = (bf16[160,512]{1,0:T(8,128)(2,1)S(1)}, bf16[160,512]{1,0:T(8,128)(2,1)}, u32[]{:S(2)}) copy-start(bf16[160,512]{1,0:T(8,128)(2,1)} %get-tuple-element.25.fhl) | copy-start | bytes 491524
  17.9 0.7 %copy-start.6 = (f32[128,512]{1,0:T(8,128)}, f32[128,512]{1,0:T(8,128)S(1)}, u32[]{:S(2)}) copy-start(f32[128,512]{1,0:T(8,128)S(1)} %get-tuple-element.32.keep) | copy-start | bytes 786436
  18.7 0.6 %copy-start.16 = (f32[9,20,128]{2,1,0:T(8,128)}, f32[9,20,128]{2,1,0:T(8,128)S(1)}, u32[]{:S(2)}) copy-start(f32[9,20,128]{2,1,0:T(8,128)S(1)} %collective-permute-done.rim0) | copy-start | bytes 276484
  19.3 0.7 %copy-start.18 = (f32[9,20,128]{2,1,0:T(8,128)}, f32[9,20,128]{2,1,0:T(8,128)S(1)}, u32[]{:S(2)}) copy-start(f32[9,20,128]{2,1,0:T(8,128)S(1)} %collective-permute-done.1.rim1) | copy-start | bytes 276484
  20.0 0.6 %copy-start.20 = (f32[9,20,128]{2,1,0:T(8,128)}, f32[9,20,128]{2,1,0:T(8,128)S(1)}, u32[]{:S(2)}) copy-start(f32[9,20,128]{2,1,0:T(8,128)S(1)} %collective-permute-done.2.rim2) | copy-start | bytes 276484
  20.6 0.6 %copy-start.22 = (f32[9,20,128]{2,1,0:T(8,128)}, f32[9,20,128]{2,1,0:T(8,128)S(1)}, u32[]{:S(2)}) copy-start(f32[9,20,128]{2,1,0:T(8,128)S(1)} %collective-permute-done.3.rim3) | copy-start | bytes 276484
  21.3 26.8 %all-to-all-start = ((f32[128,1,1664]{2,1,0:T(1,128)}), f32[128,1,1664]{2,1,0:T(1,128)S(1)}, u32[]{:S(2)}, u32[]{:S(2)}) async-start(f32[128,1,1664]{2,1,0:T(1,128)} %bitcast.4), calls=%async_computation | async-start | bytes 1703936 | tf_op jit(solution)/shard_map/all_to_all | solution.py:473
  30.3 1.3 %copy-start.2 = (f32[27,24,512]{2,1,0:T(8,128)S(1)}, f32[27,24,512]{2,1,0:T(8,128)}, u32[]{:S(2)}) copy-start(f32[27,24,512]{2,1,0:T(8,128)} %get-tuple-element.19.integ) | copy-start | bytes 3981316
  31.6 1.0 %copy-start.3 = (bf16[448,512]{1,0:T(8,128)(2,1)S(1)}, bf16[448,512]{1,0:T(8,128)(2,1)}, u32[]{:S(2)}) copy-start(bf16[448,512]{1,0:T(8,128)(2,1)} %get-tuple-element.20.ihl) | copy-start | bytes 1376260
  32.7 0.8 %copy-start.13 = (f32[4,20,16]{1,2,0:T(8,128)S(1)}, f32[4,20,16]{1,2,0:T(8,128)}, u32[]{:S(2)}) copy-start(f32[4,20,16]{1,2,0:T(8,128)} %param.29) | copy-start | bytes 15364
  33.4 0.9 %copy-start.17 = (f32[9,20,128]{2,1,0:T(8,128)S(1)}, f32[9,20,128]{2,1,0:T(8,128)}, u32[]{:S(2)}) copy-start(f32[9,20,128]{2,1,0:T(8,128)} %copy-done.16) | copy-start | bytes 276484
  34.3 0.9 %copy-start.19 = (f32[9,20,128]{2,1,0:T(8,128)S(1)}, f32[9,20,128]{2,1,0:T(8,128)}, u32[]{:S(2)}) copy-start(f32[9,20,128]{2,1,0:T(8,128)} %copy-done.18) | copy-start | bytes 276484
  35.2 0.9 %copy-start.21 = (f32[9,20,128]{2,1,0:T(8,128)S(1)}, f32[9,20,128]{2,1,0:T(8,128)}, u32[]{:S(2)}) copy-start(f32[9,20,128]{2,1,0:T(8,128)} %copy-done.20) | copy-start | bytes 276484
  36.1 0.9 %copy-start.23 = (f32[9,20,128]{2,1,0:T(8,128)S(1)}, f32[9,20,128]{2,1,0:T(8,128)}, u32[]{:S(2)}) copy-start(f32[9,20,128]{2,1,0:T(8,128)} %copy-done.22) | copy-start | bytes 276484
  37.0 0.7 %copy-start.34 = (f32[4,512]{1,0:T(4,128)S(1)}, f32[4,512]{1,0:T(4,128)}, u32[]{:S(2)}) copy-start(f32[4,512]{1,0:T(4,128)} %area.1) | copy-start | bytes 24580
  37.7 0.7 %copy-start.35 = (s32[4,512]{1,0:T(4,128)S(1)}, s32[4,512]{1,0:T(4,128)}, u32[]{:S(2)}) copy-start(s32[4,512]{1,0:T(4,128)} %nelem.1) | copy-start | bytes 24580
  38.4 0.7 %copy-start.36 = (s32[4,512]{1,0:T(4,128)S(1)}, s32[4,512]{1,0:T(4,128)}, u32[]{:S(2)}) copy-start(s32[4,512]{1,0:T(4,128)} %nface.1) | copy-start | bytes 24580
  48.0 1.0 %copy-start.7 = (f32[128,512]{1,0:T(8,128)S(1)}, f32[128,512]{1,0:T(8,128)}, u32[]{:S(2)}) copy-start(f32[128,512]{1,0:T(8,128)} %copy-done.6) | copy-start | bytes 786436
  49.0 0.7 %copy-start.27 = (s32[1,2048]{1,0:T(1,128)S(1)}, s32[1,2048]{1,0:T(1,128)}, u32[]{:S(2)}) copy-start(s32[1,2048]{1,0:T(1,128)} %fsf.3) | copy-start | bytes 24580
  49.7 0.7 %copy-start.29 = (s32[1,2048]{1,0:T(1,128)S(1)}, s32[1,2048]{1,0:T(1,128)}, u32[]{:S(2)}) copy-start(s32[1,2048]{1,0:T(1,128)} %fme.3) | copy-start | bytes 24580
  50.4 0.7 %copy-start.31 = (s32[1,2048]{1,0:T(1,128)S(1)}, s32[1,2048]{1,0:T(1,128)}, u32[]{:S(2)}) copy-start(s32[1,2048]{1,0:T(1,128)} %fmf.3) | copy-start | bytes 24580
  51.1 0.7 %copy-start.33 = (s32[1,2048]{1,0:T(1,128)S(1)}, s32[1,2048]{1,0:T(1,128)}, u32[]{:S(2)}) copy-start(s32[1,2048]{1,0:T(1,128)} %live.3) | copy-start | bytes 24580

commit v6 on v5

--- a/solution.py
+++ b/solution.py
@@ -28,7 +28,7 @@
 F32 = jnp.float32
 BF = jnp.bfloat16
 VMEM = 56 * 1024 * 1024
-VMEM_SMALL = 40 * 1024 * 1024
+VMEM_SMALL = 56 * 1024 * 1024
 FAULT_ROWS = (0, 3, 6)
 
 
@@ -77,6 +77,28 @@
         here = jnp.concatenate([index[:, t * LANES : (t + 1) * LANES]] * (rows // 16), axis=0)
         out.append(jnp.where(row == here, jnp.ones((), BF), jnp.zeros((), BF)))
     return jnp.concatenate(out, axis=1)
+
+
+def one_hot_t(index, columns):
+    column = lax.broadcasted_iota(jnp.int32, (16, columns), 1).astype(jnp.int16)
+    column = jnp.concatenate([column] * (LANES // 16), axis=0)
+    out = []
+    for t in range(index.shape[1] // LANES):
+        here = jnp.broadcast_to(index[:, t * LANES : (t + 1) * LANES], (LANES, LANES))
+        here = jnp.transpose(here, (1, 0)).astype(jnp.int16)
+        here = jnp.concatenate([here] * (columns // LANES), axis=1)
+        out.append(jnp.where(column == here, jnp.ones((), BF), jnp.zeros((), BF)))
+    return jnp.concatenate(out, axis=0)
+
+
+def fetches(sources, held, sems):
+    copies = [
+        pltpu.make_async_copy(source, place, sems.at[n])
+        for n, (source, place) in enumerate(zip(sources, held))
+    ]
+    for copy in copies:
+        copy.start()
+    return copies
 
 
 def swap_blocks(x):
@@ -205,8 +227,20 @@
     return values
 
 
-def slot_kernel(fhl, proj, fse, fsf, fme, fmf, live, load, state, out, keep, mat, fpw):
+SLOT_SHAPES = ((4, NP, NB), (160, E_DEV), *[(1, SLOTS)] * 5, (1, NP, SLOTS), (1, NP, SLOTS))
+SLOT_TYPES = (F32, BF, *[jnp.int32] * 5, F32, F32)
+
+
+def slot_kernel(*refs):
+    count = len(SLOT_SHAPES)
+    sources, (out_to, keep_to, mat, fpw, out, keep) = refs[:count], refs[count : count + 6]
+    held, sems = refs[count + 6 : -1], refs[-1]
+    fetch = fetches(sources, held, sems)
+    proj, fhl, fse, fsf, fme, fmf, live, load, state = held
+    fetch[0].wait()
     fpw[...] = left3(mat, [(0, g * NP, proj[g].T) for g in range(4)], 32, 64)
+    for copy in fetch[1:]:
+        copy.wait()
 
     def place(tile, x):
         out[pl.ds(tile, DEVICES, stride=TILES), :] = to_blocks(x)
@@ -228,6 +262,9 @@
         for g in range(2):
             at = (2 * n + g) * LANES
             keep[:, at : at + LANES] = to_blocks(x[8 * g : 8 * g + 8])
+    writes = fetches((out, keep), (out_to, keep_to), sems)
+    for copy in writes:
+        copy.wait()
 
 
 def element_kernel(
@@ -346,15 +383,32 @@
     return trial - ETA * slip, slip
 
 
+FAULT_SHAPES = (
+    (4, NP, NB), (1, SLOTS), (1, SLOTS), *[(DEVICES * TILES, LANES)] * 2, (DEVICES, 4 * LANES), *[(1, SLOTS)] * 3,
+)
+FAULT_TYPES = (F32, jnp.int32, jnp.int32, F32, F32, F32, *[jnp.int32] * 3)
+
+
 def fault_kernel(
-    base_in, mine, theirs, keep, fse, fsf, fme, fmf, live, lift,
-    base, mat, lfw, slab, sem,
+    base_in, *refs
 ):
     del base_in
+    count = len(FAULT_SHAPES)
+    sources, (base, mat, lfw, slab, spots) = refs[:count], refs[count : count + 5]
+    held = refs[count + 5 : -1]
+    sem = refs[-1].at[count]
+    fetch = fetches(sources, held, refs[-1])
+    lift, fme, fse, theirs, mine, keep, fmf, live, fsf = held
     window = base.at[:, 0:8, :]
     read_slab = pltpu.make_async_copy(window, slab, sem)
     read_slab.start()
+    fetch[0].wait()
     lfw[...] = left3(mat, [(0, f * NBP, lift[f]) for f in range(4)], 16, 96)
+    for n, elem in enumerate((fme, fse)):
+        fetch[1 + n].wait()
+        spots[n * SLOTS : (n + 1) * SLOTS, :] = one_hot_t(elem[...], E_DEV)
+    for copy in fetch[3:]:
+        copy.wait()
 
     def tile(ref, n):
         return ref[pl.ds(n, DEVICES, stride=TILES), :]
@@ -362,7 +416,7 @@
     def pair(ref, n):
         return jnp.concatenate([tile(ref, 2 * n), tile(ref, 2 * n + 1)], axis=1)
 
-    def side(one, other, load, state, kept, sign, alive, face, elem):
+    def side(one, other, load, state, kept, sign, alive, face, rows):
         pull, slip = friction(0.5 * (pair(theirs, other[0]) + pair(mine, one[0])), pair(mine, one[1]) + pair(theirs, other[1]), load, state)
         right = []
         for t in (pull - kept, sign * slip):
@@ -377,16 +431,16 @@
                 y = jnp.where(face == f, added[f * NBP : (f + 1) * NBP, at], y)
             sums.append(y * alive)
         hi, lo = split(jnp.concatenate(sums, axis=0))
-        return dot_nt(jnp.concatenate([hi, lo], axis=0), one_hot(elem, E_DEV))
+        return dot(jnp.concatenate([hi, lo], axis=0), spots[rows, :])
 
     minus = side(
         (2, 3), (0, 1), pair(mine, 4), pair(mine, 5), keep[:, 256:512], -0.5,
-        live[...].astype(F32), fmf[...], fme[...],
+        live[...].astype(F32), fmf[...], slice(0, SLOTS),
     )
     far = to_slots(tile(theirs, 12))[0:1]
     plus = side(
         (0, 1), (2, 3), pair(theirs, 4), pair(theirs, 5), keep[:, 0:256], 0.5,
-        far, fsf[...], fse[...],
+        far, fsf[...], slice(SLOTS, 2 * SLOTS),
     )
     both = minus + plus
     delta = both[0:48] + both[48:96]
@@ -423,7 +477,7 @@
     star = jnp.transpose(star, (1, 2, 0, 3))
     face_proj = jnp.transpose(face_proj, (0, 2, 1))
     rim = whole((NE, NB, BND))
-    resident = pl.BlockSpec(memory_space=pltpu.VMEM)
+    anywhere = pl.BlockSpec(memory_space=pl.ANY)
     params = pltpu.CompilerParams(vmem_limit_bytes=VMEM)
     small = pltpu.CompilerParams(vmem_limit_bytes=VMEM_SMALL)
     integ, ihl, fhl, s0, s1, s2, s3 = pl.pallas_call(
@@ -449,14 +503,19 @@
     )(dofs, star, couple, omega, wc, kdiff, send_rows)
     out, keep = pl.pallas_call(
         slot_kernel,
-        in_specs=[resident] * 9,
-        out_specs=[resident] * 2,
+        in_specs=[anywhere] * len(SLOT_SHAPES),
+        out_specs=[anywhere] * 2,
         out_shape=[shape((DEVICES * TILES, LANES), F32), shape((DEVICES, 4 * LANES), F32)],
-        scratch_shapes=[pltpu.VMEM((64, LANES), F32), pltpu.VMEM((64, 96), BF)],
+        scratch_shapes=[
+            pltpu.VMEM((64, LANES), F32), pltpu.VMEM((64, 96), BF),
+            pltpu.VMEM((DEVICES * TILES, LANES), F32), pltpu.VMEM((DEVICES, 4 * LANES), F32),
+            *[pltpu.VMEM(n, t) for n, t in zip(SLOT_SHAPES, SLOT_TYPES)],
+            pltpu.SemaphoreType.DMA((len(SLOT_SHAPES),)),
+        ],
         compiler_params=small,
         name="slots",
     )(
-        fhl, face_proj, fault_send_elem, fault_send_face, fault_minus_elem, fault_minus_face,
+        face_proj, fhl, fault_send_elem, fault_send_face, fault_minus_elem, fault_minus_face,
         fault_live, normal_load, state,
     )
     ns, nd = lax.axis_size("strike"), lax.axis_size("depth")
@@ -496,22 +555,23 @@
         integ, dofs, star, couple, omega, flux_minus, flux_plus, area, nbr_elem, nbr_face,
         ihl, r0, r1, r2, r3, kdiff, face_proj, face_lift,
     )
-    anywhere = pl.BlockSpec(memory_space=pl.ANY)
     result = pl.pallas_call(
         fault_kernel,
-        in_specs=[anywhere] + [resident] * 9,
+        in_specs=[anywhere] * (1 + len(FAULT_SHAPES)),
         out_specs=anywhere,
         out_shape=shape((NB, NQ, E_DEV), F32),
         input_output_aliases={0: 0},
         scratch_shapes=[
             pltpu.VMEM((64, LANES), F32), pltpu.VMEM((96, 48), BF),
-            pltpu.VMEM((NB, 8, E_DEV), F32), pltpu.SemaphoreType.DMA,
+            pltpu.VMEM((NB, 8, E_DEV), F32), pltpu.VMEM((2 * SLOTS, E_DEV), BF),
+            *[pltpu.VMEM(n, t) for n, t in zip(FAULT_SHAPES, FAULT_TYPES)],
+            pltpu.SemaphoreType.DMA((len(FAULT_SHAPES) + 1,)),
         ],
         compiler_params=small,
         name="fault",
     )(
-        base, sent, theirs, keep, fault_send_elem, fault_send_face, fault_minus_elem, fault_minus_face,
-        fault_live, face_lift,
+        base, face_lift, fault_minus_elem, fault_send_elem, theirs, sent, keep, fault_minus_face,
+        fault_live, fault_send_face,
     )
     return jnp.transpose(result, (1, 0, 2))
 

time: 58.1 us -> 51.1 us (0.88)
  local copies, waits for them, and re-layouts: 16.8 us -> 0.94 us
  waiting for transfers between devices: 1.83 us -> 9.47 us
  Pallas kernels: 23.1 us -> 24.7 us
    unnamed x74 -> x10, local copies, waits for them, and re-layouts: 16.8 us -> 0.94 us
    all_to_all x1, waiting for transfers between devices: 1.82 us -> 9.46 us  [per_device(): lax.all_to_all(sent.reshape(DEVICES, 1, TILES * LANES), ('strike', 'depth...]
    pallas_call x1, Pallas kernels: 7.1 us -> 8.26 us  [per_device(): pl.pallas_call(element_kernel, grid=(CHUNKS,), in_specs=[lanes(NQ, NBP),...]
  transfers between devices with their start and end apart: 5 -> 5, of which waited for: 1 -> 1; matrix products, arithmetic and copies ran while one was open for 0% -> 0% of each run, Pallas kernels for 17% -> 23%
where the time goes in v6:
time: 51.1 us; the launch traced here: 50.8 us
  Pallas kernels  24.7 us (48%)
  starting transfers between devices  15.5 us (30%)
  waiting for transfers between devices  9.47 us (19%)
  local copies, waits for them, and re-layouts  0.94 us (2%)
    all_to_all x1, waiting for transfers between devices, per_device(): lax.all_to_all(sent.reshape(DEVICES, 1, TILES * LANES), ('strike', 'depth...  9.46 us
    all_to_all x1, starting transfers between devices, per_device(): lax.all_to_all(sent.reshape(DEVICES, 1, TILES * LANES), ('strike', 'depth...  9.3 us
    pallas_call x1, Pallas kernels, per_device(): pl.pallas_call(element_kernel, grid=(CHUNKS,), in_specs=[lanes(NQ, NBP),...  8.26 us
    pallas_call x1, Pallas kernels, per_device(): pl.pallas_call(predict_kernel, grid=(CHUNKS // PAIR,), in_specs=[wide(NB,...  8.12 us
    ppermute x4, starting transfers between devices, swap(): return lax.ppermute(x, axis, ends + [(j, i) for i, j in ends])  6.23 us
    pallas_call x1, Pallas kernels, per_device(): pl.pallas_call(fault_kernel, in_specs=[anywhere] * (1 + len(FAULT_SHAPES)...  4.66 us
    pallas_call x1, Pallas kernels, per_device(): pl.pallas_call(slot_kernel, in_specs=[anywhere] * len(SLOT_SHAPES), out_s...  3.67 us
  transfers between devices with their start and end apart: 5, of which 1 were waited for; matrix products, arithmetic and copies ran while one was open for 0% of the time, Pallas kernels for 23%

profile of v6, /device:TPU:1, one launch (start us, length us, event | category | flops | bytes accessed | tf_op | source)
XLA Modules:
  0.0 50.8 jit_solution(9554724847443598328)
XLA Ops:
  0.0 8.1 %predict.1 = (f32[27,24,512]{2,1,0:T(8,128)}, bf16[448,512]{1,0:T(8,128)(2,1)}, bf16[160,512]{1,0:T(8,128)(2,1)}, f32[9,20,128]{2,1,0:T(8,128)}, f32[9,20,128]{2...) custom-call(f32[20,27,512]{2,1,0:T(8,128)} %bitcast.7, f32[9,9,3,512]{3,2,1,0:T(4,128)} %bitcast.11, ...), custom_call_target="tpu_custom_call" | custom-call | tf_op jit(solution)/shard_map/predict/pallas_call | solution.py:483
  8.1 1.5 %collective-permute-start = (f32[9,20,128]{2,1,0:T(8,128)}, f32[9,20,128]{2,1,0:T(8,128)S(1)}, u32[]{:S(2)}, u32[]{:S(2)}) collective-permute-start(f32[9,20,128]{2,1,0:T(8,128)} %get-tuple-element.21), channel_id=1, source_target_pairs={{0,4},{8,12},{16,20},{24,28},{32,36},{40,44},{48,52},{56,60},{64,6... | collective-permute-start | bytes 276488 | tf_op jit(solution)/shard_map/ppermute | solution.py:525
  9.6 1.7 %collective-permute-start.1 = (f32[9,20,128]{2,1,0:T(8,128)}, f32[9,20,128]{2,1,0:T(8,128)S(1)}, u32[]{:S(2)}, u32[]{:S(2)}) collective-permute-start(f32[9,20,128]{2,1,0:T(8,128)} %get-tuple-element.22), channel_id=1, source_target_pairs={{4,8},{12,16},{20,24},{28,32},{36,40},{44,48},{52,56},{60,64},{68,... | collective-permute-start | bytes 276488 | tf_op jit(solution)/shard_map/ppermute | solution.py:525
  11.3 1.2 %collective-permute-start.2 = (f32[9,20,128]{2,1,0:T(8,128)}, f32[9,20,128]{2,1,0:T(8,128)S(1)}, u32[]{:S(2)}, u32[]{:S(2)}) collective-permute-start(f32[9,20,128]{2,1,0:T(8,128)} %get-tuple-element.23), channel_id=1, source_target_pairs={{0,1},{2,3},{1,0},{3,2},{4,5},{6,7},{5,4},{7,6},{8,9},{10,11},{9,8... | collective-permute-start | bytes 276488 | tf_op jit(solution)/shard_map/ppermute | solution.py:525
  12.5 1.8 %collective-permute-start.3 = (f32[9,20,128]{2,1,0:T(8,128)}, f32[9,20,128]{2,1,0:T(8,128)S(1)}, u32[]{:S(2)}, u32[]{:S(2)}) collective-permute-start(f32[9,20,128]{2,1,0:T(8,128)} %get-tuple-element.24), channel_id=1, source_target_pairs={{1,2},{3,0},{2,1},{0,3},{5,6},{7,4},{6,5},{4,7},{9,10},{11,8},{10,... | collective-permute-start | bytes 276488 | tf_op jit(solution)/shard_map/ppermute | solution.py:525
  14.3 3.7 %slots.1 = (f32[1664,128]{1,0:T(8,128)}, f32[128,512]{1,0:T(8,128)}) custom-call(f32[4,16,20]{2,1,0:T(8,128)} %bitcast.13, bf16[160,512]{1,0:T(8,128)(2,1)} %get-tuple-element.25.refs_1_, s32[1,2048]{1,0:T(1,128)} %refs_2_.3, s32[1,2048]{1,0:T(1,128)} %refs_8_.3, s32[1,2048]{1,0:T(1,128)} %refs_1_.1, s32[1,2048]{1,0:T(1,128)} %refs_6_.3, s32[1,2048]{1,0:T(1,128)} %refs_7_.3, ...), custom_call_target="tpu_custom_call" | custom-call | tf_op jit(solution)/shard_map/slots/pallas_call | solution.py:504
  18.0 0.0 collective-permute-done.rim0
  18.0 0.0 copy-start.1
  18.1 0.0 collective-permute-done.1.rim1
  18.1 0.0 copy-start.2
  18.1 0.0 collective-permute-done.2.rim2
  18.1 0.0 copy-start.3
  18.1 0.0 collective-permute-done.3.rim3
  18.1 0.0 copy-start.4
  18.1 9.3 %all-to-all-start = ((f32[128,1,1664]{2,1,0:T(1,128)}), f32[128,1,1664]{2,1,0:T(1,128)S(1)}, u32[]{:S(2)}, u32[]{:S(2)}) async-start(f32[128,1,1664]{2,1,0:T(1,128)} %bitcast.9), calls=%async_computation | async-start | bytes 1703936 | tf_op jit(solution)/shard_map/all_to_all | solution.py:532
  27.4 0.0 copy-done.1
  27.4 0.0 copy-done.2
  27.4 0.0 copy-done.3
  27.5 0.0 copy-done.4
  27.5 8.3 %elements.1.base_in = f32[20,27,512]{2,1,0:T(8,128)} custom-call(f32[27,24,512]{2,1,0:T(8,128)} %get-tuple-element.19.integ, f32[20,27,512]{2,1,0:T(8,128)} %bitcast.8, f32[9,9,3,512]{3,2,1,0:T(4,128)} %bitcast.12, f32[3,6,512]{2,1,0:T(8,128)} %couple.3, f32[3,512]{1,0:T(4,128)} %omega.3, f32[9,9,512]{2,1,0:T(8,128)} %fminus.1, f32[9,9,512]{2,1,0:T(8,128)} %fplus.1, ...), custom_call_target="tpu_custom_call" | custom-call | tf_op jit(solution)/shard_map/elements/pallas_call | solution.py:535
  35.7 9.5 %all-to-all-done = f32[128,1,1664]{2,1,0:T(1,128)S(1)} async-done(((f32[128,1,1664]{2,1,0:T(1,128)}), f32[128,1,1664]{2,1,0:T(1,128)S(1)}, u32[]{:S(2)}, u32[]{:S(2)}) %all-to-all-start) | async-done | bytes 852000 | tf_op jit(solution)/shard_map/all_to_all | solution.py:532
  45.2 0.0 copy-start
  45.2 0.9 %copy-done = f32[128,1,1664]{2,1,0:T(1,128)} copy-done((f32[128,1,1664]{2,1,0:T(1,128)}, f32[128,1,1664]{2,1,0:T(1,128)S(1)}, u32[]{:S(2)}) %copy-start) | copy-done | bytes 851992
  46.1 4.7 %fault.1 = f32[20,27,512]{2,1,0:T(8,128)} custom-call(f32[20,27,512]{2,1,0:T(8,128)} %elements.1.base_in, f32[4,16,20]{2,1,0:T(8,128)} %refs_0_.1, s32[1,2048]{1,0:T(1,128)} %refs_1_.1, s32[1,2048]{1,0:T(1,128)} %refs_2_.3, f32[1664,128]{1,0:T(8,128)} %bitcast.10, f32[1664,128]{1,0:T(8,128)} %get-tuple-element.31.refs_4_, ...), custom_call_target="tpu_custom_call", output_to_operand_aliasing={{}: (0, {})} | custom-call | tf_op jit(solution)/shard_map/fault/pallas_call | solution.py:558
Async XLA Ops:
  8.1 9.9 %collective-permute-start = (f32[9,20,128]{2,1,0:T(8,128)}, f32[9,20,128]{2,1,0:T(8,128)S(1)}, u32[]{:S(2)}, u32[]{:S(2)}) collective-permute-start(f32[9,20,128]{2,1,0:T(8,128)} %get-tuple-element.21), channel_id=1, source_target_pairs={{0,4},{8,12},{16,20},{24,28},{32,36},{40,44},{48,52},{56,60},{64,6... | collective-permute-start | bytes 276488 | tf_op jit(solution)/shard_map/ppermute | solution.py:525
  9.6 8.4 %collective-permute-start.1 = (f32[9,20,128]{2,1,0:T(8,128)}, f32[9,20,128]{2,1,0:T(8,128)S(1)}, u32[]{:S(2)}, u32[]{:S(2)}) collective-permute-start(f32[9,20,128]{2,1,0:T(8,128)} %get-tuple-element.22), channel_id=1, source_target_pairs={{4,8},{12,16},{20,24},{28,32},{36,40},{44,48},{52,56},{60,64},{68,... | collective-permute-start | bytes 276488 | tf_op jit(solution)/shard_map/ppermute | solution.py:525
  11.3 6.8 %collective-permute-start.2 = (f32[9,20,128]{2,1,0:T(8,128)}, f32[9,20,128]{2,1,0:T(8,128)S(1)}, u32[]{:S(2)}, u32[]{:S(2)}) collective-permute-start(f32[9,20,128]{2,1,0:T(8,128)} %get-tuple-element.23), channel_id=1, source_target_pairs={{0,1},{2,3},{1,0},{3,2},{4,5},{6,7},{5,4},{7,6},{8,9},{10,11},{9,8... | collective-permute-start | bytes 276488 | tf_op jit(solution)/shard_map/ppermute | solution.py:525
  12.5 5.6 %collective-permute-start.3 = (f32[9,20,128]{2,1,0:T(8,128)}, f32[9,20,128]{2,1,0:T(8,128)S(1)}, u32[]{:S(2)}, u32[]{:S(2)}) collective-permute-start(f32[9,20,128]{2,1,0:T(8,128)} %get-tuple-element.24), channel_id=1, source_target_pairs={{1,2},{3,0},{2,1},{0,3},{5,6},{7,4},{6,5},{4,7},{9,10},{11,8},{10,... | collective-permute-start | bytes 276488 | tf_op jit(solution)/shard_map/ppermute | solution.py:525
  18.0 9.4 %copy-start.1 = (f32[9,20,128]{2,1,0:T(8,128)}, f32[9,20,128]{2,1,0:T(8,128)S(1)}, u32[]{:S(2)}) copy-start(f32[9,20,128]{2,1,0:T(8,128)S(1)} %collective-permute-done.rim0) | copy-start | bytes 276484
  18.1 9.4 %copy-start.2 = (f32[9,20,128]{2,1,0:T(8,128)}, f32[9,20,128]{2,1,0:T(8,128)S(1)}, u32[]{:S(2)}) copy-start(f32[9,20,128]{2,1,0:T(8,128)S(1)} %collective-permute-done.1.rim1) | copy-start | bytes 276484
  18.1 9.4 %copy-start.3 = (f32[9,20,128]{2,1,0:T(8,128)}, f32[9,20,128]{2,1,0:T(8,128)S(1)}, u32[]{:S(2)}) copy-start(f32[9,20,128]{2,1,0:T(8,128)S(1)} %collective-permute-done.2.rim2) | copy-start | bytes 276484
  18.1 9.4 %copy-start.4 = (f32[9,20,128]{2,1,0:T(8,128)}, f32[9,20,128]{2,1,0:T(8,128)S(1)}, u32[]{:S(2)}) copy-start(f32[9,20,128]{2,1,0:T(8,128)S(1)} %collective-permute-done.3.rim3) | copy-start | bytes 276484
  18.1 27.1 %all-to-all-start = ((f32[128,1,1664]{2,1,0:T(1,128)}), f32[128,1,1664]{2,1,0:T(1,128)S(1)}, u32[]{:S(2)}, u32[]{:S(2)}) async-start(f32[128,1,1664]{2,1,0:T(1,128)} %bitcast.9), calls=%async_computation | async-start | bytes 1703936 | tf_op jit(solution)/shard_map/all_to_all | solution.py:532
  45.2 0.9 %copy-start = (f32[128,1,1664]{2,1,0:T(1,128)}, f32[128,1,1664]{2,1,0:T(1,128)S(1)}, u32[]{:S(2)}) copy-start(f32[128,1,1664]{2,1,0:T(1,128)S(1)} %all-to-all-done) | copy-start | bytes 2555908

commit v7 on v6

--- a/solution.py
+++ b/solution.py
@@ -384,13 +384,13 @@
 
 
 FAULT_SHAPES = (
-    (4, NP, NB), (1, SLOTS), (1, SLOTS), *[(DEVICES * TILES, LANES)] * 2, (DEVICES, 4 * LANES), *[(1, SLOTS)] * 3,
+    (4, NP, NB), (1, SLOTS), (1, SLOTS), (DEVICES * TILES, LANES), (DEVICES, 4 * LANES), *[(1, SLOTS)] * 3,
 )
-FAULT_TYPES = (F32, jnp.int32, jnp.int32, F32, F32, F32, *[jnp.int32] * 3)
+FAULT_TYPES = (F32, jnp.int32, jnp.int32, F32, F32, *[jnp.int32] * 3)
 
 
 def fault_kernel(
-    base_in, *refs
+    base_in, theirs, *refs
 ):
     del base_in
     count = len(FAULT_SHAPES)
@@ -398,7 +398,7 @@
     held = refs[count + 5 : -1]
     sem = refs[-1].at[count]
     fetch = fetches(sources, held, refs[-1])
-    lift, fme, fse, theirs, mine, keep, fmf, live, fsf = held
+    lift, fme, fse, mine, keep, fmf, live, fsf = held
     window = base.at[:, 0:8, :]
     read_slab = pltpu.make_async_copy(window, slab, sem)
     read_slab.start()
@@ -557,7 +557,7 @@
     )
     result = pl.pallas_call(
         fault_kernel,
-        in_specs=[anywhere] * (1 + len(FAULT_SHAPES)),
+        in_specs=[anywhere, pl.BlockSpec(memory_space=pltpu.VMEM)] + [anywhere] * len(FAULT_SHAPES),
         out_specs=anywhere,
         out_shape=shape((NB, NQ, E_DEV), F32),
         input_output_aliases={0: 0},
@@ -570,7 +570,7 @@
         compiler_params=small,
         name="fault",
     )(
-        base, face_lift, fault_minus_elem, fault_send_elem, theirs, sent, keep, fault_minus_face,
+        base, theirs, face_lift, fault_minus_elem, fault_send_elem, sent, keep, fault_minus_face,
         fault_live, fault_send_face,
     )
     return jnp.transpose(result, (1, 0, 2))

time: 51.1 us -> 52.2 us (1.022)
  Pallas kernels: 24.7 us -> 25.9 us
    pallas_call x1, Pallas kernels: 4.66 us -> 5.81 us  [per_device(): pl.pallas_call(fault_kernel, in_specs=[anywhere, pl.BlockSpec(memory_spac...]
where the time goes in v7:
time: 52.2 us; the launch traced here: 51.9 us
  Pallas kernels  25.9 us (50%)
  starting transfers between devices  15.5 us (30%)
  waiting for transfers between devices  9.47 us (18%)
  local copies, waits for them, and re-layouts  0.94 us (2%)
    all_to_all x1, waiting for transfers between devices, per_device(): lax.all_to_all(sent.reshape(DEVICES, 1, TILES * LANES), ('strike', 'depth...  9.46 us
    all_to_all x1, starting transfers between devices, per_device(): lax.all_to_all(sent.reshape(DEVICES, 1, TILES * LANES), ('strike', 'depth...  9.3 us
    pallas_call x1, Pallas kernels, per_device(): pl.pallas_call(element_kernel, grid=(CHUNKS,), in_specs=[lanes(NQ, NBP),...  8.26 us
    pallas_call x1, Pallas kernels, per_device(): pl.pallas_call(predict_kernel, grid=(CHUNKS // PAIR,), in_specs=[wide(NB,...  8.12 us
    ppermute x4, starting transfers between devices, swap(): return lax.ppermute(x, axis, ends + [(j, i) for i, j in ends])  6.23 us
    pallas_call x1, Pallas kernels, per_device(): pl.pallas_call(fault_kernel, in_specs=[anywhere, pl.BlockSpec(memory_spac...  5.81 us
    pallas_call x1, Pallas kernels, per_device(): pl.pallas_call(slot_kernel, in_specs=[anywhere] * len(SLOT_SHAPES), out_s...  3.67 us
  transfers between devices with their start and end apart: 5, of which 1 were waited for; matrix products, arithmetic and copies ran while one was open for 0% of the time, Pallas kernels for 23%

profile of v7, /device:TPU:1, one launch (start us, length us, event | category | flops | bytes accessed | tf_op | source)
XLA Modules:
  0.0 51.9 jit_solution(4192430750051508339)
XLA Ops:
  0.0 8.1 %predict.1 = (f32[27,24,512]{2,1,0:T(8,128)}, bf16[448,512]{1,0:T(8,128)(2,1)}, bf16[160,512]{1,0:T(8,128)(2,1)}, f32[9,20,128]{2,1,0:T(8,128)}, f32[9,20,128]{2...) custom-call(f32[20,27,512]{2,1,0:T(8,128)} %bitcast.7, f32[9,9,3,512]{3,2,1,0:T(4,128)} %bitcast.11, ...), custom_call_target="tpu_custom_call" | custom-call | tf_op jit(solution)/shard_map/predict/pallas_call | solution.py:483
  8.1 1.5 %collective-permute-start = (f32[9,20,128]{2,1,0:T(8,128)}, f32[9,20,128]{2,1,0:T(8,128)S(1)}, u32[]{:S(2)}, u32[]{:S(2)}) collective-permute-start(f32[9,20,128]{2,1,0:T(8,128)} %get-tuple-element.21), channel_id=1, source_target_pairs={{0,4},{8,12},{16,20},{24,28},{32,36},{40,44},{48,52},{56,60},{64,6... | collective-permute-start | bytes 276488 | tf_op jit(solution)/shard_map/ppermute | solution.py:525
  9.6 1.7 %collective-permute-start.1 = (f32[9,20,128]{2,1,0:T(8,128)}, f32[9,20,128]{2,1,0:T(8,128)S(1)}, u32[]{:S(2)}, u32[]{:S(2)}) collective-permute-start(f32[9,20,128]{2,1,0:T(8,128)} %get-tuple-element.22), channel_id=1, source_target_pairs={{4,8},{12,16},{20,24},{28,32},{36,40},{44,48},{52,56},{60,64},{68,... | collective-permute-start | bytes 276488 | tf_op jit(solution)/shard_map/ppermute | solution.py:525
  11.3 1.2 %collective-permute-start.2 = (f32[9,20,128]{2,1,0:T(8,128)}, f32[9,20,128]{2,1,0:T(8,128)S(1)}, u32[]{:S(2)}, u32[]{:S(2)}) collective-permute-start(f32[9,20,128]{2,1,0:T(8,128)} %get-tuple-element.23), channel_id=1, source_target_pairs={{0,1},{2,3},{1,0},{3,2},{4,5},{6,7},{5,4},{7,6},{8,9},{10,11},{9,8... | collective-permute-start | bytes 276488 | tf_op jit(solution)/shard_map/ppermute | solution.py:525
  12.5 1.8 %collective-permute-start.3 = (f32[9,20,128]{2,1,0:T(8,128)}, f32[9,20,128]{2,1,0:T(8,128)S(1)}, u32[]{:S(2)}, u32[]{:S(2)}) collective-permute-start(f32[9,20,128]{2,1,0:T(8,128)} %get-tuple-element.24), channel_id=1, source_target_pairs={{1,2},{3,0},{2,1},{0,3},{5,6},{7,4},{6,5},{4,7},{9,10},{11,8},{10,... | collective-permute-start | bytes 276488 | tf_op jit(solution)/shard_map/ppermute | solution.py:525
  14.3 3.7 %slots.1 = (f32[1664,128]{1,0:T(8,128)}, f32[128,512]{1,0:T(8,128)}) custom-call(f32[4,16,20]{2,1,0:T(8,128)} %bitcast.13, bf16[160,512]{1,0:T(8,128)(2,1)} %get-tuple-element.25.refs_1_, s32[1,2048]{1,0:T(1,128)} %refs_2_.3, s32[1,2048]{1,0:T(1,128)} %refs_7_.3, s32[1,2048]{1,0:T(1,128)} %refs_1_.1, s32[1,2048]{1,0:T(1,128)} %refs_5_.3, s32[1,2048]{1,0:T(1,128)} %refs_6_.3, ...), custom_call_target="tpu_custom_call" | custom-call | tf_op jit(solution)/shard_map/slots/pallas_call | solution.py:504
  18.0 0.0 collective-permute-done.rim0
  18.0 0.0 copy-start.1
  18.1 0.0 collective-permute-done.1.rim1
  18.1 0.0 copy-start.2
  18.1 0.0 collective-permute-done.2.rim2
  18.1 0.0 copy-start.3
  18.1 0.0 collective-permute-done.3.rim3
  18.1 0.0 copy-start.4
  18.1 9.3 %all-to-all-start = ((f32[128,1,1664]{2,1,0:T(1,128)}), f32[128,1,1664]{2,1,0:T(1,128)S(1)}, u32[]{:S(2)}, u32[]{:S(2)}) async-start(f32[128,1,1664]{2,1,0:T(1,128)} %bitcast.9), calls=%async_computation | async-start | bytes 1703936 | tf_op jit(solution)/shard_map/all_to_all | solution.py:532
  27.4 0.0 copy-done.1
  27.4 0.0 copy-done.2
  27.4 0.0 copy-done.3
  27.5 0.0 copy-done.4
  27.5 8.3 %elements.1.base_in = f32[20,27,512]{2,1,0:T(8,128)} custom-call(f32[27,24,512]{2,1,0:T(8,128)} %get-tuple-element.19.integ, f32[20,27,512]{2,1,0:T(8,128)} %bitcast.8, f32[9,9,3,512]{3,2,1,0:T(4,128)} %bitcast.12, f32[3,6,512]{2,1,0:T(8,128)} %couple.3, f32[3,512]{1,0:T(4,128)} %omega.3, f32[9,9,512]{2,1,0:T(8,128)} %fminus.1, f32[9,9,512]{2,1,0:T(8,128)} %fplus.1, ...), custom_call_target="tpu_custom_call" | custom-call | tf_op jit(solution)/shard_map/elements/pallas_call | solution.py:535
  35.7 9.5 %all-to-all-done = f32[128,1,1664]{2,1,0:T(1,128)S(1)} async-done(((f32[128,1,1664]{2,1,0:T(1,128)}), f32[128,1,1664]{2,1,0:T(1,128)S(1)}, u32[]{:S(2)}, u32[]{:S(2)}) %all-to-all-start) | async-done | bytes 852000 | tf_op jit(solution)/shard_map/all_to_all | solution.py:532
  45.2 0.0 copy-start
  45.2 0.9 %copy-done = f32[128,1,1664]{2,1,0:T(1,128)} copy-done((f32[128,1,1664]{2,1,0:T(1,128)}, f32[128,1,1664]{2,1,0:T(1,128)S(1)}, u32[]{:S(2)}) %copy-start) | copy-done | bytes 851992
  46.1 5.8 %fault.1 = f32[20,27,512]{2,1,0:T(8,128)} custom-call(f32[20,27,512]{2,1,0:T(8,128)} %elements.1.base_in, f32[1664,128]{1,0:T(8,128)} %bitcast.10, f32[4,16,20]{2,1,0:T(8,128)} %refs_0_.1, s32[1,2048]{1,0:T(1,128)} %refs_1_.1, s32[1,2048]{1,0:T(1,128)} %refs_2_.3, f32[1664,128]{1,0:T(8,128)} %get-tuple-element.31.refs_3_, ...), custom_call_target="tpu_custom_call", output_to_operand_aliasing={{}: (0, {})} | custom-call | tf_op jit(solution)/shard_map/fault/pallas_call | solution.py:558
Async XLA Ops:
  8.1 9.9 %collective-permute-start = (f32[9,20,128]{2,1,0:T(8,128)}, f32[9,20,128]{2,1,0:T(8,128)S(1)}, u32[]{:S(2)}, u32[]{:S(2)}) collective-permute-start(f32[9,20,128]{2,1,0:T(8,128)} %get-tuple-element.21), channel_id=1, source_target_pairs={{0,4},{8,12},{16,20},{24,28},{32,36},{40,44},{48,52},{56,60},{64,6... | collective-permute-start | bytes 276488 | tf_op jit(solution)/shard_map/ppermute | solution.py:525
  9.6 8.4 %collective-permute-start.1 = (f32[9,20,128]{2,1,0:T(8,128)}, f32[9,20,128]{2,1,0:T(8,128)S(1)}, u32[]{:S(2)}, u32[]{:S(2)}) collective-permute-start(f32[9,20,128]{2,1,0:T(8,128)} %get-tuple-element.22), channel_id=1, source_target_pairs={{4,8},{12,16},{20,24},{28,32},{36,40},{44,48},{52,56},{60,64},{68,... | collective-permute-start | bytes 276488 | tf_op jit(solution)/shard_map/ppermute | solution.py:525
  11.3 6.8 %collective-permute-start.2 = (f32[9,20,128]{2,1,0:T(8,128)}, f32[9,20,128]{2,1,0:T(8,128)S(1)}, u32[]{:S(2)}, u32[]{:S(2)}) collective-permute-start(f32[9,20,128]{2,1,0:T(8,128)} %get-tuple-element.23), channel_id=1, source_target_pairs={{0,1},{2,3},{1,0},{3,2},{4,5},{6,7},{5,4},{7,6},{8,9},{10,11},{9,8... | collective-permute-start | bytes 276488 | tf_op jit(solution)/shard_map/ppermute | solution.py:525
  12.5 5.6 %collective-permute-start.3 = (f32[9,20,128]{2,1,0:T(8,128)}, f32[9,20,128]{2,1,0:T(8,128)S(1)}, u32[]{:S(2)}, u32[]{:S(2)}) collective-permute-start(f32[9,20,128]{2,1,0:T(8,128)} %get-tuple-element.24), channel_id=1, source_target_pairs={{1,2},{3,0},{2,1},{0,3},{5,6},{7,4},{6,5},{4,7},{9,10},{11,8},{10,... | collective-permute-start | bytes 276488 | tf_op jit(solution)/shard_map/ppermute | solution.py:525
  18.0 9.4 %copy-start.1 = (f32[9,20,128]{2,1,0:T(8,128)}, f32[9,20,128]{2,1,0:T(8,128)S(1)}, u32[]{:S(2)}) copy-start(f32[9,20,128]{2,1,0:T(8,128)S(1)} %collective-permute-done.rim0) | copy-start | bytes 276484
  18.1 9.4 %copy-start.2 = (f32[9,20,128]{2,1,0:T(8,128)}, f32[9,20,128]{2,1,0:T(8,128)S(1)}, u32[]{:S(2)}) copy-start(f32[9,20,128]{2,1,0:T(8,128)S(1)} %collective-permute-done.1.rim1) | copy-start | bytes 276484
  18.1 9.4 %copy-start.3 = (f32[9,20,128]{2,1,0:T(8,128)}, f32[9,20,128]{2,1,0:T(8,128)S(1)}, u32[]{:S(2)}) copy-start(f32[9,20,128]{2,1,0:T(8,128)S(1)} %collective-permute-done.2.rim2) | copy-start | bytes 276484
  18.1 9.4 %copy-start.4 = (f32[9,20,128]{2,1,0:T(8,128)}, f32[9,20,128]{2,1,0:T(8,128)S(1)}, u32[]{:S(2)}) copy-start(f32[9,20,128]{2,1,0:T(8,128)S(1)} %collective-permute-done.3.rim3) | copy-start | bytes 276484
  18.1 27.1 %all-to-all-start = ((f32[128,1,1664]{2,1,0:T(1,128)}), f32[128,1,1664]{2,1,0:T(1,128)S(1)}, u32[]{:S(2)}, u32[]{:S(2)}) async-start(f32[128,1,1664]{2,1,0:T(1,128)} %bitcast.9), calls=%async_computation | async-start | bytes 1703936 | tf_op jit(solution)/shard_map/all_to_all | solution.py:532
  45.2 0.9 %copy-start = (f32[128,1,1664]{2,1,0:T(1,128)}, f32[128,1,1664]{2,1,0:T(1,128)S(1)}, u32[]{:S(2)}) copy-start(f32[128,1,1664]{2,1,0:T(1,128)S(1)} %all-to-all-done) | copy-start | bytes 2555908

commit v8 on v7

--- a/solution.py
+++ b/solution.py
@@ -28,7 +28,7 @@
 F32 = jnp.float32
 BF = jnp.bfloat16
 VMEM = 56 * 1024 * 1024
-VMEM_SMALL = 56 * 1024 * 1024
+VMEM_SMALL = 24 * 1024 * 1024
 FAULT_ROWS = (0, 3, 6)
 
 
@@ -478,6 +478,7 @@
     face_proj = jnp.transpose(face_proj, (0, 2, 1))
     rim = whole((NE, NB, BND))
     anywhere = pl.BlockSpec(memory_space=pl.ANY)
+    outside = pl.BlockSpec(memory_space=pltpu.HBM)
     params = pltpu.CompilerParams(vmem_limit_bytes=VMEM)
     small = pltpu.CompilerParams(vmem_limit_bytes=VMEM_SMALL)
     integ, ihl, fhl, s0, s1, s2, s3 = pl.pallas_call(
@@ -512,7 +513,7 @@
             *[pltpu.VMEM(n, t) for n, t in zip(SLOT_SHAPES, SLOT_TYPES)],
             pltpu.SemaphoreType.DMA((len(SLOT_SHAPES),)),
         ],
-        compiler_params=small,
+        compiler_params=params,
         name="slots",
     )(
         face_proj, fhl, fault_send_elem, fault_send_face, fault_minus_elem, fault_minus_face,
@@ -549,7 +550,7 @@
             pltpu.VMEM((96, 96), BF), pltpu.VMEM((2 * ROWS, 4 * BND), BF),
             pltpu.VMEM((NQ, NBP, LANES), F32),
         ],
-        compiler_params=small,
+        compiler_params=params,
         name="elements",
     )(
         integ, dofs, star, couple, omega, flux_minus, flux_plus, area, nbr_elem, nbr_face,
@@ -557,8 +558,8 @@
     )
     result = pl.pallas_call(
         fault_kernel,
-        in_specs=[anywhere, pl.BlockSpec(memory_space=pltpu.VMEM)] + [anywhere] * len(FAULT_SHAPES),
-        out_specs=anywhere,
+        in_specs=[outside, pl.BlockSpec(memory_space=pltpu.VMEM)] + [outside] * len(FAULT_SHAPES),
+        out_specs=outside,
         out_shape=shape((NB, NQ, E_DEV), F32),
         input_output_aliases={0: 0},
         scratch_shapes=[
@@ -570,8 +571,14 @@
         compiler_params=small,
         name="fault",
     )(
-        base, theirs, face_lift, fault_minus_elem, fault_send_elem, sent, keep, fault_minus_face,
-        fault_live, fault_send_face,
+        base, pltpu.with_memory_space_constraint(theirs, pltpu.VMEM),
+        *[
+            pltpu.with_memory_space_constraint(x, pltpu.HBM)
+            for x in (
+                face_lift, fault_minus_elem, fault_send_elem, sent, keep, fault_minus_face, fault_live,
+                fault_send_face,
+            )
+        ],
     )
     return jnp.transpose(result, (1, 0, 2))
 

time: 52.2 us -> 50.1 us (0.960)
  Pallas kernels: 25.9 us -> 24.7 us
  local copies, waits for them, and re-layouts: 0.94 us -> 0.02 us
    pallas_call x1, Pallas kernels: 5.81 us -> 4.65 us  [per_device(): pl.pallas_call(fault_kernel, in_specs=[outside, pl.BlockSpec(memory_space...]
    unnamed x10 -> x8, local copies, waits for them, and re-layouts: 0.94 us -> 0.02 us
  transfers between devices with their start and end apart: 5 -> 5, of which waited for: 1 -> 1; matrix products, arithmetic and copies ran while one was open for 0% -> 0% of each run, Pallas kernels for 23% -> 24%
where the time goes in v8:
time: 50.1 us; the launch traced here: 49.8 us
  Pallas kernels  24.7 us (49%)
  starting transfers between devices  15.6 us (31%)
  waiting for transfers between devices  9.47 us (19%)
    all_to_all x1, waiting for transfers between devices, per_device(): lax.all_to_all(sent.reshape(DEVICES, 1, TILES * LANES), ('strike', 'depth...  9.46 us
    all_to_all x1, starting transfers between devices, per_device(): lax.all_to_all(sent.reshape(DEVICES, 1, TILES * LANES), ('strike', 'depth...  9.33 us
    pallas_call x1, Pallas kernels, per_device(): pl.pallas_call(element_kernel, grid=(CHUNKS,), in_specs=[lanes(NQ, NBP),...  8.26 us
    pallas_call x1, Pallas kernels, per_device(): pl.pallas_call(predict_kernel, grid=(CHUNKS // PAIR,), in_specs=[wide(NB,...  8.12 us
    ppermute x4, starting transfers between devices, swap(): return lax.ppermute(x, axis, ends + [(j, i) for i, j in ends])  6.23 us
    pallas_call x1, Pallas kernels, per_device(): pl.pallas_call(fault_kernel, in_specs=[outside, pl.BlockSpec(memory_space...  4.65 us
    pallas_call x1, Pallas kernels, per_device(): pl.pallas_call(slot_kernel, in_specs=[anywhere] * len(SLOT_SHAPES), out_s...  3.64 us
  transfers between devices with their start and end apart: 5, of which 1 were waited for; matrix products, arithmetic and copies ran while one was open for 0% of the time, Pallas kernels for 24%

profile of v8, /device:TPU:1, one launch (start us, length us, event | category | flops | bytes accessed | tf_op | source)
XLA Modules:
  0.0 49.8 jit_solution(10159320868034539249)
XLA Ops:
  0.0 8.1 %predict.1 = (f32[27,24,512]{2,1,0:T(8,128)}, bf16[448,512]{1,0:T(8,128)(2,1)}, bf16[160,512]{1,0:T(8,128)(2,1)}, f32[9,20,128]{2,1,0:T(8,128)}, f32[9,20,128]{2...) custom-call(f32[20,27,512]{2,1,0:T(8,128)} %bitcast.8, f32[9,9,3,512]{3,2,1,0:T(4,128)} %bitcast.11, ...), custom_call_target="tpu_custom_call" | custom-call | tf_op jit(solution)/shard_map/predict/pallas_call | solution.py:484
  8.1 1.5 %collective-permute-start = (f32[9,20,128]{2,1,0:T(8,128)}, f32[9,20,128]{2,1,0:T(8,128)S(1)}, u32[]{:S(2)}, u32[]{:S(2)}) collective-permute-start(f32[9,20,128]{2,1,0:T(8,128)} %get-tuple-element.21), channel_id=1, source_target_pairs={{0,4},{8,12},{16,20},{24,28},{32,36},{40,44},{48,52},{56,60},{64,6... | collective-permute-start | bytes 276488 | tf_op jit(solution)/shard_map/ppermute | solution.py:526
  9.6 1.7 %collective-permute-start.1 = (f32[9,20,128]{2,1,0:T(8,128)}, f32[9,20,128]{2,1,0:T(8,128)S(1)}, u32[]{:S(2)}, u32[]{:S(2)}) collective-permute-start(f32[9,20,128]{2,1,0:T(8,128)} %get-tuple-element.22), channel_id=1, source_target_pairs={{4,8},{12,16},{20,24},{28,32},{36,40},{44,48},{52,56},{60,64},{68,... | collective-permute-start | bytes 276488 | tf_op jit(solution)/shard_map/ppermute | solution.py:526
  11.3 1.2 %collective-permute-start.2 = (f32[9,20,128]{2,1,0:T(8,128)}, f32[9,20,128]{2,1,0:T(8,128)S(1)}, u32[]{:S(2)}, u32[]{:S(2)}) collective-permute-start(f32[9,20,128]{2,1,0:T(8,128)} %get-tuple-element.23), channel_id=1, source_target_pairs={{0,1},{2,3},{1,0},{3,2},{4,5},{6,7},{5,4},{7,6},{8,9},{10,11},{9,8... | collective-permute-start | bytes 276488 | tf_op jit(solution)/shard_map/ppermute | solution.py:526
  12.5 1.8 %collective-permute-start.3 = (f32[9,20,128]{2,1,0:T(8,128)}, f32[9,20,128]{2,1,0:T(8,128)S(1)}, u32[]{:S(2)}, u32[]{:S(2)}) collective-permute-start(f32[9,20,128]{2,1,0:T(8,128)} %get-tuple-element.24), channel_id=1, source_target_pairs={{1,2},{3,0},{2,1},{0,3},{5,6},{7,4},{6,5},{4,7},{9,10},{11,8},{10,... | collective-permute-start | bytes 276488 | tf_op jit(solution)/shard_map/ppermute | solution.py:526
  14.4 3.6 %slots.1 = (f32[1664,128]{1,0:T(8,128)}, f32[128,512]{1,0:T(8,128)}) custom-call(f32[4,16,20]{2,1,0:T(8,128)} %bitcast.13, bf16[160,512]{1,0:T(8,128)(2,1)} %get-tuple-element.25.refs_1_, s32[1,2048]{1,0:T(1,128)} %refs_2_.3, s32[1,2048]{1,0:T(1,128)} %refs_7_.3, s32[1,2048]{1,0:T(1,128)} %refs_1_.1, s32[1,2048]{1,0:T(1,128)} %refs_5_.3, s32[1,2048]{1,0:T(1,128)} %refs_6_.3, ...), custom_call_target="tpu_custom_call" | custom-call | tf_op jit(solution)/shard_map/slots/pallas_call | solution.py:505
  18.0 0.0 collective-permute-done.rim0
  18.0 0.0 copy-start
  18.0 0.0 collective-permute-done.1.rim1
  18.0 0.0 copy-start.1
  18.0 0.0 collective-permute-done.2.rim2
  18.1 0.0 copy-start.2
  18.1 0.0 collective-permute-done.3.rim3
  18.1 0.0 copy-start.3
  18.1 9.3 %all-to-all-start = ((f32[128,1,1664]{2,1,0:T(1,128)}), f32[128,1,1664]{2,1,0:T(1,128)S(1)}, u32[]{:S(2)}, u32[]{:S(2)}) async-start(f32[128,1,1664]{2,1,0:T(1,128)} %bitcast.10), calls=%async_computation | async-start | bytes 1703936 | tf_op jit(solution)/shard_map/all_to_all | solution.py:533
  27.4 0.0 copy-done
  27.4 0.0 copy-done.1
  27.4 0.0 copy-done.2
  27.5 0.0 copy-done.3
  27.5 8.3 %elements.1.base_in = f32[20,27,512]{2,1,0:T(8,128)} custom-call(f32[27,24,512]{2,1,0:T(8,128)} %get-tuple-element.19.integ, f32[20,27,512]{2,1,0:T(8,128)} %bitcast.9, f32[9,9,3,512]{3,2,1,0:T(4,128)} %bitcast.12, f32[3,6,512]{2,1,0:T(8,128)} %couple.3, f32[3,512]{1,0:T(4,128)} %omega.3, f32[9,9,512]{2,1,0:T(8,128)} %fminus.1, f32[9,9,512]{2,1,0:T(8,128)} %fplus.1, ...), custom_call_target="tpu_custom_call" | custom-call | tf_op jit(solution)/shard_map/elements/pallas_call | solution.py:536
  35.7 9.5 %all-to-all-done = f32[128,1,1664]{2,1,0:T(1,128)S(1)} async-done(((f32[128,1,1664]{2,1,0:T(1,128)}), f32[128,1,1664]{2,1,0:T(1,128)S(1)}, u32[]{:S(2)}, u32[]{:S(2)}) %all-to-all-start) | async-done | bytes 852000 | tf_op jit(solution)/shard_map/all_to_all | solution.py:533
  45.2 4.7 %fault.1 = f32[20,27,512]{2,1,0:T(8,128)} custom-call(f32[20,27,512]{2,1,0:T(8,128)} %elements.1.base_in, f32[1664,128]{1,0:T(8,128)S(1)} %bitcast.7, f32[4,16,20]{2,1,0:T(8,128)} %refs_0_.1, s32[1,2048]{1,0:T(1,128)} %refs_1_.1, s32[1,2048]{1,0:T(1,128)} %refs_2_.3, f32[1664,128]{1,0:T(8,128)} %get-tuple-element.31.refs_3_, ...), custom_call_target="tpu_custom_call", output_to_operand_aliasing={{}: (0, {})} | custom-call | tf_op jit(solution)/shard_map/fault/pallas_call | solution.py:559
Async XLA Ops:
  8.1 9.9 %collective-permute-start = (f32[9,20,128]{2,1,0:T(8,128)}, f32[9,20,128]{2,1,0:T(8,128)S(1)}, u32[]{:S(2)}, u32[]{:S(2)}) collective-permute-start(f32[9,20,128]{2,1,0:T(8,128)} %get-tuple-element.21), channel_id=1, source_target_pairs={{0,4},{8,12},{16,20},{24,28},{32,36},{40,44},{48,52},{56,60},{64,6... | collective-permute-start | bytes 276488 | tf_op jit(solution)/shard_map/ppermute | solution.py:526
  9.6 8.4 %collective-permute-start.1 = (f32[9,20,128]{2,1,0:T(8,128)}, f32[9,20,128]{2,1,0:T(8,128)S(1)}, u32[]{:S(2)}, u32[]{:S(2)}) collective-permute-start(f32[9,20,128]{2,1,0:T(8,128)} %get-tuple-element.22), channel_id=1, source_target_pairs={{4,8},{12,16},{20,24},{28,32},{36,40},{44,48},{52,56},{60,64},{68,... | collective-permute-start | bytes 276488 | tf_op jit(solution)/shard_map/ppermute | solution.py:526
  11.3 6.7 %collective-permute-start.2 = (f32[9,20,128]{2,1,0:T(8,128)}, f32[9,20,128]{2,1,0:T(8,128)S(1)}, u32[]{:S(2)}, u32[]{:S(2)}) collective-permute-start(f32[9,20,128]{2,1,0:T(8,128)} %get-tuple-element.23), channel_id=1, source_target_pairs={{0,1},{2,3},{1,0},{3,2},{4,5},{6,7},{5,4},{7,6},{8,9},{10,11},{9,8... | collective-permute-start | bytes 276488 | tf_op jit(solution)/shard_map/ppermute | solution.py:526
  12.5 5.5 %collective-permute-start.3 = (f32[9,20,128]{2,1,0:T(8,128)}, f32[9,20,128]{2,1,0:T(8,128)S(1)}, u32[]{:S(2)}, u32[]{:S(2)}) collective-permute-start(f32[9,20,128]{2,1,0:T(8,128)} %get-tuple-element.24), channel_id=1, source_target_pairs={{1,2},{3,0},{2,1},{0,3},{5,6},{7,4},{6,5},{4,7},{9,10},{11,8},{10,... | collective-permute-start | bytes 276488 | tf_op jit(solution)/shard_map/ppermute | solution.py:526
  18.0 9.4 %copy-start = (f32[9,20,128]{2,1,0:T(8,128)}, f32[9,20,128]{2,1,0:T(8,128)S(1)}, u32[]{:S(2)}) copy-start(f32[9,20,128]{2,1,0:T(8,128)S(1)} %collective-permute-done.rim0) | copy-start | bytes 276484
  18.0 9.4 %copy-start.1 = (f32[9,20,128]{2,1,0:T(8,128)}, f32[9,20,128]{2,1,0:T(8,128)S(1)}, u32[]{:S(2)}) copy-start(f32[9,20,128]{2,1,0:T(8,128)S(1)} %collective-permute-done.1.rim1) | copy-start | bytes 276484
  18.1 9.4 %copy-start.2 = (f32[9,20,128]{2,1,0:T(8,128)}, f32[9,20,128]{2,1,0:T(8,128)S(1)}, u32[]{:S(2)}) copy-start(f32[9,20,128]{2,1,0:T(8,128)S(1)} %collective-permute-done.2.rim2) | copy-start | bytes 276484
  18.1 9.4 %copy-start.3 = (f32[9,20,128]{2,1,0:T(8,128)}, f32[9,20,128]{2,1,0:T(8,128)S(1)}, u32[]{:S(2)}) copy-start(f32[9,20,128]{2,1,0:T(8,128)S(1)} %collective-permute-done.3.rim3) | copy-start | bytes 276484
  18.1 27.1 %all-to-all-start = ((f32[128,1,1664]{2,1,0:T(1,128)}), f32[128,1,1664]{2,1,0:T(1,128)S(1)}, u32[]{:S(2)}, u32[]{:S(2)}) async-start(f32[128,1,1664]{2,1,0:T(1,128)} %bitcast.10), calls=%async_computation | async-start | bytes 1703936 | tf_op jit(solution)/shard_map/all_to_all | solution.py:533

commit v9 on v8

--- a/solution.py
+++ b/solution.py
@@ -237,10 +237,9 @@
     held, sems = refs[count + 6 : -1], refs[-1]
     fetch = fetches(sources, held, sems)
     proj, fhl, fse, fsf, fme, fmf, live, load, state = held
-    fetch[0].wait()
+    for copy in fetch:
+        copy.wait()
     fpw[...] = left3(mat, [(0, g * NP, proj[g].T) for g in range(4)], 32, 64)
-    for copy in fetch[1:]:
-        copy.wait()
 
     def place(tile, x):
         out[pl.ds(tile, DEVICES, stride=TILES), :] = to_blocks(x)
@@ -402,10 +401,10 @@
     window = base.at[:, 0:8, :]
     read_slab = pltpu.make_async_copy(window, slab, sem)
     read_slab.start()
-    fetch[0].wait()
+    for copy in fetch[:3]:
+        copy.wait()
     lfw[...] = left3(mat, [(0, f * NBP, lift[f]) for f in range(4)], 16, 96)
     for n, elem in enumerate((fme, fse)):
-        fetch[1 + n].wait()
         spots[n * SLOTS : (n + 1) * SLOTS, :] = one_hot_t(elem[...], E_DEV)
     for copy in fetch[3:]:
         copy.wait()

time: 50.1 us -> 50 us (level)
  no operation moved by 1% of the time
where the time goes in v9:
time: 50 us; the launch traced here: 49.7 us
  Pallas kernels  24.5 us (49%)
  starting transfers between devices  15.6 us (31%)
  waiting for transfers between devices  9.47 us (19%)
    all_to_all x1, waiting for transfers between devices, per_device(): lax.all_to_all(sent.reshape(DEVICES, 1, TILES * LANES), ('strike', 'depth...  9.46 us
    all_to_all x1, starting transfers between devices, per_device(): lax.all_to_all(sent.reshape(DEVICES, 1, TILES * LANES), ('strike', 'depth...  9.33 us
    pallas_call x1, Pallas kernels, per_device(): pl.pallas_call(element_kernel, grid=(CHUNKS,), in_specs=[lanes(NQ, NBP),...  8.26 us
    pallas_call x1, Pallas kernels, per_device(): pl.pallas_call(predict_kernel, grid=(CHUNKS // PAIR,), in_specs=[wide(NB,...  8.12 us
    ppermute x4, starting transfers between devices, swap(): return lax.ppermute(x, axis, ends + [(j, i) for i, j in ends])  6.23 us
    pallas_call x1, Pallas kernels, per_device(): pl.pallas_call(fault_kernel, in_specs=[outside, pl.BlockSpec(memory_space...  4.49 us
    pallas_call x1, Pallas kernels, per_device(): pl.pallas_call(slot_kernel, in_specs=[anywhere] * len(SLOT_SHAPES), out_s...  3.64 us
  transfers between devices with their start and end apart: 5, of which 1 were waited for; matrix products, arithmetic and copies ran while one was open for 0% of the time, Pallas kernels for 24%

profile of v9, /device:TPU:1, one launch (start us, length us, event | category | flops | bytes accessed | tf_op | source)
XLA Modules:
  0.0 49.7 jit_solution(10636459258252820502)
XLA Ops:
  0.0 8.1 %predict.1 = (f32[27,24,512]{2,1,0:T(8,128)}, bf16[448,512]{1,0:T(8,128)(2,1)}, bf16[160,512]{1,0:T(8,128)(2,1)}, f32[9,20,128]{2,1,0:T(8,128)}, f32[9,20,128]{2...) custom-call(f32[20,27,512]{2,1,0:T(8,128)} %bitcast.8, f32[9,9,3,512]{3,2,1,0:T(4,128)} %bitcast.11, ...), custom_call_target="tpu_custom_call" | custom-call | tf_op jit(solution)/shard_map/predict/pallas_call | solution.py:483
  8.1 1.5 %collective-permute-start = (f32[9,20,128]{2,1,0:T(8,128)}, f32[9,20,128]{2,1,0:T(8,128)S(1)}, u32[]{:S(2)}, u32[]{:S(2)}) collective-permute-start(f32[9,20,128]{2,1,0:T(8,128)} %get-tuple-element.21), channel_id=1, source_target_pairs={{0,4},{8,12},{16,20},{24,28},{32,36},{40,44},{48,52},{56,60},{64,6... | collective-permute-start | bytes 276488 | tf_op jit(solution)/shard_map/ppermute | solution.py:525
  9.6 1.7 %collective-permute-start.1 = (f32[9,20,128]{2,1,0:T(8,128)}, f32[9,20,128]{2,1,0:T(8,128)S(1)}, u32[]{:S(2)}, u32[]{:S(2)}) collective-permute-start(f32[9,20,128]{2,1,0:T(8,128)} %get-tuple-element.22), channel_id=1, source_target_pairs={{4,8},{12,16},{20,24},{28,32},{36,40},{44,48},{52,56},{60,64},{68,... | collective-permute-start | bytes 276488 | tf_op jit(solution)/shard_map/ppermute | solution.py:525
  11.3 1.2 %collective-permute-start.2 = (f32[9,20,128]{2,1,0:T(8,128)}, f32[9,20,128]{2,1,0:T(8,128)S(1)}, u32[]{:S(2)}, u32[]{:S(2)}) collective-permute-start(f32[9,20,128]{2,1,0:T(8,128)} %get-tuple-element.23), channel_id=1, source_target_pairs={{0,1},{2,3},{1,0},{3,2},{4,5},{6,7},{5,4},{7,6},{8,9},{10,11},{9,8... | collective-permute-start | bytes 276488 | tf_op jit(solution)/shard_map/ppermute | solution.py:525
  12.5 1.8 %collective-permute-start.3 = (f32[9,20,128]{2,1,0:T(8,128)}, f32[9,20,128]{2,1,0:T(8,128)S(1)}, u32[]{:S(2)}, u32[]{:S(2)}) collective-permute-start(f32[9,20,128]{2,1,0:T(8,128)} %get-tuple-element.24), channel_id=1, source_target_pairs={{1,2},{3,0},{2,1},{0,3},{5,6},{7,4},{6,5},{4,7},{9,10},{11,8},{10,... | collective-permute-start | bytes 276488 | tf_op jit(solution)/shard_map/ppermute | solution.py:525
  14.4 3.6 %slots.1 = (f32[1664,128]{1,0:T(8,128)}, f32[128,512]{1,0:T(8,128)}) custom-call(f32[4,16,20]{2,1,0:T(8,128)} %bitcast.13, bf16[160,512]{1,0:T(8,128)(2,1)} %get-tuple-element.25.refs_1_, s32[1,2048]{1,0:T(1,128)} %refs_2_.3, s32[1,2048]{1,0:T(1,128)} %refs_7_.3, s32[1,2048]{1,0:T(1,128)} %refs_1_.1, s32[1,2048]{1,0:T(1,128)} %refs_5_.3, s32[1,2048]{1,0:T(1,128)} %refs_6_.3, ...), custom_call_target="tpu_custom_call" | custom-call | tf_op jit(solution)/shard_map/slots/pallas_call | solution.py:504
  18.0 0.0 collective-permute-done.rim0
  18.0 0.0 copy-start
  18.0 0.0 collective-permute-done.1.rim1
  18.0 0.0 copy-start.1
  18.0 0.0 collective-permute-done.2.rim2
  18.1 0.0 copy-start.2
  18.1 0.0 collective-permute-done.3.rim3
  18.1 0.0 copy-start.3
  18.1 9.3 %all-to-all-start = ((f32[128,1,1664]{2,1,0:T(1,128)}), f32[128,1,1664]{2,1,0:T(1,128)S(1)}, u32[]{:S(2)}, u32[]{:S(2)}) async-start(f32[128,1,1664]{2,1,0:T(1,128)} %bitcast.10), calls=%async_computation | async-start | bytes 1703936 | tf_op jit(solution)/shard_map/all_to_all | solution.py:532
  27.4 0.0 copy-done
  27.4 0.0 copy-done.1
  27.4 0.0 copy-done.2
  27.5 0.0 copy-done.3
  27.5 8.3 %elements.1.base_in = f32[20,27,512]{2,1,0:T(8,128)} custom-call(f32[27,24,512]{2,1,0:T(8,128)} %get-tuple-element.19.integ, f32[20,27,512]{2,1,0:T(8,128)} %bitcast.9, f32[9,9,3,512]{3,2,1,0:T(4,128)} %bitcast.12, f32[3,6,512]{2,1,0:T(8,128)} %couple.3, f32[3,512]{1,0:T(4,128)} %omega.3, f32[9,9,512]{2,1,0:T(8,128)} %fminus.1, f32[9,9,512]{2,1,0:T(8,128)} %fplus.1, ...), custom_call_target="tpu_custom_call" | custom-call | tf_op jit(solution)/shard_map/elements/pallas_call | solution.py:535
  35.7 9.5 %all-to-all-done = f32[128,1,1664]{2,1,0:T(1,128)S(1)} async-done(((f32[128,1,1664]{2,1,0:T(1,128)}), f32[128,1,1664]{2,1,0:T(1,128)S(1)}, u32[]{:S(2)}, u32[]{:S(2)}) %all-to-all-start) | async-done | bytes 852000 | tf_op jit(solution)/shard_map/all_to_all | solution.py:532
  45.2 4.5 %fault.1 = f32[20,27,512]{2,1,0:T(8,128)} custom-call(f32[20,27,512]{2,1,0:T(8,128)} %elements.1.base_in, f32[1664,128]{1,0:T(8,128)S(1)} %bitcast.7, f32[4,16,20]{2,1,0:T(8,128)} %refs_0_.1, s32[1,2048]{1,0:T(1,128)} %refs_1_.1, s32[1,2048]{1,0:T(1,128)} %refs_2_.3, f32[1664,128]{1,0:T(8,128)} %get-tuple-element.31.refs_3_, ...), custom_call_target="tpu_custom_call", output_to_operand_aliasing={{}: (0, {})} | custom-call | tf_op jit(solution)/shard_map/fault/pallas_call | solution.py:558
Async XLA Ops:
  8.1 9.9 %collective-permute-start = (f32[9,20,128]{2,1,0:T(8,128)}, f32[9,20,128]{2,1,0:T(8,128)S(1)}, u32[]{:S(2)}, u32[]{:S(2)}) collective-permute-start(f32[9,20,128]{2,1,0:T(8,128)} %get-tuple-element.21), channel_id=1, source_target_pairs={{0,4},{8,12},{16,20},{24,28},{32,36},{40,44},{48,52},{56,60},{64,6... | collective-permute-start | bytes 276488 | tf_op jit(solution)/shard_map/ppermute | solution.py:525
  9.6 8.4 %collective-permute-start.1 = (f32[9,20,128]{2,1,0:T(8,128)}, f32[9,20,128]{2,1,0:T(8,128)S(1)}, u32[]{:S(2)}, u32[]{:S(2)}) collective-permute-start(f32[9,20,128]{2,1,0:T(8,128)} %get-tuple-element.22), channel_id=1, source_target_pairs={{4,8},{12,16},{20,24},{28,32},{36,40},{44,48},{52,56},{60,64},{68,... | collective-permute-start | bytes 276488 | tf_op jit(solution)/shard_map/ppermute | solution.py:525
  11.3 6.7 %collective-permute-start.2 = (f32[9,20,128]{2,1,0:T(8,128)}, f32[9,20,128]{2,1,0:T(8,128)S(1)}, u32[]{:S(2)}, u32[]{:S(2)}) collective-permute-start(f32[9,20,128]{2,1,0:T(8,128)} %get-tuple-element.23), channel_id=1, source_target_pairs={{0,1},{2,3},{1,0},{3,2},{4,5},{6,7},{5,4},{7,6},{8,9},{10,11},{9,8... | collective-permute-start | bytes 276488 | tf_op jit(solution)/shard_map/ppermute | solution.py:525
  12.5 5.5 %collective-permute-start.3 = (f32[9,20,128]{2,1,0:T(8,128)}, f32[9,20,128]{2,1,0:T(8,128)S(1)}, u32[]{:S(2)}, u32[]{:S(2)}) collective-permute-start(f32[9,20,128]{2,1,0:T(8,128)} %get-tuple-element.24), channel_id=1, source_target_pairs={{1,2},{3,0},{2,1},{0,3},{5,6},{7,4},{6,5},{4,7},{9,10},{11,8},{10,... | collective-permute-start | bytes 276488 | tf_op jit(solution)/shard_map/ppermute | solution.py:525
  18.0 9.4 %copy-start = (f32[9,20,128]{2,1,0:T(8,128)}, f32[9,20,128]{2,1,0:T(8,128)S(1)}, u32[]{:S(2)}) copy-start(f32[9,20,128]{2,1,0:T(8,128)S(1)} %collective-permute-done.rim0) | copy-start | bytes 276484
  18.0 9.4 %copy-start.1 = (f32[9,20,128]{2,1,0:T(8,128)}, f32[9,20,128]{2,1,0:T(8,128)S(1)}, u32[]{:S(2)}) copy-start(f32[9,20,128]{2,1,0:T(8,128)S(1)} %collective-permute-done.1.rim1) | copy-start | bytes 276484
  18.1 9.4 %copy-start.2 = (f32[9,20,128]{2,1,0:T(8,128)}, f32[9,20,128]{2,1,0:T(8,128)S(1)}, u32[]{:S(2)}) copy-start(f32[9,20,128]{2,1,0:T(8,128)S(1)} %collective-permute-done.2.rim2) | copy-start | bytes 276484
  18.1 9.4 %copy-start.3 = (f32[9,20,128]{2,1,0:T(8,128)}, f32[9,20,128]{2,1,0:T(8,128)S(1)}, u32[]{:S(2)}) copy-start(f32[9,20,128]{2,1,0:T(8,128)S(1)} %collective-permute-done.3.rim3) | copy-start | bytes 276484
  18.1 27.1 %all-to-all-start = ((f32[128,1,1664]{2,1,0:T(1,128)}), f32[128,1,1664]{2,1,0:T(1,128)S(1)}, u32[]{:S(2)}, u32[]{:S(2)}) async-start(f32[128,1,1664]{2,1,0:T(1,128)} %bitcast.10), calls=%async_computation | async-start | bytes 1703936 | tf_op jit(solution)/shard_map/all_to_all | solution.py:532
